TPU v7x, 32 devices: a whole 2x2x4 slice. The times are simulated.
32 devices in a mesh: orb: 8 (over z, core), vec: 4 (over y, x).
Axes of the slice: x: 2, y: 2, z: 4, core: 2. Of those that a mesh axis runs over, the one named last changes fastest.
Arguments:
- orbitals: bfloat16 [8, 96, 9216], P('orb'), may hold values from -6 to 6
- energies: float32 [8], P('orb'), may hold values from -1 to 0
- trial_potential: bfloat16 [4, 96, 9216], P('vec', 'orb'), may hold values from -6 to 6
- local_potential: bfloat16 [96, 9216], P('orb'), may hold values from 0.5 to 2
Outputs:
- ortho: float32 [4, 96, 9216], P('vec', 'orb')
- factor: float32 [4, 4], replicated
All inputs are finite; a program needn't handle non-finite values.
Results may differ from a plain program's by a relative error of at most 0.0003.
Values may be sent and summed in bfloat16 or wider, within the bound.
No kernel may reach another device: no remote copies, remote signals or barrier semaphores. Data moves between devices by JAX's collectives and lax.ppermute only.
A program may use at most 64 MiB of HBM per device.

v0:
```python
import functools
import math

import jax
import jax.numpy as jnp
import ml_dtypes
import numpy as np
from jax import lax
from jax.experimental import pallas as pl
from jax.experimental.pallas import tpu as pltpu
from jax.sharding import PartitionSpec as P

NZ = 96
NY = 96
NX = 96
STEPS = 4

BF16 = jnp.bfloat16
F32 = jnp.float32
LANES = 128
WEIGHTS = [1.0 / (1.0 + 0.8 * math.cos(math.pi * (2 * s + 1) / (2 * STEPS))) for s in range(STEPS)]


def neighbours(field):
    depth, flat = field.shape
    zero_plane = jnp.zeros((1, flat), field.dtype)
    total = jnp.concatenate([zero_plane, field[:-1]], 0) + jnp.concatenate(
        [field[1:], zero_plane], 0
    )
    zero_rows = jnp.zeros((depth, NX), field.dtype)
    total = (
        total
        + jnp.concatenate([zero_rows, field[:, :-NX]], 1)
        + jnp.concatenate([field[:, NX:], zero_rows], 1)
    )
    column = jnp.arange(flat) % NX
    zero_col = jnp.zeros((depth, 1), field.dtype)
    left = jnp.concatenate([zero_col, field[:, :-1]], 1) * (column > 0).astype(field.dtype)
    right = jnp.concatenate([field[:, 1:], zero_col], 1) * (column < NX - 1).astype(field.dtype)
    return total + left + right


def solve(psi, perturb, potential, energy):
    diag = 3.25 + potential - energy
    source = -perturb * psi
    answer = jnp.zeros_like(psi)
    for step in range(STEPS):
        weight = 1.0 / (1.0 + 0.8 * jnp.cos(jnp.pi * (2 * step + 1) / (2 * STEPS)))
        applied = diag * answer - 0.5 * neighbours(answer)
        answer = answer + weight * (source - applied) / diag
    return answer


def sine_basis(count):
    index = jnp.arange(count, dtype=jnp.float32) + 1.0
    return jnp.sqrt(2.0 / (count + 1)) * jnp.sin(
        jnp.pi * index[:, None] * index[None, :] / (count + 1)
    )


def eigen_of(position, count):
    return 2.0 - 2.0 * jnp.cos(jnp.pi * (position.astype(jnp.float32) + 1.0) / (count + 1))


def planes(field):
    high = lax.Precision.HIGHEST
    depth = field.shape[0]
    cube = field.reshape(depth, NY, NX)
    cube = jnp.einsum("zyx,cx->zyc", cube, sine_basis(NX), precision=high)
    cube = jnp.einsum("zyc,by->zbc", cube, sine_basis(NY), precision=high)
    return cube.reshape(depth, NY * NX)


def scale_columns(columns, start):
    high = lax.Precision.HIGHEST
    width = columns.shape[1]
    position = start + jnp.arange(width)
    denom = (
        eigen_of(jnp.arange(NZ), NZ)[:, None]
        + eigen_of(position // NX, NY)[None, :]
        + eigen_of(position % NX, NX)[None, :]
    )
    basis = sine_basis(NZ)
    spectral = jnp.dot(basis, columns, precision=high) * (jnp.sqrt(4.0 * jnp.pi) / jnp.sqrt(denom))
    return jnp.dot(basis, spectral, precision=high)


def coulomb_slab(slab):
    columns = lax.all_to_all(planes(slab), "orb", split_axis=1, concat_axis=0, tiled=True)
    scaled = scale_columns(columns, lax.axis_index("orb") * columns.shape[1])
    back = lax.all_to_all(scaled, "orb", split_axis=0, concat_axis=1, tiled=True)
    return planes(back)


def factorize(partial_gram):
    lower = jnp.linalg.cholesky(partial_gram / (NZ * NY * NX))
    inverse = lax.linalg.triangular_solve(
        lower, jnp.eye(lower.shape[0], dtype=jnp.float32), left_side=True, lower=True
    )
    return (lower, inverse)


def general_body(orbitals, energies, trial_potential, local_potential):
    high = lax.Precision.HIGHEST
    depth = local_potential.shape[0]
    plane_cells = local_potential.shape[1]
    vector_slab = trial_potential.reshape(depth, plane_cells)
    perturb_full, potential_full = (
        lax.all_gather(vector_slab, "orb", axis=0, tiled=True),
        lax.all_gather(local_potential, "orb", axis=0, tiled=True),
    )
    perturb = perturb_full.astype(jnp.float32)
    potential = potential_full.astype(jnp.float32)
    weight = 4.0 / (orbitals.shape[0] * lax.axis_size("orb"))
    psi = orbitals[0].astype(jnp.float32)
    partial_value = psi * solve(psi, perturb, potential, energies[0])
    partial_value = partial_value * weight
    slab = lax.psum_scatter(partial_value, "orb", scatter_dimension=0, tiled=True)
    slab = coulomb_slab(slab)
    mine = slab.reshape(1, depth, plane_cells)
    gathered = lax.all_gather(mine, "vec", axis=0, tiled=True)
    flat = gathered.reshape(gathered.shape[0], depth * plane_cells)
    partial_gram = jnp.dot(flat, flat.T, precision=high)
    lower, inverse = factorize(lax.psum(partial_gram, "orb"))
    row = lax.dynamic_slice_in_dim(inverse, lax.axis_index("vec"), 1, 0)
    ortho = jnp.dot(row, flat, precision=high).reshape(1, depth, plane_cells)
    return (ortho, lower.T)


TILES = 3
GROUP = 4
SUB = 8
ROWS = GROUP * SUB
WTILES = TILES * SUB
HALO = STEPS - 1


def fits(orb, vec, norb, nv):
    return (
        norb == orb
        and nv == vec
        and orb % 2 == 0
        and NZ % orb == 0
        and NZ // orb >= 4
        and NZ // orb % 2 == 0
        and NY == vec * (ROWS - 2 * GROUP)
        and NY == TILES * ROWS
        and vec * ROWS == LANES
        and NX * GROUP == TILES * LANES
        and NX % (orb * vec) == 0
        and NZ % (orb * vec) == 0
        and STEPS <= GROUP
    )


def split(x):
    high = x.astype(BF16)
    return high, (x - high.astype(F32)).astype(BF16)


def np_split(x):
    x = np.asarray(x, np.float64)
    high = x.astype(ml_dtypes.bfloat16)
    return np.stack([high, (x - high.astype(np.float64)).astype(ml_dtypes.bfloat16)])


def dot3(a, b, dims):
    one = functools.partial(
        lax.dot_general, dimension_numbers=(dims, ((), ())), preferred_element_type=F32
    )
    return one(a[0], b[0]) + (one(a[0], b[1]) + one(a[1], b[0]))


def np_basis(count):
    index = np.arange(count, dtype=np.float64) + 1.0
    return np.sqrt(2.0 / (count + 1)) * np.sin(np.pi * np.outer(index, index) / (count + 1))


def np_eigen(count):
    return 4.0 * np.sin(np.pi * (np.arange(count, dtype=np.float64) + 1.0) / (2 * (count + 1))) ** 2


def to_rows(tiles):
    lane = lax.broadcasted_iota(jnp.int32, tiles[0].shape, 1)
    a, b, c = tiles
    return [
        a,
        pltpu.roll(jnp.where(lane >= 96, a, b), 32, 1),
        pltpu.roll(jnp.where(lane >= 64, b, c), 64, 1),
        pltpu.roll(c, 96, 1),
    ]


def to_tiles(rows):
    lane = lax.broadcasted_iota(jnp.int32, rows[0].shape, 1)
    r1, r2 = pltpu.roll(rows[1], 96, 1), pltpu.roll(rows[2], 64, 1)
    return [
        jnp.where(lane < 96, rows[0], r1),
        jnp.where(lane < 64, r1, r2),
        jnp.where(lane < 32, r2, pltpu.roll(rows[3], 32, 1)),
    ]


def first_tile(strip):
    return strip * (WTILES - 2 * TILES) - TILES


def tile_lanes(strip, t):
    tile = jnp.clip(first_tile(strip) + t, 0, NY * NX // LANES - 1)
    return pl.ds(pl.multiple_of(tile * LANES, LANES), LANES)


def pack_planes(src, plane, out, pairs):
    def one(pair, carry):
        for i in range(TILES):
            top = pl.multiple_of((plane + 2 * pair) * WTILES + i * SUB, SUB)
            low = pl.multiple_of((plane + 2 * pair + 1) * WTILES + i * SUB, SUB)
            block = jnp.concatenate([src[pl.ds(top, SUB), :], src[pl.ds(low, SUB), :]], 0)
            out[pair, i] = block.astype(BF16)
        return carry

    lax.fori_loop(0, pairs, one, 0)


def orbital_windows_kernel(orb, energy_ref, psi_ref, *refs):
    outs, planes_ref = refs[:-1], refs[-1]
    chips = orb // 2
    slab = NZ // chips
    chip = lax.axis_index("orb") // 2
    strip = lax.axis_index("vec")
    zero = jnp.zeros((HALO * WTILES, LANES), F32)
    planes_ref[: HALO * WTILES, :] = zero
    planes_ref[(NZ + HALO) * WTILES :, :] = zero
    for t in range(WTILES):
        row = HALO * WTILES + (t % TILES) * SUB + t // TILES
        planes_ref[pl.ds(row, NZ, WTILES), :] = psi_ref[0, :, tile_lanes(strip, t)].astype(F32)
    energy = jnp.full((1, LANES), energy_ref[0], F32)
    high = energy.astype(BF16).astype(F32)
    middle = (energy - high).astype(BF16).astype(F32)
    low = energy - high - middle
    lane = lax.broadcasted_iota(jnp.int32, (1, LANES), 1)
    for at in range(chips):
        row = at * slab * WTILES
        held = planes_ref[row : row + 1, :]
        held = jnp.where(lane == 0, high, jnp.where(lane == 1, middle, jnp.where(lane == 2, low, held)))
        planes_ref[row : row + 1, :] = held
    for shift in range(chips):
        pack_planes(planes_ref, ((chip + shift) % chips) * slab, outs[shift], (slab + 2 * HALO) // 2)


def orbital_windows(orbitals, energies, orb):
    chips = orb // 2
    pairs = (NZ // chips + 2 * HALO) // 2
    return pl.pallas_call(
        functools.partial(orbital_windows_kernel, orb),
        out_shape=[jax.ShapeDtypeStruct((pairs, TILES, 2 * SUB, LANES), BF16)] * chips,
        in_specs=[
            pl.BlockSpec(memory_space=pltpu.SMEM),
            pl.BlockSpec(memory_space=pltpu.VMEM),
        ],
        out_specs=[pl.BlockSpec(memory_space=pltpu.VMEM)] * chips,
        scratch_shapes=[pltpu.VMEM(((NZ + 2 * HALO) * WTILES, LANES), F32)],
        compiler_params=pltpu.CompilerParams(vmem_limit_bytes=24 << 20),
        name="orbital_windows",
    )(energies, orbitals)


def potential_windows_kernel(vec, v_ref, pot_ref, halo_ref, *refs):
    outs, planes_ref = refs[:-1], refs[-1]
    core = lax.axis_index("orb") % 2
    strip = lax.axis_index("vec")
    depth = v_ref.shape[1]
    half = depth + GROUP
    own = (1 - core) * GROUP
    other = core * depth
    for n in range(vec + 1):
        src, part, to = (v_ref.at[0], 0, lax.rem(strip + n, vec)) if n < vec else (pot_ref, GROUP, strip)
        for t in range(WTILES):
            row = (n * half) * WTILES + (t % TILES) * SUB + t // TILES
            lanes = tile_lanes(to, t)
            planes_ref[pl.ds(row + own * WTILES, depth, WTILES), :] = src[:, lanes].astype(F32)
            edge = halo_ref[:, lanes].astype(F32)[part : part + GROUP]
            planes_ref[pl.ds(row + other * WTILES, GROUP, WTILES), :] = edge
        pack_planes(planes_ref, n * half, outs[n], half // 2)


def potential_windows(trial, potential, halo, vec):
    half = potential.shape[0] + GROUP
    return pl.pallas_call(
        functools.partial(potential_windows_kernel, vec),
        out_shape=[jax.ShapeDtypeStruct((half // 2, TILES, 2 * SUB, LANES), BF16)] * (vec + 1),
        in_specs=[pl.BlockSpec(memory_space=pltpu.VMEM)] * 3,
        out_specs=[pl.BlockSpec(memory_space=pltpu.VMEM)] * (vec + 1),
        scratch_shapes=[pltpu.VMEM(((vec + 1) * half * WTILES, LANES), F32)],
        compiler_params=pltpu.CompilerParams(vmem_limit_bytes=24 << 20),
        name="potential_windows",
    )(trial, potential, halo)


def potential_rows_kernel(vec, mine_ref, other_ref, v_ref, d_ref):
    core = lax.axis_index("orb") % 2
    strip = lax.axis_index("vec")
    pairs = mine_ref.shape[1]
    for src, first in ((mine_ref, core * pairs), (other_ref, (1 - core) * pairs)):

        def one(pair, carry, src=src, first=first):
            plane = 2 * (first + pair)
            for n in range(vec + 1):
                rows = to_rows([src[n, pair, i].astype(F32) for i in range(TILES)])
                for zz in range(2):
                    for i in range(GROUP):
                        row = rows[i][zz * SUB : (zz + 1) * SUB]
                        if n < vec:
                            v_ref[lax.rem(strip - n + vec, vec), plane + zz, i] = row
                        else:
                            d_ref[plane + zz, i] = 3.25 + row
            return carry

        lax.fori_loop(0, pairs, one, 0)


def potential_rows(mine, other, vec):
    planes = 4 * mine.shape[1]
    return pl.pallas_call(
        functools.partial(potential_rows_kernel, vec),
        out_shape=[
            jax.ShapeDtypeStruct((vec, planes, GROUP, SUB, LANES), F32),
            jax.ShapeDtypeStruct((planes, GROUP, SUB, LANES), F32),
        ],
        in_specs=[pl.BlockSpec(memory_space=pltpu.VMEM)] * 2,
        out_specs=[pl.BlockSpec(memory_space=pltpu.VMEM)] * 2,
        compiler_params=pltpu.CompilerParams(vmem_limit_bytes=24 << 20),
        name="potential_rows",
    )(mine, other)


def solve_kernel(vec, first, last, *refs):
    psi_ref, v_ref, d_ref = refs[:3]
    refs = refs[3:]
    sum_ref = None if first else refs[0]
    outs = refs[0 if first else 1 : -5]
    psi_s, h_s, c_s, u_a, u_b = refs[-5:]
    planes = d_ref.shape[0]
    depth = (planes - 2 * GROUP) // 2
    core = lax.axis_index("orb") % 2
    top = (lax.axis_index("orb") // 2) * 2 * depth - GROUP
    top_row = lax.axis_index("vec") * (ROWS - 2 * GROUP) - GROUP
    lane = lax.broadcasted_iota(jnp.int32, (SUB, LANES), 1)
    group = lax.broadcasted_iota(jnp.int32, (SUB, LANES), 0)
    inside = []
    for i in range(GROUP):
        y = top_row + group * GROUP + i
        inside.append(jnp.where((y >= 0) & (y < NY) & (lane < NX), 0.5, 0.0))
    block = psi_ref[0, 0].astype(F32)
    energy = block[0:1, 0:1] + block[0:1, 1:2] + block[0:1, 2:3]

    def begin(pair, carry):
        rows = to_rows([psi_ref[pair, i].astype(F32) for i in range(TILES)])
        for zz in range(2):
            w = GROUP - HALO + 2 * pair + zz
            z = top + w
            there = jnp.where((z >= 0) & (z < NZ), 1.0, 0.0)
            for i in range(GROUP):
                psi = rows[i][zz * SUB : (zz + 1) * SUB]
                h = inside[i] * there / (d_ref[w, i] - energy)
                psi_s[w, i] = psi
                h_s[w, i] = h
                scaled = -2.0 * psi * h
                for k in range(vec):
                    c = scaled * v_ref[k, w, i]
                    c_s[k, w, i] = c
                    u_a[k, w, i] = WEIGHTS[0] * c
        return carry

    lax.fori_loop(0, psi_ref.shape[0], begin, 0)

    def stepped(src, k, w, weight):
        u = [src[k, w, i] for i in range(GROUP)]
        new = []
        for i in range(GROUP):
            north = u[i - 1] if i > 0 else pltpu.roll(u[GROUP - 1], 1, 0)
            south = u[i + 1] if i < GROUP - 1 else pltpu.roll(u[0], SUB - 1, 0)
            near = (src[k, w - 1, i] + src[k, w + 1, i]) + (north + south)
            near = near + (pltpu.roll(u[i], 1, 1) + pltpu.roll(u[i], LANES - 1, 1))
            new.append((1.0 - weight) * u[i] + weight * (c_s[k, w, i] + h_s[w, i] * near))
        return new

    src, dst = u_a, u_b
    for step in range(1, STEPS - 1):
        low = GROUP - HALO + step

        def middle(w, carry, src=src, dst=dst, step=step):
            for k in range(vec):
                for i, new in enumerate(stepped(src, k, w, WEIGHTS[step])):
                    dst[k, w, i] = new
            return carry

        lax.fori_loop(low, planes - low, middle, 0)
        src, dst = dst, src

    def end(p, carry, out, start, src=src):
        w = GROUP + start + p
        for k in range(vec):
            for i, new in enumerate(stepped(src, k, w, WEIGHTS[STEPS - 1])):
                rows = pl.ds(k * ROWS + i * SUB, SUB)
                total = psi_s[w, i] * new
                if not first:
                    total = total + sum_ref[start + p, rows, :]
                out[p, rows, :] = total
        return carry

    if last:
        lax.fori_loop(0, depth, functools.partial(end, out=outs[1], start=(1 - core) * depth), 0)
        lax.fori_loop(0, depth, functools.partial(end, out=outs[0], start=core * depth), 0)
    else:
        lax.fori_loop(0, 2 * depth, functools.partial(end, out=outs[0], start=0), 0)


def solve_window(psi, v, d, total, vec, last):
    planes = d.shape[0]
    depth = (planes - 2 * GROUP) // 2
    first = total is None
    if last:
        outs = [jax.ShapeDtypeStruct((depth, LANES, LANES), F32)] * 2
    else:
        outs = [jax.ShapeDtypeStruct((2 * depth, LANES, LANES), F32)]
    args = (psi, v, d) if first else (psi, v, d, total)
    rows = (planes, GROUP, SUB, LANES)
    got = pl.pallas_call(
        functools.partial(solve_kernel, vec, first, last),
        out_shape=outs,
        in_specs=[pl.BlockSpec(memory_space=pltpu.VMEM)] * len(args),
        out_specs=[pl.BlockSpec(memory_space=pltpu.VMEM)] * len(outs),
        scratch_shapes=[pltpu.VMEM(rows, F32)] * 2 + [pltpu.VMEM((vec, *rows), F32)] * 3,
        compiler_params=pltpu.CompilerParams(vmem_limit_bytes=32 << 20),
        name="solve_window",
    )(*args)
    return got if last else got[0]


def forward_x_kernel(ndev, basis_ref, own_ref, other_ref, out_ref):
    depth = own_ref.shape[0]
    parts = NX // ndev
    rows = out_ref.shape[0] // ndev
    basis = (basis_ref[0], basis_ref[1])
    for z in range(depth):
        chi = split(own_ref[z] + other_ref[z])
        got = dot3(basis, chi, ((1,), (1,)))
        for part in range(parts):
            out_ref[pl.ds(part * depth + z, ndev, rows), :] = got[part * ndev : (part + 1) * ndev]
    for row in range(parts * depth, rows):
        out_ref[pl.ds(row, ndev, rows), :] = jnp.zeros((ndev, LANES), F32)


def forward_x(own, other, basis, ndev):
    rows = -(-(NX // ndev) * own.shape[0] // SUB) * SUB
    out = pl.pallas_call(
        functools.partial(forward_x_kernel, ndev),
        out_shape=jax.ShapeDtypeStruct((ndev * rows, LANES), F32),
        in_specs=[pl.BlockSpec(memory_space=pltpu.VMEM)] * 3,
        out_specs=pl.BlockSpec(memory_space=pltpu.VMEM),
        compiler_params=pltpu.CompilerParams(vmem_limit_bytes=24 << 20),
        name="forward_x",
    )(basis, own, other)
    return out.reshape(ndev, rows, LANES)


def spectral_kernel(orb, vec, mux_ref, muzy_ref, wy_ref, kz_ref, kzb_ref, wyb_ref, got_ref, out_ref):
    ndev = orb * vec
    parts = NX // ndev
    me = lax.axis_index("orb") * vec + lax.axis_index("vec")
    rows = got_ref.shape[1]
    x = jnp.concatenate(
        [
            jnp.concatenate([got_ref[o * vec + v] for o in range(orb)], 0)
            for v in range(vec)
        ],
        1,
    )
    mm = ((1,), (0,))
    t = dot3(split(x), (wy_ref[0], wy_ref[1]), mm)
    t = dot3((kz_ref[0], kz_ref[1]), split(t), mm)
    scale = jnp.concatenate(
        [
            math.sqrt(4.0 * math.pi) / jnp.sqrt(muzy_ref[...] + mux_ref[part * ndev + me])
            for part in range(parts)
        ],
        0,
    )
    fields = [t[:, k * LANES : (k + 1) * LANES] * scale for k in range(vec)]
    lane = lax.broadcasted_iota(jnp.int32, (1, LANES), 1)
    gram = jnp.zeros((1, LANES), F32)
    for k in range(vec):
        for l in range(k + 1):
            entry = jnp.sum(jnp.sum(fields[k] * fields[l], axis=0, keepdims=True), axis=1, keepdims=True)
            gram = jnp.where(lane == k * vec + l, entry, gram)
    t = jnp.concatenate(fields, 1)
    t = dot3((kzb_ref[0], kzb_ref[1]), split(t), mm)
    t = dot3(split(t), (wyb_ref[0], wyb_ref[1]), mm)
    rows = out_ref.shape[0] // ndev
    groups = t.shape[0] // ndev
    for r in range(groups):
        for yt in range(TILES):
            out_ref[pl.ds(r * TILES + yt, ndev, rows), :] = t[
                r * ndev : (r + 1) * ndev, yt * LANES : (yt + 1) * LANES
            ]
    out_ref[pl.ds(groups * TILES, ndev, rows), :] = jnp.broadcast_to(gram, (ndev, LANES))


def spectral(got, orb, vec):
    ndev = orb * vec
    parts, zs = NX // ndev, NZ // ndev
    depth = NZ // orb
    strip = ROWS - 2 * GROUP
    rows_in = got.shape[1]
    rows_out = -(-(parts * zs * TILES + 1) // SUB) * SUB
    sy, sz = np_basis(NY), np_basis(NZ)
    wy = np.zeros((vec, vec, GROUP, SUB, vec, LANES))
    wyb = np.zeros((vec, LANES, TILES, vec, GROUP, SUB))
    for k in range(vec):
        for i in range(GROUP):
            for g in range(SUB):
                for v in range(vec):
                    row = v * strip - GROUP + GROUP * g + i
                    if v * strip <= row < (v + 1) * strip:
                        wy[v, k, i, g, k, :NY] = sy[row]
                for yt in range(TILES):
                    wyb[k, :NY, yt, k, i, g] = sy[yt * ROWS + GROUP * g + i]
    wy = wy.reshape(vec * LANES, vec * LANES)
    wyb = wyb.reshape(vec * LANES, TILES * LANES)
    kz = np.zeros((parts, NZ, orb, rows_in))
    kzb = np.zeros((zs, parts, ndev, parts, NZ))
    for part in range(parts):
        for o in range(orb):
            kz[part, :, o, part * depth : (part + 1) * depth] = sz[:, o * depth : (o + 1) * depth]
        for z in range(zs):
            kzb[z, part, :, part, :] = sz[z::zs]
    kz = kz.reshape(parts * NZ, orb * rows_in)
    kzb = kzb.reshape(zs * parts * ndev, parts * NZ)
    muzy = np.ones((NZ, LANES), np.float32)
    muzy[:, :NY] = np_eigen(NZ)[:, None] + np_eigen(NY)[None, :]
    mux = np_eigen(NX).astype(np.float32)
    out = pl.pallas_call(
        functools.partial(spectral_kernel, orb, vec),
        out_shape=jax.ShapeDtypeStruct((ndev * rows_out, LANES), F32),
        in_specs=[pl.BlockSpec(memory_space=pltpu.SMEM)] + [pl.BlockSpec(memory_space=pltpu.VMEM)] * 6,
        out_specs=pl.BlockSpec(memory_space=pltpu.VMEM),
        compiler_params=pltpu.CompilerParams(vmem_limit_bytes=32 << 20),
        name="spectral",
    )(mux, muzy, np_split(wy), np_split(kz), np_split(kzb), np_split(wyb), got)
    return out.reshape(ndev, rows_out, LANES)


def back_kernel(ndev, vec, basis_ref, got_ref, factor_ref, *outs):
    parts, zs = NX // ndev, NZ // ndev
    rows = got_ref.shape[0] // ndev
    strip = lax.axis_index("vec")
    basis = (basis_ref[0], basis_ref[1])
    gram = jnp.sum(got_ref[pl.ds(zs * parts * TILES, ndev, rows), :], axis=0, keepdims=True)
    gram = gram / (NZ * NY * NX)
    entry = lambda k, l: gram[:, k * vec + l : k * vec + l + 1]
    lower = [[None] * vec for _ in range(vec)]
    inverse = [[jnp.zeros((1, 1), F32)] * vec for _ in range(vec)]
    for l in range(vec):
        pivot = entry(l, l)
        for m in range(l):
            pivot = pivot - lower[l][m] * lower[l][m]
        lower[l][l] = jnp.sqrt(pivot)
        inverse[l][l] = 1.0 / lower[l][l]
        for k in range(l + 1, vec):
            value = entry(k, l)
            for m in range(l):
                value = value - lower[k][m] * lower[l][m]
            lower[k][l] = value * inverse[l][l]
    for l in range(vec):
        for k in range(l + 1, vec):
            value = lower[k][l] * inverse[l][l]
            for m in range(l + 1, k):
                value = value + lower[k][m] * inverse[m][l]
            inverse[k][l] = -value * inverse[k][k]
    at_row = lax.broadcasted_iota(jnp.int32, (vec, vec), 0)
    at_col = lax.broadcasted_iota(jnp.int32, (vec, vec), 1)
    factor = jnp.zeros((vec, vec), F32)
    for k in range(vec):
        for l in range(k + 1):
            factor = jnp.where((at_row == l) & (at_col == k), lower[k][l], factor)
    factor_ref[...] = factor
    coefficients = []
    for s in range(vec):
        to = lax.rem(strip + s, vec)
        line = []
        for k in range(vec):
            value = inverse[0][k]
            for m in range(1, vec):
                value = jnp.where(to == m, inverse[m][k], value)
            line.append(value)
        coefficients.append(line)
    for z in range(zs):
        for yt in range(TILES):
            x = jnp.concatenate(
                [
                    got_ref[pl.ds((z * parts + part) * TILES + yt, ndev, rows), :]
                    for part in range(parts)
                ],
                0,
            )
            y = dot3(split(x), basis, ((0,), (0,)))
            for s in range(vec):
                mixed = coefficients[s][0] * y[:ROWS]
                for k in range(1, vec):
                    mixed = mixed + coefficients[s][k] * y[k * ROWS : (k + 1) * ROWS]
                tiles = to_tiles([mixed[i * SUB : (i + 1) * SUB] for i in range(GROUP)])
                for i in range(TILES):
                    outs[s][z, (yt * TILES + i) * SUB : (yt * TILES + i + 1) * SUB, :] = tiles[i]


def back(got, basis, ndev, vec):
    zs = NZ // ndev
    tiles = NY * NX // LANES
    return pl.pallas_call(
        functools.partial(back_kernel, ndev, vec),
        out_shape=[jax.ShapeDtypeStruct((vec, vec), F32)]
        + [jax.ShapeDtypeStruct((zs, tiles, LANES), F32)] * vec,
        in_specs=[pl.BlockSpec(memory_space=pltpu.VMEM)] * 2,
        out_specs=[pl.BlockSpec(memory_space=pltpu.VMEM)] * (vec + 1),
        compiler_params=pltpu.CompilerParams(vmem_limit_bytes=24 << 20),
        name="back",
    )(basis, got.reshape(-1, LANES))


def assemble_kernel(vec, *refs):
    gots, out_ref, all_ref = refs[:vec], refs[vec], refs[vec + 1]
    strip = lax.axis_index("vec")
    zs, tiles = gots[0].shape[:2]
    depth = zs * vec
    for s in range(vec):
        first = lax.rem(strip - s + vec, vec) * zs
        for z in range(zs):
            start = pl.multiple_of((first + z) * tiles, SUB)
            all_ref[pl.ds(start, tiles), :] = gots[s][z]
    for yt in range(TILES):
        for i in range(TILES):
            for g in range(SUB):
                row = (yt * TILES + i) * SUB + g
                tile = yt * WTILES + g * TILES + i
                out_ref[0, :, tile * LANES : (tile + 1) * LANES] = all_ref[pl.ds(row, depth, tiles), :]


def assemble(gots, vec):
    zs, tiles = gots[0].shape[:2]
    return pl.pallas_call(
        functools.partial(assemble_kernel, vec),
        out_shape=jax.ShapeDtypeStruct((1, zs * vec, tiles * LANES), F32),
        in_specs=[pl.BlockSpec(memory_space=pltpu.VMEM)] * vec,
        out_specs=pl.BlockSpec(memory_space=pltpu.VMEM),
        scratch_shapes=[pltpu.VMEM((zs * vec * tiles, LANES), F32)],
        compiler_params=pltpu.CompilerParams(vmem_limit_bytes=24 << 20),
        name="assemble",
    )(*gots)


def swap_cores(x, orb):
    return lax.ppermute(x, "orb", [(o, o ^ 1) for o in range(orb)])


def shift(x, axis, count):
    n = lax.axis_size(axis)
    return lax.ppermute(x, axis, [(i, (i + count) % n) for i in range(n)])


def responses(orbitals, energies, trial_potential, local_potential):
    orb, vec = lax.axis_size("orb"), lax.axis_size("vec")
    core = lax.axis_index("orb") % 2
    depth = local_potential.shape[0]
    chips = orb // 2
    edges = [
        jnp.concatenate([trial_potential[0, at : at + GROUP], local_potential[at : at + GROUP]], 0)
        for at in (0, depth - GROUP)
    ]
    edge = jnp.where(core == 0, edges[0], edges[1])
    pairs = [(o, o + 1) for o in range(1, orb - 1, 2)] + [(o + 1, o) for o in range(1, orb - 1, 2)]
    halo = lax.ppermute(edge, "orb", pairs)
    windows = orbital_windows(orbitals, energies, orb)
    psis = [windows[0]]
    for r in range(1, chips):
        perm = [(2 * a + c, 2 * ((a + r) % chips) + c) for a in range(chips) for c in range(2)]
        psis.append(lax.ppermute(windows[r], "orb", perm))
    parts = potential_windows(trial_potential, local_potential, halo, vec)
    mine = jnp.stack([parts[0]] + [shift(parts[n], "vec", n) for n in range(1, vec)] + [parts[vec]])
    v, d = potential_rows(mine, swap_cores(mine, orb), vec)
    total = None
    for r in range(chips):
        total = solve_window(psis[r], v, d, total, vec, r == chips - 1)
    return total[0], swap_cores(total[1], orb)


def block_body(orbitals, energies, trial_potential, local_potential):
    orb, vec = lax.axis_size("orb"), lax.axis_size("vec")
    ndev = orb * vec
    both = ("orb", "vec")
    own, other = responses(orbitals, energies, trial_potential, local_potential)
    sx = np_basis(NX)
    padded = np.zeros((NX, LANES))
    padded[:, :NX] = sx
    sent = forward_x(own, other, np_split(padded * (4.0 / orb)), ndev)
    got = lax.all_to_all(sent, both, 0, 0, tiled=True)
    sent = spectral(got, orb, vec)
    got = lax.all_to_all(sent, both, 0, 0, tiled=True)
    factor, *slots = back(got, np_split(padded), ndev, vec)
    gots = [slots[0]] + [shift(slots[s], "vec", s) for s in range(1, vec)]
    return assemble(gots, vec), factor


def solution(mesh):
    orb, vec = mesh.shape["orb"], mesh.shape["vec"]
    placed = (P("orb", None, None), P("orb"), P("vec", "orb", None), P("orb", None))

    def body(orbitals, energies, trial_potential, local_potential):
        one = orbitals.shape[0] == 1 and trial_potential.shape[0] == 1
        plan = block_body if one and fits(orb, vec, orb, vec) else general_body
        return plan(orbitals, energies, trial_potential, local_potential)

    return jax.shard_map(
        body, mesh=mesh, in_specs=placed, out_specs=(P("vec", "orb", None), P()), check_vma=False
    )
```

profile of v0, /device:TPU:0, one launch (start us, length us, event | category | flops | bytes accessed | tf_op | source)
XLA Modules:
  0.0 126.9 jit_solution(9093451344433779911)
XLA Ops:
  0.7 1.2 slice_bitcast_fusion
  6.2 3.0 %collective-permute-start.2 = (bf16[8,3,16,128]{3,2,1,0:T(8,128)(2,1)S(1)}, bf16[8,3,16,128]{3,2,1,0:T(8,128)(2,1)S(1)}, u32[]{:S(2)}, u32[]{:S(2)}) collective-permute-start(bf16[8,3,16,128]{3,2,1,0:T(8,128)(2,1)S(1)} %get-tuple-element.22), channel_id=1, source_target_pairs={{0,1},{1,2},{2,3},{3,0},{4,5},{5,6},{6,7},{7,4},{8,9},{9,10},{10,1... | collective-permute-start | bytes 294920 | tf_op jit(solution)/shard_map/ppermute | solution.py:668
  9.2 1.5 %collective-permute-start.3 = (bf16[8,3,16,128]{3,2,1,0:T(8,128)(2,1)S(1)}, bf16[8,3,16,128]{3,2,1,0:T(8,128)(2,1)S(1)}, u32[]{:S(2)}, u32[]{:S(2)}) collective-permute-start(bf16[8,3,16,128]{3,2,1,0:T(8,128)(2,1)S(1)} %get-tuple-element.23), channel_id=1, source_target_pairs={{0,2},{1,3},{2,0},{3,1},{4,6},{5,7},{6,4},{7,5},{8,10},{9,11},{10,... | collective-permute-start | bytes 294920 | tf_op jit(solution)/shard_map/ppermute | solution.py:668
  10.8 1.4 %collective-permute-start.4 = (bf16[8,3,16,128]{3,2,1,0:T(8,128)(2,1)S(1)}, bf16[8,3,16,128]{3,2,1,0:T(8,128)(2,1)S(1)}, u32[]{:S(2)}, u32[]{:S(2)}) collective-permute-start(bf16[8,3,16,128]{3,2,1,0:T(8,128)(2,1)S(1)} %get-tuple-element.24), channel_id=1, source_target_pairs={{0,3},{1,0},{2,1},{3,2},{4,7},{5,4},{6,5},{7,6},{8,11},{9,8},{10,9... | collective-permute-start | bytes 294920 | tf_op jit(solution)/shard_map/ppermute | solution.py:668
  12.8 1.0 collective-permute-done.3
  13.9 1.5 %collective-permute-done.4 = bf16[8,3,16,128]{3,2,1,0:T(8,128)(2,1)S(1)} collective-permute-done((bf16[8,3,16,128]{3,2,1,0:T(8,128)(2,1)S(1)}, bf16[8,3,16,128]{3,2,1,0:T(8,128)(2,1)S(1)}, u32[]{:S(2)}, u32[]{:S(2)}) %collective-permute-start.4) | collective-permute-done | bytes 98336 | tf_op jit(solution)/shard_map/ppermute | solution.py:668
  15.4 4.1 %collective-permute-start.5 = (bf16[5,8,3,16,128]{4,3,2,1,0:T(8,128)(2,1)S(1)}, bf16[5,8,3,16,128]{4,3,2,1,0:T(8,128)(2,1)S(1)}, u32[]{:S(2)}, u32[]{:S(2)}) collective-permute-start(bf16[5,8,3,16,128]{4,3,2,1,0:T(8,128)(2,1)S(1)} %bitcast_dynamic-update-slice_fusion.mine_ref), channel_id=1, source_target_pairs={{0,4},{4,0},{8,12},{12,8},{16,20},{20,16},{24,28},{28,24},{1,5},{5... | collective-permute-start | bytes 1474568 | tf_op jit(solution)/shard_map/ppermute | solution.py:663
  20.9 3.6 %collective-permute-start.7 = (bf16[15,3,16,128]{3,2,1,0:T(8,128)(2,1)S(1)}, bf16[15,3,16,128]{3,2,1,0:T(8,128)(2,1)S(1)}, u32[]{:S(2)}, u32[]{:S(2)}) collective-permute-start(bf16[15,3,16,128]{3,2,1,0:T(8,128)(2,1)S(1)} %get-tuple-element.29), channel_id=1, source_target_pairs={{0,8},{4,12},{8,16},{12,20},{16,24},{20,28},{24,0},{28,4},{1,9},{5... | collective-permute-start | bytes 552968 | tf_op jit(solution)/shard_map/ppermute | solution.py:687
  24.6 2.3 %collective-permute-start.6 = (bf16[15,3,16,128]{3,2,1,0:T(8,128)(2,1)S(1)}, bf16[15,3,16,128]{3,2,1,0:T(8,128)(2,1)S(1)}, u32[]{:S(2)}, u32[]{:S(2)}) collective-permute-start(bf16[15,3,16,128]{3,2,1,0:T(8,128)(2,1)S(1)} %get-tuple-element.28), channel_id=1, source_target_pairs={{0,16},{4,20},{8,24},{12,28},{16,0},{20,4},{24,8},{28,12},{1,17},{... | collective-permute-start | bytes 552968 | tf_op jit(solution)/shard_map/ppermute | solution.py:687
  26.9 1.6 %collective-permute-start = (bf16[15,3,16,128]{3,2,1,0:T(8,128)(2,1)S(1)}, bf16[15,3,16,128]{3,2,1,0:T(8,128)(2,1)S(1)}, u32[]{:S(2)}, u32[]{:S(2)}) collective-permute-start(bf16[15,3,16,128]{3,2,1,0:T(8,128)(2,1)S(1)} %get-tuple-element.20), channel_id=1, source_target_pairs={{0,24},{4,28},{8,0},{12,4},{16,8},{20,12},{24,16},{28,20},{1,25},{... | collective-permute-start | bytes 552968 | tf_op jit(solution)/shard_map/ppermute | solution.py:687
  28.5 1.4 %potential_rows.1 = (f32[4,32,4,8,128]{4,3,2,1,0:T(8,128)S(1)}, f32[32,4,8,128]{3,2,1,0:T(8,128)S(1)}) custom-call(bf16[5,8,3,16,128]{4,3,2,1,0:T(8,128)(2,1)S(1)} %bitcast_dynamic-update-slice_fusion.mine_ref, bf16[5,8,3,16,128]{4,3,2,1,0:T(8,128)(2,1)S(1)} %collective-permute-done.5.other_ref), custom_call_target="tpu_custom_call" | custom-call | tf_op jit(solution)/shard_map/potential_rows/pallas_call | solution.py:324
  29.9 9.8 %solve_window.4.refs_3_ = f32[24,128,128]{2,1,0:T(8,128)S(1)} custom-call(bf16[15,3,16,128]{3,2,1,0:T(8,128)(2,1)S(1)} %get-tuple-element.30.refs_0_, f32[4,32,4,8,128]{4,3,2,1,0:T(8,128)S(1)} %get-tuple-element.26.refs_1_, f32[32,4,8,128]{3,2,1,0:T(8,128)S(1)} %get-tuple-element.27.refs_2_), custom_call_target="tpu_custom_call" | custom-call | tf_op jit(solution)/shard_map/solve_window/pallas_call | solution.py:429
  39.8 9.9 %solve_window.5.refs_3_ = f32[24,128,128]{2,1,0:T(8,128)S(1)} custom-call(bf16[15,3,16,128]{3,2,1,0:T(8,128)(2,1)S(1)} %collective-permute-done.7.refs_0_, f32[4,32,4,8,128]{4,3,2,1,0:T(8,128)S(1)} %get-tuple-element.26.refs_1_, f32[32,4,8,128]{3,2,1,0:T(8,128)S(1)} %get-tuple-element.27.refs_2_, f32[24,128,128]{2,1,0:T(8,128)S(1)} %solve_window.4.refs_3_), custom_call_target="tpu_custom_call" | custom-call | tf_op jit(solution)/shard_map/solve_window/pallas_call | solution.py:429
  49.7 9.9 %solve_window.6.refs_3_ = f32[24,128,128]{2,1,0:T(8,128)S(1)} custom-call(bf16[15,3,16,128]{3,2,1,0:T(8,128)(2,1)S(1)} %collective-permute-done.6.refs_0_, f32[4,32,4,8,128]{4,3,2,1,0:T(8,128)S(1)} %get-tuple-element.26.refs_1_, f32[32,4,8,128]{3,2,1,0:T(8,128)S(1)} %get-tuple-element.27.refs_2_, f32[24,128,128]{2,1,0:T(8,128)S(1)} %solve_window.5.refs_3_), custom_call_target="tpu_custom_call" | custom-call | tf_op jit(solution)/shard_map/solve_window/pallas_call | solution.py:429
  59.5 9.9 %solve_window.7 = (f32[12,128,128]{2,1,0:T(8,128)S(1)}, f32[12,128,128]{2,1,0:T(8,128)S(1)}) custom-call(bf16[15,3,16,128]{3,2,1,0:T(8,128)(2,1)S(1)} %collective-permute-done.refs_0_, f32[4,32,4,8,128]{4,3,2,1,0:T(8,128)S(1)} %get-tuple-element.26.refs_1_, f32[32,4,8,128]{3,2,1,0:T(8,128)S(1)} %get-tuple-element.27.refs_2_, ...), custom_call_target="tpu_custom_call" | custom-call | tf_op jit(solution)/shard_map/solve_window/pallas_call | solution.py:429
  69.5 2.3 %collective-permute-done.8.other_ref = f32[12,128,128]{2,1,0:T(8,128)S(1)} collective-permute-done((f32[12,128,128]{2,1,0:T(8,128)S(1)}, f32[12,128,128]{2,1,0:T(8,128)S(1)}, u32[]{:S(2)}, u32[]{:S(2)}) %collective-permute-start.8) | collective-permute-done | bytes 786464 | tf_op jit(solution)/shard_map/ppermute | solution.py:663
  72.8 21.6 %all_to_all.10.got_ref = f32[32,40,128]{2,1,0:T(8,128)S(1)} all-to-all(f32[32,40,128]{2,1,0:T(8,128)S(1)} %bitcast.17), channel_id=1, replica_groups=mesh['orb'=8,'vec'=4] {'orb','vec'}, dimensions={0} | all-to-all | bytes 1310720 | tf_op jit(solution)/shard_map/all_to_all | solution.py:706
  94.5 3.2 %spectral.1 = f32[1024,128]{1,0:T(8,128)S(1)} custom-call(f32[96]{0:T(128)S(1)} %copy-done.10, f32[96,128]{1,0:T(8,128)S(1)} %copy-done.7, bf16[2,512,512]{2,1,0:T(8,128)(2,1)S(1)} %copy-done.1, bf16[2,288,320]{2,1,0:T(8,128)(2,1)S(1)} %copy-done.6, bf16[2,288,288]{2,1,0:T(8,128)(2,1)S(1)} %copy-done.5, bf16[2,512,384]{2,1,0:T(8,128)(2,1)S(1)} %copy-done.2, ...), custom_call_target="tpu_custom_call" | custom-call | tf_op jit(solution)/shard_map/spectral/pallas_call | solution.py:543
  97.7 18.7 %all_to_all.11 = f32[32,32,128]{2,1,0:T(8,128)S(1)} all-to-all(f32[32,32,128]{2,1,0:T(8,128)S(1)} %bitcast.18), channel_id=1, replica_groups=mesh['orb'=8,'vec'=4] {'orb','vec'}, dimensions={0} | all-to-all | bytes 1048576 | tf_op jit(solution)/shard_map/all_to_all | solution.py:708
  116.4 1.5 %back.1 = (f32[4,4]{1,0:T(4,128)}, f32[3,72,128]{2,1,0:T(8,128)S(1)}, f32[3,72,128]{2,1,0:T(8,128)S(1)}, f32[3,72,128]{2,1,0:T(8,128)S(1)}, f32[3,72,128]{2,1,0:T(8,128)S(1)}) custom-call(bf16[2,96,128]{2,1,0:T(8,128)(2,1)S(1)} %copy-done.8, f32[1024,128]{1,0:T(8,128)S(1)} %bitcast.19), custom_call_target="tpu_custom_call" | custom-call | tf_op jit(solution)/shard_map/back/pallas_call | solution.py:620
  118.1 1.5 %collective-permute-start.10 = (f32[3,72,128]{2,1,0:T(8,128)S(1)}, f32[3,72,128]{2,1,0:T(8,128)S(1)}, u32[]{:S(2)}, u32[]{:S(2)}) collective-permute-start(f32[3,72,128]{2,1,0:T(8,128)S(1)} %get-tuple-element.35), channel_id=1, source_target_pairs={{0,2},{1,3},{2,0},{3,1},{4,6},{5,7},{6,4},{7,5},{8,10},{9,11},{10,... | collective-permute-start | bytes 331784 | tf_op jit(solution)/shard_map/ppermute | solution.py:668
  119.6 1.4 %collective-permute-start.11 = (f32[3,72,128]{2,1,0:T(8,128)S(1)}, f32[3,72,128]{2,1,0:T(8,128)S(1)}, u32[]{:S(2)}, u32[]{:S(2)}) collective-permute-start(f32[3,72,128]{2,1,0:T(8,128)S(1)} %get-tuple-element.36), channel_id=1, source_target_pairs={{0,3},{1,0},{2,1},{3,2},{4,7},{5,4},{6,5},{7,6},{8,11},{9,8},{10,9... | collective-permute-start | bytes 331784 | tf_op jit(solution)/shard_map/ppermute | solution.py:668
  121.1 3.2 %collective-permute-done.9.refs_1_ = f32[3,72,128]{2,1,0:T(8,128)S(1)} collective-permute-done((f32[3,72,128]{2,1,0:T(8,128)S(1)}, f32[3,72,128]{2,1,0:T(8,128)S(1)}, u32[]{:S(2)}, u32[]{:S(2)}) %collective-permute-start.9) | collective-permute-done | bytes 110624 | tf_op jit(solution)/shard_map/ppermute | solution.py:668
  125.6 1.2 copy.14
  (44 shorter events, 8.4 us)
Async XLA Ops:
  0.6 19.5 %copy-start = (bf16[1,96,9216]{2,1,0:T(8,128)(2,1)S(1)}, bf16[1,96,9216]{2,1,0:T(8,128)(2,1)}, u32[]{:S(2)}) copy-start(bf16[1,96,9216]{2,1,0:T(8,128)(2,1)} %psi_ref.1) | copy-start | bytes 5308420
  3.0 0.7 collective-permute-start.1
  3.7 1.0 copy-start.3
  4.7 1.0 copy-start.4
  6.2 6.5 %collective-permute-start.2 = (bf16[8,3,16,128]{3,2,1,0:T(8,128)(2,1)S(1)}, bf16[8,3,16,128]{3,2,1,0:T(8,128)(2,1)S(1)}, u32[]{:S(2)}, u32[]{:S(2)}) collective-permute-start(bf16[8,3,16,128]{3,2,1,0:T(8,128)(2,1)S(1)} %get-tuple-element.22), channel_id=1, source_target_pairs={{0,1},{1,2},{2,3},{3,0},{4,5},{5,6},{6,7},{7,4},{8,9},{9,10},{10,1... | collective-permute-start | bytes 294920 | tf_op jit(solution)/shard_map/ppermute | solution.py:668
  9.2 4.6 %collective-permute-start.3 = (bf16[8,3,16,128]{3,2,1,0:T(8,128)(2,1)S(1)}, bf16[8,3,16,128]{3,2,1,0:T(8,128)(2,1)S(1)}, u32[]{:S(2)}, u32[]{:S(2)}) collective-permute-start(bf16[8,3,16,128]{3,2,1,0:T(8,128)(2,1)S(1)} %get-tuple-element.23), channel_id=1, source_target_pairs={{0,2},{1,3},{2,0},{3,1},{4,6},{5,7},{6,4},{7,5},{8,10},{9,11},{10,... | collective-permute-start | bytes 294920 | tf_op jit(solution)/shard_map/ppermute | solution.py:668
  10.8 4.6 %collective-permute-start.4 = (bf16[8,3,16,128]{3,2,1,0:T(8,128)(2,1)S(1)}, bf16[8,3,16,128]{3,2,1,0:T(8,128)(2,1)S(1)}, u32[]{:S(2)}, u32[]{:S(2)}) collective-permute-start(bf16[8,3,16,128]{3,2,1,0:T(8,128)(2,1)S(1)} %get-tuple-element.24), channel_id=1, source_target_pairs={{0,3},{1,0},{2,1},{3,2},{4,7},{5,4},{6,5},{7,6},{8,11},{9,8},{10,9... | collective-permute-start | bytes 294920 | tf_op jit(solution)/shard_map/ppermute | solution.py:668
  15.4 13.1 %collective-permute-start.5 = (bf16[5,8,3,16,128]{4,3,2,1,0:T(8,128)(2,1)S(1)}, bf16[5,8,3,16,128]{4,3,2,1,0:T(8,128)(2,1)S(1)}, u32[]{:S(2)}, u32[]{:S(2)}) collective-permute-start(bf16[5,8,3,16,128]{4,3,2,1,0:T(8,128)(2,1)S(1)} %bitcast_dynamic-update-slice_fusion.mine_ref), channel_id=1, source_target_pairs={{0,4},{4,0},{8,12},{12,8},{16,20},{20,16},{24,28},{28,24},{1,5},{5... | collective-permute-start | bytes 1474568 | tf_op jit(solution)/shard_map/ppermute | solution.py:663
  20.9 18.8 %collective-permute-start.7 = (bf16[15,3,16,128]{3,2,1,0:T(8,128)(2,1)S(1)}, bf16[15,3,16,128]{3,2,1,0:T(8,128)(2,1)S(1)}, u32[]{:S(2)}, u32[]{:S(2)}) collective-permute-start(bf16[15,3,16,128]{3,2,1,0:T(8,128)(2,1)S(1)} %get-tuple-element.29), channel_id=1, source_target_pairs={{0,8},{4,12},{8,16},{12,20},{16,24},{20,28},{24,0},{28,4},{1,9},{5... | collective-permute-start | bytes 552968 | tf_op jit(solution)/shard_map/ppermute | solution.py:687
  24.6 25.1 %collective-permute-start.6 = (bf16[15,3,16,128]{3,2,1,0:T(8,128)(2,1)S(1)}, bf16[15,3,16,128]{3,2,1,0:T(8,128)(2,1)S(1)}, u32[]{:S(2)}, u32[]{:S(2)}) collective-permute-start(bf16[15,3,16,128]{3,2,1,0:T(8,128)(2,1)S(1)} %get-tuple-element.28), channel_id=1, source_target_pairs={{0,16},{4,20},{8,24},{12,28},{16,0},{20,4},{24,8},{28,12},{1,17},{... | collective-permute-start | bytes 552968 | tf_op jit(solution)/shard_map/ppermute | solution.py:687
  26.9 32.6 %collective-permute-start = (bf16[15,3,16,128]{3,2,1,0:T(8,128)(2,1)S(1)}, bf16[15,3,16,128]{3,2,1,0:T(8,128)(2,1)S(1)}, u32[]{:S(2)}, u32[]{:S(2)}) collective-permute-start(bf16[15,3,16,128]{3,2,1,0:T(8,128)(2,1)S(1)} %get-tuple-element.20), channel_id=1, source_target_pairs={{0,24},{4,28},{8,0},{12,4},{16,8},{20,12},{24,16},{28,20},{1,25},{... | collective-permute-start | bytes 552968 | tf_op jit(solution)/shard_map/ppermute | solution.py:687
  59.5 12.3 %copy-start.9 = (bf16[2,96,128]{2,1,0:T(8,128)(2,1)S(1)}, bf16[2,96,128]{2,1,0:T(8,128)(2,1)}, u32[]{:S(2)}) copy-start(bf16[2,96,128]{2,1,0:T(8,128)(2,1)} %constant.36.clone.basis_ref) | copy-start | bytes 147460
  69.4 2.4 %collective-permute-start.8 = (f32[12,128,128]{2,1,0:T(8,128)S(1)}, f32[12,128,128]{2,1,0:T(8,128)S(1)}, u32[]{:S(2)}, u32[]{:S(2)}) collective-permute-start(f32[12,128,128]{2,1,0:T(8,128)S(1)} %get-tuple-element.32), channel_id=1, source_target_pairs={{0,4},{4,0},{8,12},{12,8},{16,20},{20,16},{24,28},{28,24},{1,5},{5... | collective-permute-start | bytes 2359304 | tf_op jit(solution)/shard_map/ppermute | solution.py:663
  71.8 22.6 %copy-start.1 = (bf16[2,512,512]{2,1,0:T(8,128)(2,1)S(1)}, bf16[2,512,512]{2,1,0:T(8,128)(2,1)}, u32[]{:S(2)}) copy-start(bf16[2,512,512]{2,1,0:T(8,128)(2,1)} %constant.39.clone.wy_ref) | copy-start | bytes 3145732
  71.8 22.6 %copy-start.2 = (bf16[2,512,384]{2,1,0:T(8,128)(2,1)S(1)}, bf16[2,512,384]{2,1,0:T(8,128)(2,1)}, u32[]{:S(2)}) copy-start(bf16[2,512,384]{2,1,0:T(8,128)(2,1)} %constant.42.clone.wyb_ref) | copy-start | bytes 2359300
  71.8 22.6 %copy-start.5 = (bf16[2,288,288]{2,1,0:T(8,128)(2,1)S(1)}, bf16[2,288,288]{2,1,0:T(8,128)(2,1)}, u32[]{:S(2)}) copy-start(bf16[2,288,288]{2,1,0:T(8,128)(2,1)} %constant.41.clone.kzb_ref) | copy-start | bytes 995332
  71.8 22.6 %copy-start.6 = (bf16[2,288,320]{2,1,0:T(8,128)(2,1)S(1)}, bf16[2,288,320]{2,1,0:T(8,128)(2,1)}, u32[]{:S(2)}) copy-start(bf16[2,288,320]{2,1,0:T(8,128)(2,1)} %constant.40.clone.kz_ref) | copy-start | bytes 1105924
  71.8 22.6 %copy-start.7 = (f32[96,128]{1,0:T(8,128)S(1)}, f32[96,128]{1,0:T(8,128)}, u32[]{:S(2)}) copy-start(f32[96,128]{1,0:T(8,128)} %constant.38.clone.muzy_ref) | copy-start | bytes 147460
  71.8 22.6 %copy-start.10 = (f32[96]{0:T(128)S(1)}, f32[96]{0:T(128)}, u32[]{:S(2)}) copy-start(f32[96]{0:T(128)} %constant.37.clone.mux_ref) | copy-start | bytes 1156
  94.5 21.9 %copy-start.8 = (bf16[2,96,128]{2,1,0:T(8,128)(2,1)S(1)}, bf16[2,96,128]{2,1,0:T(8,128)(2,1)}, u32[]{:S(2)}) copy-start(bf16[2,96,128]{2,1,0:T(8,128)(2,1)} %constant.43.clone.basis_ref) | copy-start | bytes 147460
  117.9 6.4 %collective-permute-start.9 = (f32[3,72,128]{2,1,0:T(8,128)S(1)}, f32[3,72,128]{2,1,0:T(8,128)S(1)}, u32[]{:S(2)}, u32[]{:S(2)}) collective-permute-start(f32[3,72,128]{2,1,0:T(8,128)S(1)} %get-tuple-element.34), channel_id=1, source_target_pairs={{0,1},{1,2},{2,3},{3,0},{4,5},{5,6},{6,7},{7,4},{8,9},{9,10},{10,1... | collective-permute-start | bytes 331784 | tf_op jit(solution)/shard_map/ppermute | solution.py:668
  118.1 6.9 %collective-permute-start.10 = (f32[3,72,128]{2,1,0:T(8,128)S(1)}, f32[3,72,128]{2,1,0:T(8,128)S(1)}, u32[]{:S(2)}, u32[]{:S(2)}) collective-permute-start(f32[3,72,128]{2,1,0:T(8,128)S(1)} %get-tuple-element.35), channel_id=1, source_target_pairs={{0,2},{1,3},{2,0},{3,1},{4,6},{5,7},{6,4},{7,5},{8,10},{9,11},{10,... | collective-permute-start | bytes 331784 | tf_op jit(solution)/shard_map/ppermute | solution.py:668
  119.6 5.9 %collective-permute-start.11 = (f32[3,72,128]{2,1,0:T(8,128)S(1)}, f32[3,72,128]{2,1,0:T(8,128)S(1)}, u32[]{:S(2)}, u32[]{:S(2)}) collective-permute-start(f32[3,72,128]{2,1,0:T(8,128)S(1)} %get-tuple-element.36), channel_id=1, source_target_pairs={{0,3},{1,0},{2,1},{3,2},{4,7},{5,4},{6,5},{7,6},{8,11},{9,8},{10,9... | collective-permute-start | bytes 331784 | tf_op jit(solution)/shard_map/ppermute | solution.py:668
where the time goes:
time: 127 us
  Pallas kernels  48.1 us (38%)
  blocking collectives  40.3 us (32%)
  starting transfers between devices  21.5 us (17%)
  waiting for transfers between devices  9.85 us (8%)
  local copies, waits for them, and re-layouts  5.43 us (4%)
  between operations  1.54 us (1%)
    all_to_all x2, blocking collectives, block_body(): got = lax.all_to_all(sent, both, 0, 0, tiled=True)  40.3 us
    pallas_call x4, Pallas kernels, solve_window(): pl.pallas_call(functools.partial(solve_kernel, vec, first, last), out_sha...  39.4 us
    ppermute x6, starting transfers between devices, shift(): return lax.ppermute(x, axis, [(i, (i + count) % n) for i in range(n)])  9.1 us
    ppermute x3, starting transfers between devices, responses(): psis.append(lax.ppermute(windows[r], 'orb', perm))  7.58 us
    ppermute x6, waiting for transfers between devices, shift(): return lax.ppermute(x, axis, [(i, (i + count) % n) for i in range(n)])  7.56 us
    ppermute x2, starting transfers between devices, swap_cores(): return lax.ppermute(x, 'orb', [(o, o ^ 1) for o in range(orb)])  4.16 us
    unnamed x27, local copies, waits for them, and re-layouts  3.24 us
    pallas_call x1, Pallas kernels, spectral(): pl.pallas_call(functools.partial(spectral_kernel, orb, vec), out_shape=ja...  3.2 us
  transfers between devices with their start and end apart: 12, of which 7 were waited for; matrix products, arithmetic and copies ran while one was open for 0% of the time, Pallas kernels for 25%

commit v1 on v0

--- a/solution.py
+++ b/solution.py
@@ -308,12 +308,12 @@
             for n in range(vec + 1):
                 rows = to_rows([src[n, pair, i].astype(F32) for i in range(TILES)])
                 for zz in range(2):
-                    for i in range(GROUP):
-                        row = rows[i][zz * SUB : (zz + 1) * SUB]
-                        if n < vec:
-                            v_ref[lax.rem(strip - n + vec, vec), plane + zz, i] = row
-                        else:
-                            d_ref[plane + zz, i] = 3.25 + row
+                    block = jnp.concatenate([rows[i][zz * SUB : (zz + 1) * SUB] for i in range(GROUP)], 0)
+                    if n < vec:
+                        k = lax.rem(strip - n + vec, vec)
+                        v_ref[plane + zz, pl.ds(pl.multiple_of(k * ROWS, ROWS), ROWS), :] = block
+                    else:
+                        d_ref[plane + zz] = 3.25 + block
             return carry
 
         lax.fori_loop(0, pairs, one, 0)
@@ -324,8 +324,8 @@
     return pl.pallas_call(
         functools.partial(potential_rows_kernel, vec),
         out_shape=[
-            jax.ShapeDtypeStruct((vec, planes, GROUP, SUB, LANES), F32),
-            jax.ShapeDtypeStruct((planes, GROUP, SUB, LANES), F32),
+            jax.ShapeDtypeStruct((planes, vec * ROWS, LANES), F32),
+            jax.ShapeDtypeStruct((planes, ROWS, LANES), F32),
         ],
         in_specs=[pl.BlockSpec(memory_space=pltpu.VMEM)] * 2,
         out_specs=[pl.BlockSpec(memory_space=pltpu.VMEM)] * 2,
@@ -351,8 +351,12 @@
     for i in range(GROUP):
         y = top_row + group * GROUP + i
         inside.append(jnp.where((y >= 0) & (y < NY) & (lane < NX), 0.5, 0.0))
+    inside = jnp.concatenate(inside, 0)
     block = psi_ref[0, 0].astype(F32)
     energy = block[0:1, 0:1] + block[0:1, 1:2] + block[0:1, 2:3]
+    at = lax.broadcasted_iota(jnp.int32, (2 * LANES, LANES), 0) % LANES
+    to = lax.broadcasted_iota(jnp.int32, (2 * LANES, LANES), 1)
+    beside = jnp.where((at == to - 1) | (at == to + 1), 1.0, 0.0).astype(BF16)
 
     def begin(pair, carry):
         rows = to_rows([psi_ref[pair, i].astype(F32) for i in range(TILES)])
@@ -360,29 +364,35 @@
             w = GROUP - HALO + 2 * pair + zz
             z = top + w
             there = jnp.where((z >= 0) & (z < NZ), 1.0, 0.0)
-            for i in range(GROUP):
-                psi = rows[i][zz * SUB : (zz + 1) * SUB]
-                h = inside[i] * there / (d_ref[w, i] - energy)
-                psi_s[w, i] = psi
-                h_s[w, i] = h
-                scaled = -2.0 * psi * h
-                for k in range(vec):
-                    c = scaled * v_ref[k, w, i]
-                    c_s[k, w, i] = c
-                    u_a[k, w, i] = WEIGHTS[0] * c
+            psi = jnp.concatenate([rows[i][zz * SUB : (zz + 1) * SUB] for i in range(GROUP)], 0)
+            h = inside * there / (d_ref[w] - energy)
+            psi_s[w] = psi
+            h_s[w] = h
+            scaled = -2.0 * psi * h
+            for k in range(vec):
+                rows_k = pl.ds(k * ROWS, ROWS)
+                c = scaled * v_ref[w, rows_k, :]
+                c_s[w, rows_k, :] = c
+                u_a[w, rows_k, :] = WEIGHTS[0] * c
         return carry
 
-    lax.fori_loop(0, psi_ref.shape[0], begin, 0)
-
-    def stepped(src, k, w, weight):
-        u = [src[k, w, i] for i in range(GROUP)]
+    lax.fori_loop(0, psi_ref.shape[0], begin, 0, unroll=5)
+
+    def stepped(src, w, weight):
+        u = src[w]
+        high, low = split(u)
+        x = jnp.dot(jnp.concatenate([high, low], 1), beside, preferred_element_type=F32)
+        near = x + (src[w - 1] + src[w + 1])
+        h = h_s[w]
         new = []
-        for i in range(GROUP):
-            north = u[i - 1] if i > 0 else pltpu.roll(u[GROUP - 1], 1, 0)
-            south = u[i + 1] if i < GROUP - 1 else pltpu.roll(u[0], SUB - 1, 0)
-            near = (src[k, w - 1, i] + src[k, w + 1, i]) + (north + south)
-            near = near + (pltpu.roll(u[i], 1, 1) + pltpu.roll(u[i], LANES - 1, 1))
-            new.append((1.0 - weight) * u[i] + weight * (c_s[k, w, i] + h_s[w, i] * near))
+        for k in range(vec):
+            rows = [u[k * ROWS + i * SUB : k * ROWS + (i + 1) * SUB] for i in range(GROUP)]
+            north = jnp.concatenate([pltpu.roll(rows[-1], 1, 0)] + rows[:-1], 0)
+            south = jnp.concatenate(rows[1:] + [pltpu.roll(rows[0], SUB - 1, 0)], 0)
+            at_k = slice(k * ROWS, (k + 1) * ROWS)
+            total = near[at_k] + (north + south)
+            change = c_s[w, at_k, :] + h * total
+            new.append((1.0 - weight) * u[at_k] + weight * change)
         return new
 
     src, dst = u_a, u_b
@@ -390,30 +400,26 @@
         low = GROUP - HALO + step
 
         def middle(w, carry, src=src, dst=dst, step=step):
-            for k in range(vec):
-                for i, new in enumerate(stepped(src, k, w, WEIGHTS[step])):
-                    dst[k, w, i] = new
+            dst[w] = jnp.concatenate(stepped(src, w, WEIGHTS[step]), 0)
             return carry
 
-        lax.fori_loop(low, planes - low, middle, 0)
+        lax.fori_loop(low, planes - low, middle, 0, unroll=True)
         src, dst = dst, src
 
     def end(p, carry, out, start, src=src):
         w = GROUP + start + p
-        for k in range(vec):
-            for i, new in enumerate(stepped(src, k, w, WEIGHTS[STEPS - 1])):
-                rows = pl.ds(k * ROWS + i * SUB, SUB)
-                total = psi_s[w, i] * new
-                if not first:
-                    total = total + sum_ref[start + p, rows, :]
-                out[p, rows, :] = total
+        psi = psi_s[w]
+        total = jnp.concatenate([psi * new for new in stepped(src, w, WEIGHTS[STEPS - 1])], 0)
+        if not first:
+            total = total + sum_ref[start + p]
+        out[p] = total
         return carry
 
     if last:
-        lax.fori_loop(0, depth, functools.partial(end, out=outs[1], start=(1 - core) * depth), 0)
-        lax.fori_loop(0, depth, functools.partial(end, out=outs[0], start=core * depth), 0)
+        lax.fori_loop(0, depth, functools.partial(end, out=outs[1], start=(1 - core) * depth), 0, unroll=True)
+        lax.fori_loop(0, depth, functools.partial(end, out=outs[0], start=core * depth), 0, unroll=True)
     else:
-        lax.fori_loop(0, 2 * depth, functools.partial(end, out=outs[0], start=0), 0)
+        lax.fori_loop(0, 2 * depth, functools.partial(end, out=outs[0], start=0), 0, unroll=True)
 
 
 def solve_window(psi, v, d, total, vec, last):
@@ -425,13 +431,13 @@
     else:
         outs = [jax.ShapeDtypeStruct((2 * depth, LANES, LANES), F32)]
     args = (psi, v, d) if first else (psi, v, d, total)
-    rows = (planes, GROUP, SUB, LANES)
     got = pl.pallas_call(
         functools.partial(solve_kernel, vec, first, last),
         out_shape=outs,
         in_specs=[pl.BlockSpec(memory_space=pltpu.VMEM)] * len(args),
         out_specs=[pl.BlockSpec(memory_space=pltpu.VMEM)] * len(outs),
-        scratch_shapes=[pltpu.VMEM(rows, F32)] * 2 + [pltpu.VMEM((vec, *rows), F32)] * 3,
+        scratch_shapes=[pltpu.VMEM((planes, ROWS, LANES), F32)] * 2
+        + [pltpu.VMEM((planes, vec * ROWS, LANES), F32)] * 3,
         compiler_params=pltpu.CompilerParams(vmem_limit_bytes=32 << 20),
         name="solve_window",
     )(*args)

time: 127 us -> 109 us (0.86)
  Pallas kernels: 48.1 us -> 22.4 us
  blocking collectives: 40.3 us -> 44.9 us
  waiting for transfers between devices: 9.85 us -> 12.9 us
    pallas_call x4, Pallas kernels: 39.4 us -> 13.8 us  [solve_window(): pl.pallas_call(functools.partial(solve_kernel, vec, first, last), out_sha...]
    all_to_all x2, blocking collectives: 40.3 us -> 44.9 us  [block_body(): got = lax.all_to_all(sent, both, 0, 0, tiled=True)]
    ppermute x3, waiting for transfers between devices: 0.01 us -> 3.03 us  [responses(): psis.append(lax.ppermute(windows[r], 'orb', perm))]
  transfers between devices with their start and end apart: 12 -> 12, of which waited for: 7 -> 8; matrix products, arithmetic and copies ran while one was open for 0% -> 0% of each run, Pallas kernels for 25% -> 11%
where the time goes in v1:
time: 109 us
  blocking collectives  44.9 us (41%)
  Pallas kernels  22.4 us (21%)
  starting transfers between devices  21.5 us (20%)
  waiting for transfers between devices  12.9 us (12%)
  local copies, waits for them, and re-layouts  5.43 us (5%)
  between operations  1.54 us (1%)
    all_to_all x2, blocking collectives, block_body(): got = lax.all_to_all(sent, both, 0, 0, tiled=True)  44.9 us
    pallas_call x4, Pallas kernels, solve_window(): pl.pallas_call(functools.partial(solve_kernel, vec, first, last), out_sha...  13.8 us
    ppermute x6, starting transfers between devices, shift(): return lax.ppermute(x, axis, [(i, (i + count) % n) for i in range(n)])  9.1 us
    ppermute x3, starting transfers between devices, responses(): psis.append(lax.ppermute(windows[r], 'orb', perm))  7.58 us
    ppermute x6, waiting for transfers between devices, shift(): return lax.ppermute(x, axis, [(i, (i + count) % n) for i in range(n)])  7.56 us
    ppermute x2, starting transfers between devices, swap_cores(): return lax.ppermute(x, 'orb', [(o, o ^ 1) for o in range(orb)])  4.16 us
    unnamed x27, local copies, waits for them, and re-layouts  3.24 us
    pallas_call x1, Pallas kernels, spectral(): pl.pallas_call(functools.partial(spectral_kernel, orb, vec), out_shape=ja...  3.2 us
  transfers between devices with their start and end apart: 12, of which 8 were waited for; matrix products, arithmetic and copies ran while one was open for 0% of the time, Pallas kernels for 11%

profile of v1, /device:TPU:0, one launch (start us, length us, event | category | flops | bytes accessed | tf_op | source)
XLA Modules:
  0.0 108.8 jit_solution(879284725164145711)
XLA Ops:
  0.7 1.2 %slice_bitcast_fusion = (bf16[4,9216]{1,0:T(4,128)(2,1)S(1)}, bf16[4,9216]{1,0:T(4,128)(2,1)S(1)}) fusion(bf16[1,12,9216]{2,1,0:T(8,128)(2,1)} %v_ref.1), kind=kLoop, calls=%fused_computation.6 | loop fusion | bytes 294912 | tf_op jit(solution)/shard_map/squeeze | solution.py:683
  6.2 3.0 %collective-permute-start.2 = (bf16[8,3,16,128]{3,2,1,0:T(8,128)(2,1)S(1)}, bf16[8,3,16,128]{3,2,1,0:T(8,128)(2,1)S(1)}, u32[]{:S(2)}, u32[]{:S(2)}) collective-permute-start(bf16[8,3,16,128]{3,2,1,0:T(8,128)(2,1)S(1)} %get-tuple-element.22), channel_id=1, source_target_pairs={{0,1},{1,2},{2,3},{3,0},{4,5},{5,6},{6,7},{7,4},{8,9},{9,10},{10,1... | collective-permute-start | bytes 294920 | tf_op jit(solution)/shard_map/ppermute | solution.py:674
  9.2 1.5 %collective-permute-start.3 = (bf16[8,3,16,128]{3,2,1,0:T(8,128)(2,1)S(1)}, bf16[8,3,16,128]{3,2,1,0:T(8,128)(2,1)S(1)}, u32[]{:S(2)}, u32[]{:S(2)}) collective-permute-start(bf16[8,3,16,128]{3,2,1,0:T(8,128)(2,1)S(1)} %get-tuple-element.23), channel_id=1, source_target_pairs={{0,2},{1,3},{2,0},{3,1},{4,6},{5,7},{6,4},{7,5},{8,10},{9,11},{10,... | collective-permute-start | bytes 294920 | tf_op jit(solution)/shard_map/ppermute | solution.py:674
  10.8 1.4 %collective-permute-start.4 = (bf16[8,3,16,128]{3,2,1,0:T(8,128)(2,1)S(1)}, bf16[8,3,16,128]{3,2,1,0:T(8,128)(2,1)S(1)}, u32[]{:S(2)}, u32[]{:S(2)}) collective-permute-start(bf16[8,3,16,128]{3,2,1,0:T(8,128)(2,1)S(1)} %get-tuple-element.24), channel_id=1, source_target_pairs={{0,3},{1,0},{2,1},{3,2},{4,7},{5,4},{6,5},{7,6},{8,11},{9,8},{10,9... | collective-permute-start | bytes 294920 | tf_op jit(solution)/shard_map/ppermute | solution.py:674
  13.9 1.5 %collective-permute-done.4 = bf16[8,3,16,128]{3,2,1,0:T(8,128)(2,1)S(1)} collective-permute-done((bf16[8,3,16,128]{3,2,1,0:T(8,128)(2,1)S(1)}, bf16[8,3,16,128]{3,2,1,0:T(8,128)(2,1)S(1)}, u32[]{:S(2)}, u32[]{:S(2)}) %collective-permute-start.4) | collective-permute-done | bytes 98336 | tf_op jit(solution)/shard_map/ppermute | solution.py:674
  15.4 4.1 %collective-permute-start.5 = (bf16[5,8,3,16,128]{4,3,2,1,0:T(8,128)(2,1)S(1)}, bf16[5,8,3,16,128]{4,3,2,1,0:T(8,128)(2,1)S(1)}, u32[]{:S(2)}, u32[]{:S(2)}) collective-permute-start(bf16[5,8,3,16,128]{4,3,2,1,0:T(8,128)(2,1)S(1)} %bitcast_dynamic-update-slice_fusion.mine_ref), channel_id=1, source_target_pairs={{0,4},{4,0},{8,12},{12,8},{16,20},{20,16},{24,28},{28,24},{1,5},{5... | collective-permute-start | bytes 1474568 | tf_op jit(solution)/shard_map/ppermute | solution.py:669
  20.9 3.6 %collective-permute-start.7 = (bf16[15,3,16,128]{3,2,1,0:T(8,128)(2,1)S(1)}, bf16[15,3,16,128]{3,2,1,0:T(8,128)(2,1)S(1)}, u32[]{:S(2)}, u32[]{:S(2)}) collective-permute-start(bf16[15,3,16,128]{3,2,1,0:T(8,128)(2,1)S(1)} %get-tuple-element.29), channel_id=1, source_target_pairs={{0,8},{4,12},{8,16},{12,20},{16,24},{20,28},{24,0},{28,4},{1,9},{5... | collective-permute-start | bytes 552968 | tf_op jit(solution)/shard_map/ppermute | solution.py:693
  24.6 2.3 %collective-permute-start.6 = (bf16[15,3,16,128]{3,2,1,0:T(8,128)(2,1)S(1)}, bf16[15,3,16,128]{3,2,1,0:T(8,128)(2,1)S(1)}, u32[]{:S(2)}, u32[]{:S(2)}) collective-permute-start(bf16[15,3,16,128]{3,2,1,0:T(8,128)(2,1)S(1)} %get-tuple-element.28), channel_id=1, source_target_pairs={{0,16},{4,20},{8,24},{12,28},{16,0},{20,4},{24,8},{28,12},{1,17},{... | collective-permute-start | bytes 552968 | tf_op jit(solution)/shard_map/ppermute | solution.py:693
  26.9 1.6 %collective-permute-start = (bf16[15,3,16,128]{3,2,1,0:T(8,128)(2,1)S(1)}, bf16[15,3,16,128]{3,2,1,0:T(8,128)(2,1)S(1)}, u32[]{:S(2)}, u32[]{:S(2)}) collective-permute-start(bf16[15,3,16,128]{3,2,1,0:T(8,128)(2,1)S(1)} %get-tuple-element.20), channel_id=1, source_target_pairs={{0,24},{4,28},{8,0},{12,4},{16,8},{20,12},{24,16},{28,20},{1,25},{... | collective-permute-start | bytes 552968 | tf_op jit(solution)/shard_map/ppermute | solution.py:693
  28.5 1.4 %potential_rows.1 = (f32[32,128,128]{2,1,0:T(8,128)S(1)}, f32[32,32,128]{2,1,0:T(8,128)S(1)}) custom-call(bf16[5,8,3,16,128]{4,3,2,1,0:T(8,128)(2,1)S(1)} %bitcast_dynamic-update-slice_fusion.mine_ref, bf16[5,8,3,16,128]{4,3,2,1,0:T(8,128)(2,1)S(1)} %collective-permute-done.5.other_ref), custom_call_target="tpu_custom_call" | custom-call | tf_op jit(solution)/shard_map/potential_rows/pallas_call | solution.py:324
  29.9 3.3 %solve_window.4.refs_3_ = f32[24,128,128]{2,1,0:T(8,128)S(1)} custom-call(bf16[15,3,16,128]{3,2,1,0:T(8,128)(2,1)S(1)} %get-tuple-element.30.refs_0_, f32[32,128,128]{2,1,0:T(8,128)S(1)} %get-tuple-element.26.refs_1_, f32[32,32,128]{2,1,0:T(8,128)S(1)} %get-tuple-element.27.refs_2_), custom_call_target="tpu_custom_call" | custom-call | tf_op jit(solution)/shard_map/solve_window/pallas_call | solution.py:434
  33.2 3.4 %solve_window.5.refs_3_ = f32[24,128,128]{2,1,0:T(8,128)S(1)} custom-call(bf16[15,3,16,128]{3,2,1,0:T(8,128)(2,1)S(1)} %collective-permute-done.7.refs_0_, f32[32,128,128]{2,1,0:T(8,128)S(1)} %get-tuple-element.26.refs_1_, f32[32,32,128]{2,1,0:T(8,128)S(1)} %get-tuple-element.27.refs_2_, f32[24,128,128]{2,1,0:T(8,128)S(1)} %solve_window.4.refs_3_), custom_call_target="tpu_custom_call" | custom-call | tf_op jit(solution)/shard_map/solve_window/pallas_call | solution.py:434
  36.6 3.0 %collective-permute-done.6.refs_0_ = bf16[15,3,16,128]{3,2,1,0:T(8,128)(2,1)S(1)} collective-permute-done((bf16[15,3,16,128]{3,2,1,0:T(8,128)(2,1)S(1)}, bf16[15,3,16,128]{3,2,1,0:T(8,128)(2,1)S(1)}, u32[]{:S(2)}, u32[]{:S(2)}) %collective-permute-start.6) | collective-permute-done | bytes 184352 | tf_op jit(solution)/shard_map/ppermute | solution.py:693
  39.7 3.4 %solve_window.6.refs_3_ = f32[24,128,128]{2,1,0:T(8,128)S(1)} custom-call(bf16[15,3,16,128]{3,2,1,0:T(8,128)(2,1)S(1)} %collective-permute-done.6.refs_0_, f32[32,128,128]{2,1,0:T(8,128)S(1)} %get-tuple-element.26.refs_1_, f32[32,32,128]{2,1,0:T(8,128)S(1)} %get-tuple-element.27.refs_2_, f32[24,128,128]{2,1,0:T(8,128)S(1)} %solve_window.5.refs_3_), custom_call_target="tpu_custom_call" | custom-call | tf_op jit(solution)/shard_map/solve_window/pallas_call | solution.py:434
  43.1 3.7 %solve_window.7 = (f32[12,128,128]{2,1,0:T(8,128)S(1)}, f32[12,128,128]{2,1,0:T(8,128)S(1)}) custom-call(bf16[15,3,16,128]{3,2,1,0:T(8,128)(2,1)S(1)} %collective-permute-done.refs_0_, f32[32,128,128]{2,1,0:T(8,128)S(1)} %get-tuple-element.26.refs_1_, f32[32,32,128]{2,1,0:T(8,128)S(1)} %get-tuple-element.27.refs_2_, f32[24,128,128]{2,1,0:T(8,128)S(1)} %solve_window.6.refs_3_), custom_call_target="tpu_custom_call" | custom-call | tf_op jit(solution)/shard_map/solve_window/pallas_call | solution.py:434
  46.8 2.3 %collective-permute-done.8.other_ref = f32[12,128,128]{2,1,0:T(8,128)S(1)} collective-permute-done((f32[12,128,128]{2,1,0:T(8,128)S(1)}, f32[12,128,128]{2,1,0:T(8,128)S(1)}, u32[]{:S(2)}, u32[]{:S(2)}) %collective-permute-start.8) | collective-permute-done | bytes 786464 | tf_op jit(solution)/shard_map/ppermute | solution.py:669
  50.1 26.2 %all_to_all.10.got_ref = f32[32,40,128]{2,1,0:T(8,128)S(1)} all-to-all(f32[32,40,128]{2,1,0:T(8,128)S(1)} %bitcast.17), channel_id=1, replica_groups=mesh['orb'=8,'vec'=4] {'orb','vec'}, dimensions={0} | all-to-all | bytes 1310720 | tf_op jit(solution)/shard_map/all_to_all | solution.py:712
  76.4 3.2 %spectral.1 = f32[1024,128]{1,0:T(8,128)S(1)} custom-call(f32[96]{0:T(128)S(1)} %copy-done.10, f32[96,128]{1,0:T(8,128)S(1)} %copy-done.7, bf16[2,512,512]{2,1,0:T(8,128)(2,1)S(1)} %copy-done.1, bf16[2,288,320]{2,1,0:T(8,128)(2,1)S(1)} %copy-done.6, bf16[2,288,288]{2,1,0:T(8,128)(2,1)S(1)} %copy-done.5, bf16[2,512,384]{2,1,0:T(8,128)(2,1)S(1)} %copy-done.2, ...), custom_call_target="tpu_custom_call" | custom-call | tf_op jit(solution)/shard_map/spectral/pallas_call | solution.py:549
  79.6 18.7 %all_to_all.11 = f32[32,32,128]{2,1,0:T(8,128)S(1)} all-to-all(f32[32,32,128]{2,1,0:T(8,128)S(1)} %bitcast.18), channel_id=1, replica_groups=mesh['orb'=8,'vec'=4] {'orb','vec'}, dimensions={0} | all-to-all | bytes 1048576 | tf_op jit(solution)/shard_map/all_to_all | solution.py:714
  98.3 1.5 %back.1 = (f32[4,4]{1,0:T(4,128)}, f32[3,72,128]{2,1,0:T(8,128)S(1)}, f32[3,72,128]{2,1,0:T(8,128)S(1)}, f32[3,72,128]{2,1,0:T(8,128)S(1)}, f32[3,72,128]{2,1,0:T(8,128)S(1)}) custom-call(bf16[2,96,128]{2,1,0:T(8,128)(2,1)S(1)} %copy-done.8, f32[1024,128]{1,0:T(8,128)S(1)} %bitcast.19), custom_call_target="tpu_custom_call" | custom-call | tf_op jit(solution)/shard_map/back/pallas_call | solution.py:626
  100.0 1.5 %collective-permute-start.10 = (f32[3,72,128]{2,1,0:T(8,128)S(1)}, f32[3,72,128]{2,1,0:T(8,128)S(1)}, u32[]{:S(2)}, u32[]{:S(2)}) collective-permute-start(f32[3,72,128]{2,1,0:T(8,128)S(1)} %get-tuple-element.35), channel_id=1, source_target_pairs={{0,2},{1,3},{2,0},{3,1},{4,6},{5,7},{6,4},{7,5},{8,10},{9,11},{10,... | collective-permute-start | bytes 331784 | tf_op jit(solution)/shard_map/ppermute | solution.py:674
  101.5 1.4 %collective-permute-start.11 = (f32[3,72,128]{2,1,0:T(8,128)S(1)}, f32[3,72,128]{2,1,0:T(8,128)S(1)}, u32[]{:S(2)}, u32[]{:S(2)}) collective-permute-start(f32[3,72,128]{2,1,0:T(8,128)S(1)} %get-tuple-element.36), channel_id=1, source_target_pairs={{0,3},{1,0},{2,1},{3,2},{4,7},{5,4},{6,5},{7,6},{8,11},{9,8},{10,9... | collective-permute-start | bytes 331784 | tf_op jit(solution)/shard_map/ppermute | solution.py:674
  103.0 3.2 %collective-permute-done.9.refs_1_ = f32[3,72,128]{2,1,0:T(8,128)S(1)} collective-permute-done((f32[3,72,128]{2,1,0:T(8,128)S(1)}, f32[3,72,128]{2,1,0:T(8,128)S(1)}, u32[]{:S(2)}, u32[]{:S(2)}) %collective-permute-start.9) | collective-permute-done | bytes 110624 | tf_op jit(solution)/shard_map/ppermute | solution.py:674
  107.5 1.2 %copy.14 = f32[1,12,9216]{2,0,1:T(1,128)} copy(f32[1,12,9216]{2,1,0:T(8,128)S(1)} %assemble.1) | data formatting | bytes 884736
  (44 shorter events, 9.5 us)
Async XLA Ops:
  0.6 19.5 %copy-start = (bf16[1,96,9216]{2,1,0:T(8,128)(2,1)S(1)}, bf16[1,96,9216]{2,1,0:T(8,128)(2,1)}, u32[]{:S(2)}) copy-start(bf16[1,96,9216]{2,1,0:T(8,128)(2,1)} %psi_ref.1) | copy-start | bytes 5308420
  3.0 0.7 collective-permute-start.1
  3.7 1.0 copy-start.3
  4.7 1.0 copy-start.4
  6.2 6.5 %collective-permute-start.2 = (bf16[8,3,16,128]{3,2,1,0:T(8,128)(2,1)S(1)}, bf16[8,3,16,128]{3,2,1,0:T(8,128)(2,1)S(1)}, u32[]{:S(2)}, u32[]{:S(2)}) collective-permute-start(bf16[8,3,16,128]{3,2,1,0:T(8,128)(2,1)S(1)} %get-tuple-element.22), channel_id=1, source_target_pairs={{0,1},{1,2},{2,3},{3,0},{4,5},{5,6},{6,7},{7,4},{8,9},{9,10},{10,1... | collective-permute-start | bytes 294920 | tf_op jit(solution)/shard_map/ppermute | solution.py:674
  9.2 4.6 %collective-permute-start.3 = (bf16[8,3,16,128]{3,2,1,0:T(8,128)(2,1)S(1)}, bf16[8,3,16,128]{3,2,1,0:T(8,128)(2,1)S(1)}, u32[]{:S(2)}, u32[]{:S(2)}) collective-permute-start(bf16[8,3,16,128]{3,2,1,0:T(8,128)(2,1)S(1)} %get-tuple-element.23), channel_id=1, source_target_pairs={{0,2},{1,3},{2,0},{3,1},{4,6},{5,7},{6,4},{7,5},{8,10},{9,11},{10,... | collective-permute-start | bytes 294920 | tf_op jit(solution)/shard_map/ppermute | solution.py:674
  10.8 4.6 %collective-permute-start.4 = (bf16[8,3,16,128]{3,2,1,0:T(8,128)(2,1)S(1)}, bf16[8,3,16,128]{3,2,1,0:T(8,128)(2,1)S(1)}, u32[]{:S(2)}, u32[]{:S(2)}) collective-permute-start(bf16[8,3,16,128]{3,2,1,0:T(8,128)(2,1)S(1)} %get-tuple-element.24), channel_id=1, source_target_pairs={{0,3},{1,0},{2,1},{3,2},{4,7},{5,4},{6,5},{7,6},{8,11},{9,8},{10,9... | collective-permute-start | bytes 294920 | tf_op jit(solution)/shard_map/ppermute | solution.py:674
  15.4 13.1 %collective-permute-start.5 = (bf16[5,8,3,16,128]{4,3,2,1,0:T(8,128)(2,1)S(1)}, bf16[5,8,3,16,128]{4,3,2,1,0:T(8,128)(2,1)S(1)}, u32[]{:S(2)}, u32[]{:S(2)}) collective-permute-start(bf16[5,8,3,16,128]{4,3,2,1,0:T(8,128)(2,1)S(1)} %bitcast_dynamic-update-slice_fusion.mine_ref), channel_id=1, source_target_pairs={{0,4},{4,0},{8,12},{12,8},{16,20},{20,16},{24,28},{28,24},{1,5},{5... | collective-permute-start | bytes 1474568 | tf_op jit(solution)/shard_map/ppermute | solution.py:669
  20.9 12.3 %collective-permute-start.7 = (bf16[15,3,16,128]{3,2,1,0:T(8,128)(2,1)S(1)}, bf16[15,3,16,128]{3,2,1,0:T(8,128)(2,1)S(1)}, u32[]{:S(2)}, u32[]{:S(2)}) collective-permute-start(bf16[15,3,16,128]{3,2,1,0:T(8,128)(2,1)S(1)} %get-tuple-element.29), channel_id=1, source_target_pairs={{0,8},{4,12},{8,16},{12,20},{16,24},{20,28},{24,0},{28,4},{1,9},{5... | collective-permute-start | bytes 552968 | tf_op jit(solution)/shard_map/ppermute | solution.py:693
  24.6 15.1 %collective-permute-start.6 = (bf16[15,3,16,128]{3,2,1,0:T(8,128)(2,1)S(1)}, bf16[15,3,16,128]{3,2,1,0:T(8,128)(2,1)S(1)}, u32[]{:S(2)}, u32[]{:S(2)}) collective-permute-start(bf16[15,3,16,128]{3,2,1,0:T(8,128)(2,1)S(1)} %get-tuple-element.28), channel_id=1, source_target_pairs={{0,16},{4,20},{8,24},{12,28},{16,0},{20,4},{24,8},{28,12},{1,17},{... | collective-permute-start | bytes 552968 | tf_op jit(solution)/shard_map/ppermute | solution.py:693
  26.9 16.2 %collective-permute-start = (bf16[15,3,16,128]{3,2,1,0:T(8,128)(2,1)S(1)}, bf16[15,3,16,128]{3,2,1,0:T(8,128)(2,1)S(1)}, u32[]{:S(2)}, u32[]{:S(2)}) collective-permute-start(bf16[15,3,16,128]{3,2,1,0:T(8,128)(2,1)S(1)} %get-tuple-element.20), channel_id=1, source_target_pairs={{0,24},{4,28},{8,0},{12,4},{16,8},{20,12},{24,16},{28,20},{1,25},{... | collective-permute-start | bytes 552968 | tf_op jit(solution)/shard_map/ppermute | solution.py:693
  43.1 6.1 %copy-start.9 = (bf16[2,96,128]{2,1,0:T(8,128)(2,1)S(1)}, bf16[2,96,128]{2,1,0:T(8,128)(2,1)}, u32[]{:S(2)}) copy-start(bf16[2,96,128]{2,1,0:T(8,128)(2,1)} %constant.36.clone.basis_ref) | copy-start | bytes 147460
  46.8 2.4 %collective-permute-start.8 = (f32[12,128,128]{2,1,0:T(8,128)S(1)}, f32[12,128,128]{2,1,0:T(8,128)S(1)}, u32[]{:S(2)}, u32[]{:S(2)}) collective-permute-start(f32[12,128,128]{2,1,0:T(8,128)S(1)} %get-tuple-element.32), channel_id=1, source_target_pairs={{0,4},{4,0},{8,12},{12,8},{16,20},{20,16},{24,28},{28,24},{1,5},{5... | collective-permute-start | bytes 2359304 | tf_op jit(solution)/shard_map/ppermute | solution.py:669
  49.1 27.2 %copy-start.1 = (bf16[2,512,512]{2,1,0:T(8,128)(2,1)S(1)}, bf16[2,512,512]{2,1,0:T(8,128)(2,1)}, u32[]{:S(2)}) copy-start(bf16[2,512,512]{2,1,0:T(8,128)(2,1)} %constant.39.clone.wy_ref) | copy-start | bytes 3145732
  49.1 27.2 %copy-start.2 = (bf16[2,512,384]{2,1,0:T(8,128)(2,1)S(1)}, bf16[2,512,384]{2,1,0:T(8,128)(2,1)}, u32[]{:S(2)}) copy-start(bf16[2,512,384]{2,1,0:T(8,128)(2,1)} %constant.42.clone.wyb_ref) | copy-start | bytes 2359300
  49.1 27.2 %copy-start.5 = (bf16[2,288,288]{2,1,0:T(8,128)(2,1)S(1)}, bf16[2,288,288]{2,1,0:T(8,128)(2,1)}, u32[]{:S(2)}) copy-start(bf16[2,288,288]{2,1,0:T(8,128)(2,1)} %constant.41.clone.kzb_ref) | copy-start | bytes 995332
  49.1 27.2 %copy-start.6 = (bf16[2,288,320]{2,1,0:T(8,128)(2,1)S(1)}, bf16[2,288,320]{2,1,0:T(8,128)(2,1)}, u32[]{:S(2)}) copy-start(bf16[2,288,320]{2,1,0:T(8,128)(2,1)} %constant.40.clone.kz_ref) | copy-start | bytes 1105924
  49.1 27.2 %copy-start.7 = (f32[96,128]{1,0:T(8,128)S(1)}, f32[96,128]{1,0:T(8,128)}, u32[]{:S(2)}) copy-start(f32[96,128]{1,0:T(8,128)} %constant.38.clone.muzy_ref) | copy-start | bytes 147460
  49.2 27.2 %copy-start.10 = (f32[96]{0:T(128)S(1)}, f32[96]{0:T(128)}, u32[]{:S(2)}) copy-start(f32[96]{0:T(128)} %constant.37.clone.mux_ref) | copy-start | bytes 1156
  76.4 21.9 %copy-start.8 = (bf16[2,96,128]{2,1,0:T(8,128)(2,1)S(1)}, bf16[2,96,128]{2,1,0:T(8,128)(2,1)}, u32[]{:S(2)}) copy-start(bf16[2,96,128]{2,1,0:T(8,128)(2,1)} %constant.43.clone.basis_ref) | copy-start | bytes 147460
  99.8 6.4 %collective-permute-start.9 = (f32[3,72,128]{2,1,0:T(8,128)S(1)}, f32[3,72,128]{2,1,0:T(8,128)S(1)}, u32[]{:S(2)}, u32[]{:S(2)}) collective-permute-start(f32[3,72,128]{2,1,0:T(8,128)S(1)} %get-tuple-element.34), channel_id=1, source_target_pairs={{0,1},{1,2},{2,3},{3,0},{4,5},{5,6},{6,7},{7,4},{8,9},{9,10},{10,1... | collective-permute-start | bytes 331784 | tf_op jit(solution)/shard_map/ppermute | solution.py:674
  100.0 6.9 %collective-permute-start.10 = (f32[3,72,128]{2,1,0:T(8,128)S(1)}, f32[3,72,128]{2,1,0:T(8,128)S(1)}, u32[]{:S(2)}, u32[]{:S(2)}) collective-permute-start(f32[3,72,128]{2,1,0:T(8,128)S(1)} %get-tuple-element.35), channel_id=1, source_target_pairs={{0,2},{1,3},{2,0},{3,1},{4,6},{5,7},{6,4},{7,5},{8,10},{9,11},{10,... | collective-permute-start | bytes 331784 | tf_op jit(solution)/shard_map/ppermute | solution.py:674
  101.5 5.9 %collective-permute-start.11 = (f32[3,72,128]{2,1,0:T(8,128)S(1)}, f32[3,72,128]{2,1,0:T(8,128)S(1)}, u32[]{:S(2)}, u32[]{:S(2)}) collective-permute-start(f32[3,72,128]{2,1,0:T(8,128)S(1)} %get-tuple-element.36), channel_id=1, source_target_pairs={{0,3},{1,0},{2,1},{3,2},{4,7},{5,4},{6,5},{7,6},{8,11},{9,8},{10,9... | collective-permute-start | bytes 331784 | tf_op jit(solution)/shard_map/ppermute | solution.py:674

commit v2 on v1

--- a/solution.py
+++ b/solution.py
@@ -205,8 +205,12 @@
     return strip * (WTILES - 2 * TILES) - TILES
 
 
-def tile_lanes(strip, t):
-    tile = jnp.clip(first_tile(strip) + t, 0, NY * NX // LANES - 1)
+def window_start(strip):
+    return jnp.clip(first_tile(strip), 0, NY * NX // LANES - WTILES)
+
+
+def tile_lanes(strip, t, start=0):
+    tile = jnp.clip(first_tile(strip) + t, 0, NY * NX // LANES - 1) - start
     return pl.ds(pl.multiple_of(tile * LANES, LANES), LANES)
 
 
@@ -222,18 +226,39 @@
     lax.fori_loop(0, pairs, one, 0)
 
 
-def orbital_windows_kernel(orb, energy_ref, psi_ref, *refs):
-    outs, planes_ref = refs[:-1], refs[-1]
+def windows_kernel(orb, vec, energy_ref, psi_any, v_any, pot_any, *refs):
+    outs, (planes_ref, more_ref, psi_ref, v_ref, pot_ref, sem) = refs[:-6], refs[-6:]
     chips = orb // 2
     slab = NZ // chips
+    depth = v_ref.shape[0]
     chip = lax.axis_index("orb") // 2
     strip = lax.axis_index("vec")
+    start = window_start(strip)
+    lanes = pl.ds(pl.multiple_of(start * LANES, LANES), WTILES * LANES)
+    copies = [
+        pltpu.make_async_copy(v_any.at[0], v_ref, sem.at[0]),
+        pltpu.make_async_copy(pot_any.at[:, lanes], pot_ref, sem.at[1]),
+        pltpu.make_async_copy(psi_any.at[0, :, lanes], psi_ref, sem.at[2]),
+    ]
+    for copy in copies:
+        copy.start()
+    for copy in copies:
+        copy.wait()
+    for n in range(vec + 1):
+        for t in range(WTILES):
+            row = (n * depth) * WTILES + (t % TILES) * SUB + t // TILES
+            if n < vec:
+                tile = v_ref[:, tile_lanes(lax.rem(strip + n, vec), t)]
+            else:
+                tile = pot_ref[:, tile_lanes(strip, t, start)]
+            more_ref[pl.ds(row, depth, WTILES), :] = tile.astype(F32)
+        pack_planes(more_ref, n * depth, outs[chips + n], depth // 2)
     zero = jnp.zeros((HALO * WTILES, LANES), F32)
     planes_ref[: HALO * WTILES, :] = zero
     planes_ref[(NZ + HALO) * WTILES :, :] = zero
     for t in range(WTILES):
         row = HALO * WTILES + (t % TILES) * SUB + t // TILES
-        planes_ref[pl.ds(row, NZ, WTILES), :] = psi_ref[0, :, tile_lanes(strip, t)].astype(F32)
+        planes_ref[pl.ds(row, NZ, WTILES), :] = psi_ref[:, tile_lanes(strip, t, start)].astype(F32)
     energy = jnp.full((1, LANES), energy_ref[0], F32)
     high = energy.astype(BF16).astype(F32)
     middle = (energy - high).astype(BF16).astype(F32)
@@ -248,56 +273,80 @@
         pack_planes(planes_ref, ((chip + shift) % chips) * slab, outs[shift], (slab + 2 * HALO) // 2)
 
 
-def orbital_windows(orbitals, energies, orb):
+def windows(orbitals, energies, trial, potential, orb, vec):
     chips = orb // 2
+    depth = potential.shape[0]
+    block = (TILES, 2 * SUB, LANES)
     pairs = (NZ // chips + 2 * HALO) // 2
+    outs = [jax.ShapeDtypeStruct((pairs, *block), BF16)] * chips
+    outs += [jax.ShapeDtypeStruct((depth // 2, *block), BF16)] * (vec + 1)
+    got = pl.pallas_call(
+        functools.partial(windows_kernel, orb, vec),
+        out_shape=outs,
+        in_specs=[pl.BlockSpec(memory_space=pltpu.SMEM)] + [pl.BlockSpec(memory_space=pltpu.HBM)] * 3,
+        out_specs=[pl.BlockSpec(memory_space=pltpu.VMEM)] * len(outs),
+        scratch_shapes=[
+            pltpu.VMEM(((NZ + 2 * HALO) * WTILES, LANES), F32),
+            pltpu.VMEM(((vec + 1) * depth * WTILES, LANES), F32),
+            pltpu.VMEM((NZ, WTILES * LANES), BF16),
+            pltpu.VMEM((depth, NY * NX), BF16),
+            pltpu.VMEM((depth, WTILES * LANES), BF16),
+            pltpu.SemaphoreType.DMA((3,)),
+        ],
+        compiler_params=pltpu.CompilerParams(vmem_limit_bytes=24 << 20),
+        name="windows",
+    )(energies, *(pltpu.with_memory_space_constraint(x, pltpu.HBM) for x in (orbitals, trial, potential)))
+    return list(got[:chips]), list(got[chips:])
+
+
+def edges_kernel(n, parts_and_more, *refs):
+    parts, (own_ref, edge_ref) = refs[:n], refs[parts_and_more:]
+    core = lax.axis_index("orb") % 2
+    first = core * (own_ref.shape[1] - edge_ref.shape[1])
+    for i, part in enumerate(parts):
+        own_ref[i] = part[...]
+        edge_ref[i] = part[pl.ds(first, edge_ref.shape[1])]
+
+
+def edges(parts, arrived):
+    pairs, *block = parts[0].shape
+    n = len(parts)
+    more = n + len(arrived)
     return pl.pallas_call(
-        functools.partial(orbital_windows_kernel, orb),
-        out_shape=[jax.ShapeDtypeStruct((pairs, TILES, 2 * SUB, LANES), BF16)] * chips,
-        in_specs=[
-            pl.BlockSpec(memory_space=pltpu.SMEM),
-            pl.BlockSpec(memory_space=pltpu.VMEM),
+        functools.partial(edges_kernel, n, more),
+        out_shape=[
+            jax.ShapeDtypeStruct((n, pairs, *block), BF16),
+            jax.ShapeDtypeStruct((n, GROUP // 2, *block), BF16),
         ],
-        out_specs=[pl.BlockSpec(memory_space=pltpu.VMEM)] * chips,
-        scratch_shapes=[pltpu.VMEM(((NZ + 2 * HALO) * WTILES, LANES), F32)],
+        in_specs=[pl.BlockSpec(memory_space=pltpu.VMEM)] * more,
+        out_specs=[pl.BlockSpec(memory_space=pltpu.VMEM)] * 2,
         compiler_params=pltpu.CompilerParams(vmem_limit_bytes=24 << 20),
-        name="orbital_windows",
-    )(energies, orbitals)
-
-
-def potential_windows_kernel(vec, v_ref, pot_ref, halo_ref, *refs):
-    outs, planes_ref = refs[:-1], refs[-1]
+        name="edges",
+    )(*parts, *arrived)
+
+
+def with_edge_kernel(n, own_ref, edge_ref, *refs):
+    out_ref = refs[n]
     core = lax.axis_index("orb") % 2
-    strip = lax.axis_index("vec")
-    depth = v_ref.shape[1]
-    half = depth + GROUP
-    own = (1 - core) * GROUP
-    other = core * depth
-    for n in range(vec + 1):
-        src, part, to = (v_ref.at[0], 0, lax.rem(strip + n, vec)) if n < vec else (pot_ref, GROUP, strip)
-        for t in range(WTILES):
-            row = (n * half) * WTILES + (t % TILES) * SUB + t // TILES
-            lanes = tile_lanes(to, t)
-            planes_ref[pl.ds(row + own * WTILES, depth, WTILES), :] = src[:, lanes].astype(F32)
-            edge = halo_ref[:, lanes].astype(F32)[part : part + GROUP]
-            planes_ref[pl.ds(row + other * WTILES, GROUP, WTILES), :] = edge
-        pack_planes(planes_ref, n * half, outs[n], half // 2)
-
-
-def potential_windows(trial, potential, halo, vec):
-    half = potential.shape[0] + GROUP
+    pairs, edge = own_ref.shape[1], edge_ref.shape[1]
+    out_ref[:, pl.ds((1 - core) * edge, pairs)] = own_ref[...]
+    out_ref[:, pl.ds(core * pairs, edge)] = edge_ref[...]
+
+
+def with_edge(own, edge, arrived):
+    n, pairs, *block = own.shape
     return pl.pallas_call(
-        functools.partial(potential_windows_kernel, vec),
-        out_shape=[jax.ShapeDtypeStruct((half // 2, TILES, 2 * SUB, LANES), BF16)] * (vec + 1),
-        in_specs=[pl.BlockSpec(memory_space=pltpu.VMEM)] * 3,
-        out_specs=[pl.BlockSpec(memory_space=pltpu.VMEM)] * (vec + 1),
-        scratch_shapes=[pltpu.VMEM(((vec + 1) * half * WTILES, LANES), F32)],
+        functools.partial(with_edge_kernel, len(arrived)),
+        out_shape=jax.ShapeDtypeStruct((n, pairs + edge.shape[1], *block), own.dtype),
+        in_specs=[pl.BlockSpec(memory_space=pltpu.VMEM)] * (2 + len(arrived)),
+        out_specs=pl.BlockSpec(memory_space=pltpu.VMEM),
         compiler_params=pltpu.CompilerParams(vmem_limit_bytes=24 << 20),
-        name="potential_windows",
-    )(trial, potential, halo)
-
-
-def potential_rows_kernel(vec, mine_ref, other_ref, v_ref, d_ref):
+        name="with_edge",
+    )(own, edge, *arrived)
+
+
+def potential_rows_kernel(vec, n, mine_ref, other_ref, *refs):
+    v_ref, d_ref = refs[n:]
     core = lax.axis_index("orb") % 2
     strip = lax.axis_index("vec")
     pairs = mine_ref.shape[1]
@@ -316,22 +365,22 @@
                         d_ref[plane + zz] = 3.25 + block
             return carry
 
-        lax.fori_loop(0, pairs, one, 0)
-
-
-def potential_rows(mine, other, vec):
+        lax.fori_loop(0, pairs, one, 0, unroll=True)
+
+
+def potential_rows(mine, other, vec, arrived):
     planes = 4 * mine.shape[1]
     return pl.pallas_call(
-        functools.partial(potential_rows_kernel, vec),
+        functools.partial(potential_rows_kernel, vec, len(arrived)),
         out_shape=[
             jax.ShapeDtypeStruct((planes, vec * ROWS, LANES), F32),
             jax.ShapeDtypeStruct((planes, ROWS, LANES), F32),
         ],
-        in_specs=[pl.BlockSpec(memory_space=pltpu.VMEM)] * 2,
+        in_specs=[pl.BlockSpec(memory_space=pltpu.VMEM)] * (2 + len(arrived)),
         out_specs=[pl.BlockSpec(memory_space=pltpu.VMEM)] * 2,
         compiler_params=pltpu.CompilerParams(vmem_limit_bytes=24 << 20),
         name="potential_rows",
-    )(mine, other)
+    )(mine, other, *arrived)
 
 
 def solve_kernel(vec, first, last, *refs):
@@ -617,7 +666,7 @@
                     mixed = mixed + coefficients[s][k] * y[k * ROWS : (k + 1) * ROWS]
                 tiles = to_tiles([mixed[i * SUB : (i + 1) * SUB] for i in range(GROUP)])
                 for i in range(TILES):
-                    outs[s][z, (yt * TILES + i) * SUB : (yt * TILES + i + 1) * SUB, :] = tiles[i]
+                    outs[s][pl.ds((z * TILES + yt) * WTILES + i, SUB, TILES), :] = tiles[i]
 
 
 def back(got, basis, ndev, vec):
@@ -626,7 +675,7 @@
     return pl.pallas_call(
         functools.partial(back_kernel, ndev, vec),
         out_shape=[jax.ShapeDtypeStruct((vec, vec), F32)]
-        + [jax.ShapeDtypeStruct((zs, tiles, LANES), F32)] * vec,
+        + [jax.ShapeDtypeStruct((zs * tiles, LANES), F32)] * vec,
         in_specs=[pl.BlockSpec(memory_space=pltpu.VMEM)] * 2,
         out_specs=[pl.BlockSpec(memory_space=pltpu.VMEM)] * (vec + 1),
         compiler_params=pltpu.CompilerParams(vmem_limit_bytes=24 << 20),
@@ -635,34 +684,26 @@
 
 
 def assemble_kernel(vec, *refs):
-    gots, out_ref, all_ref = refs[:vec], refs[vec], refs[vec + 1]
-    strip = lax.axis_index("vec")
-    zs, tiles = gots[0].shape[:2]
-    depth = zs * vec
+    gots, out_ref = refs[:vec], refs[vec]
+    line = lax.axis_index("vec")
+    rows = gots[0].shape[0]
     for s in range(vec):
-        first = lax.rem(strip - s + vec, vec) * zs
-        for z in range(zs):
-            start = pl.multiple_of((first + z) * tiles, SUB)
-            all_ref[pl.ds(start, tiles), :] = gots[s][z]
-    for yt in range(TILES):
-        for i in range(TILES):
-            for g in range(SUB):
-                row = (yt * TILES + i) * SUB + g
-                tile = yt * WTILES + g * TILES + i
-                out_ref[0, :, tile * LANES : (tile + 1) * LANES] = all_ref[pl.ds(row, depth, tiles), :]
-
-
-def assemble(gots, vec):
-    zs, tiles = gots[0].shape[:2]
-    return pl.pallas_call(
+        start = pl.multiple_of(lax.rem(line - s + vec, vec) * rows, 8)
+        out_ref[pl.ds(start, rows), :] = gots[s][...]
+
+
+def assemble(gots):
+    vec = len(gots)
+    rows = gots[0].shape[0] * vec
+    out = pl.pallas_call(
         functools.partial(assemble_kernel, vec),
-        out_shape=jax.ShapeDtypeStruct((1, zs * vec, tiles * LANES), F32),
+        out_shape=jax.ShapeDtypeStruct((rows, LANES), F32),
         in_specs=[pl.BlockSpec(memory_space=pltpu.VMEM)] * vec,
         out_specs=pl.BlockSpec(memory_space=pltpu.VMEM),
-        scratch_shapes=[pltpu.VMEM((zs * vec * tiles, LANES), F32)],
         compiler_params=pltpu.CompilerParams(vmem_limit_bytes=24 << 20),
         name="assemble",
     )(*gots)
+    return out.reshape(1, rows * LANES // (NY * NX), NY * NX)
 
 
 def swap_cores(x, orb):
@@ -676,27 +717,26 @@
 
 def responses(orbitals, energies, trial_potential, local_potential):
     orb, vec = lax.axis_size("orb"), lax.axis_size("vec")
-    core = lax.axis_index("orb") % 2
-    depth = local_potential.shape[0]
     chips = orb // 2
-    edges = [
-        jnp.concatenate([trial_potential[0, at : at + GROUP], local_potential[at : at + GROUP]], 0)
-        for at in (0, depth - GROUP)
-    ]
-    edge = jnp.where(core == 0, edges[0], edges[1])
-    pairs = [(o, o + 1) for o in range(1, orb - 1, 2)] + [(o + 1, o) for o in range(1, orb - 1, 2)]
-    halo = lax.ppermute(edge, "orb", pairs)
-    windows = orbital_windows(orbitals, energies, orb)
-    psis = [windows[0]]
-    for r in range(1, chips):
+    psis, parts = windows(orbitals, energies, trial_potential, local_potential, orb, vec)
+    def to_chip(r):
         perm = [(2 * a + c, 2 * ((a + r) % chips) + c) for a in range(chips) for c in range(2)]
-        psis.append(lax.ppermute(windows[r], "orb", perm))
-    parts = potential_windows(trial_potential, local_potential, halo, vec)
-    mine = jnp.stack([parts[0]] + [shift(parts[n], "vec", n) for n in range(1, vec)] + [parts[vec]])
-    v, d = potential_rows(mine, swap_cores(mine, orb), vec)
+        return lax.ppermute(psis[r], "orb", perm)
+
+    order = [1, *range(2, chips - 1), chips - 1]
+    for r in order:
+        psis[r] = to_chip(r)
+    for n in range(1, vec):
+        parts[n] = shift(parts[n], "vec", n)
+    arrived = [psis[r] for r in order]
+    own, edge = edges(parts, arrived[:-2])
+    near = [(o, o + 1) for o in range(1, orb - 1, 2)] + [(o + 1, o) for o in range(1, orb - 1, 2)]
+    edge = lax.ppermute(edge, "orb", near + [(0, 0), (orb - 1, orb - 1)])
+    mine = with_edge(own, edge, arrived[-2:-1])
+    v, d = potential_rows(mine, swap_cores(mine, orb), vec, [])
     total = None
-    for r in range(chips):
-        total = solve_window(psis[r], v, d, total, vec, r == chips - 1)
+    for r in [0] + order:
+        total = solve_window(psis[r], v, d, total, vec, r == order[-1])
     return total[0], swap_cores(total[1], orb)
 
 
@@ -714,7 +754,7 @@
     got = lax.all_to_all(sent, both, 0, 0, tiled=True)
     factor, *slots = back(got, np_split(padded), ndev, vec)
     gots = [slots[0]] + [shift(slots[s], "vec", s) for s in range(1, vec)]
-    return assemble(gots, vec), factor
+    return assemble(gots), factor
 
 
 def solution(mesh):

time: 109 us -> 98 us (0.90)
  local copies, waits for them, and re-layouts: 5.43 us -> 0.05 us
  starting transfers between devices: 21.5 us -> 17.9 us
  blocking collectives: 44.9 us -> 41.8 us
    ppermute x4, waiting for transfers between devices: 3.03 us -> 6.59 us  [the longest x3 6.59 us: to_chip(): return lax.ppermute(psis[r], 'orb', perm)]
    unnamed x27 -> x16, local copies, waits for them, and re-layouts: 3.24 us -> 0.05 us
    all_to_all x2, blocking collectives: 44.9 us -> 41.8 us  [block_body(): got = lax.all_to_all(sent, both, 0, 0, tiled=True)]
    ppermute x2, starting transfers between devices: 4.16 us -> 1.33 us  [swap_cores(): return lax.ppermute(x, 'orb', [(o, o ^ 1) for o in range(orb)])]
    ppermute x6, waiting for transfers between devices: 7.56 us -> 4.74 us  [shift(): return lax.ppermute(x, axis, [(i, (i + count) % n) for i in range(n)])]
    ppermute x6, starting transfers between devices: 9.1 us -> 7.6 us  [shift(): return lax.ppermute(x, axis, [(i, (i + count) % n) for i in range(n)])]
    squeeze x1 -> x0, local copies, waits for them, and re-layouts: 1.15 us -> none  [responses(): trial_potential[0, at:at + GROUP]]
    pallas_call x3 -> x4, Pallas kernels: 2.78 us -> 2.89 us  [the longest x1 2.48 us: windows(): pl.pallas_call(functools.partial(windows_kernel, orb, vec), out_shape=out...]
  transfers between devices with their start and end apart: 12 -> 12, of which waited for: 8 -> 6; matrix products, arithmetic and copies ran while one was open for 0% -> 0% of each run, Pallas kernels for 11% -> 11%
where the time goes in v2:
time: 98 us; the launch traced here: 97.8 us
  blocking collectives  41.8 us (43%)
  Pallas kernels  23.2 us (24%)
  starting transfers between devices  17.9 us (18%)
  waiting for transfers between devices  13.5 us (14%)
  between operations  1.44 us (1%)
    all_to_all x2, blocking collectives, block_body(): got = lax.all_to_all(sent, both, 0, 0, tiled=True)  41.8 us
    pallas_call x4, Pallas kernels, solve_window(): pl.pallas_call(functools.partial(solve_kernel, vec, first, last), out_sha...  13.8 us
    ppermute x3, starting transfers between devices, to_chip(): return lax.ppermute(psis[r], 'orb', perm)  8.27 us
    ppermute x6, starting transfers between devices, shift(): return lax.ppermute(x, axis, [(i, (i + count) % n) for i in range(n)])  7.6 us
    ppermute x3, waiting for transfers between devices, to_chip(): return lax.ppermute(psis[r], 'orb', perm)  6.59 us
    ppermute x6, waiting for transfers between devices, shift(): return lax.ppermute(x, axis, [(i, (i + count) % n) for i in range(n)])  4.74 us
    pallas_call x1, Pallas kernels, spectral(): pl.pallas_call(functools.partial(spectral_kernel, orb, vec), out_shape=ja...  3.2 us
    pallas_call x1, Pallas kernels, windows(): pl.pallas_call(functools.partial(windows_kernel, orb, vec), out_shape=out...  2.48 us
  transfers between devices with their start and end apart: 12, of which 6 were waited for; matrix products, arithmetic and copies ran while one was open for 0% of the time, Pallas kernels for 11%

profile of v2, /device:TPU:0, one launch (start us, length us, event | category | flops | bytes accessed | tf_op | source)
XLA Modules:
  0.0 97.8 jit_solution(13569877867728680193)
XLA Ops:
  1.3 2.5 %windows.1 = (bf16[15,3,16,128]{3,2,1,0:T(8,128)(2,1)S(1)}, bf16[15,3,16,128]{3,2,1,0:T(8,128)(2,1)S(1)}, bf16[15,3,16,128]{3,2,1,0:T(8,128)(2,1)S(1)}, bf16[15,...) custom-call(f32[1]{0:T(128)S(6)} %copy.16.energy_ref, ...), custom_call_target="tpu_custom_call" | custom-call | tf_op jit(solution)/shard_map/windows/pallas_call | solution.py:283
  3.8 3.1 %collective-permute-start.4 = (bf16[15,3,16,128]{3,2,1,0:T(8,128)(2,1)S(1)}, bf16[15,3,16,128]{3,2,1,0:T(8,128)(2,1)S(1)}, u32[]{:S(2)}, u32[]{:S(2)}) collective-permute-start(bf16[15,3,16,128]{3,2,1,0:T(8,128)(2,1)S(1)} %get-tuple-element.28), channel_id=1, source_target_pairs={{0,8},{4,12},{8,16},{12,20},{16,24},{20,28},{24,0},{28,4},{1,9},{5... | collective-permute-start | bytes 552968 | tf_op jit(solution)/shard_map/ppermute | solution.py:724
  6.8 1.5 %collective-permute-start.1 = (bf16[6,3,16,128]{3,2,1,0:T(8,128)(2,1)S(1)}, bf16[6,3,16,128]{3,2,1,0:T(8,128)(2,1)S(1)}, u32[]{:S(2)}, u32[]{:S(2)}) collective-permute-start(bf16[6,3,16,128]{3,2,1,0:T(8,128)(2,1)S(1)} %get-tuple-element.24), channel_id=1, source_target_pairs={{0,1},{1,2},{2,3},{3,0},{4,5},{5,6},{6,7},{7,4},{8,9},{9,10},{10,1... | collective-permute-start | bytes 221192 | tf_op jit(solution)/shard_map/ppermute | solution.py:715
  8.3 1.5 %collective-permute-start.2 = (bf16[6,3,16,128]{3,2,1,0:T(8,128)(2,1)S(1)}, bf16[6,3,16,128]{3,2,1,0:T(8,128)(2,1)S(1)}, u32[]{:S(2)}, u32[]{:S(2)}) collective-permute-start(bf16[6,3,16,128]{3,2,1,0:T(8,128)(2,1)S(1)} %get-tuple-element.25), channel_id=1, source_target_pairs={{0,2},{1,3},{2,0},{3,1},{4,6},{5,7},{6,4},{7,5},{8,10},{9,11},{10,... | collective-permute-start | bytes 221192 | tf_op jit(solution)/shard_map/ppermute | solution.py:715
  9.9 1.4 %collective-permute-start.3 = (bf16[6,3,16,128]{3,2,1,0:T(8,128)(2,1)S(1)}, bf16[6,3,16,128]{3,2,1,0:T(8,128)(2,1)S(1)}, u32[]{:S(2)}, u32[]{:S(2)}) collective-permute-start(bf16[6,3,16,128]{3,2,1,0:T(8,128)(2,1)S(1)} %get-tuple-element.26), channel_id=1, source_target_pairs={{0,3},{1,0},{2,1},{3,2},{4,7},{5,4},{6,5},{7,6},{8,11},{9,8},{10,9... | collective-permute-start | bytes 221192 | tf_op jit(solution)/shard_map/ppermute | solution.py:715
  11.3 2.6 %collective-permute-start.6 = (bf16[15,3,16,128]{3,2,1,0:T(8,128)(2,1)S(1)}, bf16[15,3,16,128]{3,2,1,0:T(8,128)(2,1)S(1)}, u32[]{:S(2)}, u32[]{:S(2)}) collective-permute-start(bf16[15,3,16,128]{3,2,1,0:T(8,128)(2,1)S(1)} %get-tuple-element.31), channel_id=1, source_target_pairs={{0,16},{4,20},{8,24},{12,28},{16,0},{20,4},{24,8},{28,12},{1,17},{... | collective-permute-start | bytes 552968 | tf_op jit(solution)/shard_map/ppermute | solution.py:724
  14.9 6.6 %collective-permute-done.6.refs_0_ = bf16[15,3,16,128]{3,2,1,0:T(8,128)(2,1)S(1)} collective-permute-done((bf16[15,3,16,128]{3,2,1,0:T(8,128)(2,1)S(1)}, bf16[15,3,16,128]{3,2,1,0:T(8,128)(2,1)S(1)}, u32[]{:S(2)}, u32[]{:S(2)}) %collective-permute-start.6) | collective-permute-done | bytes 184352 | tf_op jit(solution)/shard_map/ppermute | solution.py:724
  21.6 1.1 %collective-permute-start.7 = (bf16[5,8,3,16,128]{4,3,2,1,0:T(8,128)(2,1)S(1)}, bf16[5,8,3,16,128]{4,3,2,1,0:T(8,128)(2,1)S(1)}, u32[]{:S(2)}, u32[]{:S(2)}) collective-permute-start(bf16[5,8,3,16,128]{4,3,2,1,0:T(8,128)(2,1)S(1)} %with_edge.1.mine_ref), channel_id=1, source_target_pairs={{0,4},{4,0},{8,12},{12,8},{16,20},{20,16},{24,28},{28,24},{1,5},{5... | collective-permute-start | bytes 1474568 | tf_op jit(solution)/shard_map/ppermute | solution.py:710
  22.7 2.6 %collective-permute-start = (bf16[15,3,16,128]{3,2,1,0:T(8,128)(2,1)S(1)}, bf16[15,3,16,128]{3,2,1,0:T(8,128)(2,1)S(1)}, u32[]{:S(2)}, u32[]{:S(2)}) collective-permute-start(bf16[15,3,16,128]{3,2,1,0:T(8,128)(2,1)S(1)} %get-tuple-element.22), channel_id=1, source_target_pairs={{0,24},{4,28},{8,0},{12,4},{16,8},{20,12},{24,16},{28,20},{1,25},{... | collective-permute-start | bytes 552968 | tf_op jit(solution)/shard_map/ppermute | solution.py:724
  25.6 3.3 %solve_window.4.refs_3_ = f32[24,128,128]{2,1,0:T(8,128)S(1)} custom-call(bf16[15,3,16,128]{3,2,1,0:T(8,128)(2,1)S(1)} %get-tuple-element.34.refs_0_, f32[32,128,128]{2,1,0:T(8,128)S(1)} %get-tuple-element.32.refs_1_, f32[32,32,128]{2,1,0:T(8,128)S(1)} %get-tuple-element.33.refs_2_), custom_call_target="tpu_custom_call" | custom-call | tf_op jit(solution)/shard_map/solve_window/pallas_call | solution.py:483
  28.9 3.4 %solve_window.5.refs_3_ = f32[24,128,128]{2,1,0:T(8,128)S(1)} custom-call(bf16[15,3,16,128]{3,2,1,0:T(8,128)(2,1)S(1)} %collective-permute-done.4.refs_5_.refs_0_, f32[32,128,128]{2,1,0:T(8,128)S(1)} %get-tuple-element.32.refs_1_, f32[32,32,128]{2,1,0:T(8,128)S(1)} %get-tuple-element.33.refs_2_, f32[24,128,128]{2,1,0:T(8,128)S(1)} %solve_window.4.refs_3_), custom_call_target="tpu_custom_call" | custom-call | tf_op jit(solution)/shard_map/solve_window/pallas_call | solution.py:483
  32.3 3.4 %solve_window.6.refs_3_ = f32[24,128,128]{2,1,0:T(8,128)S(1)} custom-call(bf16[15,3,16,128]{3,2,1,0:T(8,128)(2,1)S(1)} %collective-permute-done.6.refs_0_, f32[32,128,128]{2,1,0:T(8,128)S(1)} %get-tuple-element.32.refs_1_, f32[32,32,128]{2,1,0:T(8,128)S(1)} %get-tuple-element.33.refs_2_, f32[24,128,128]{2,1,0:T(8,128)S(1)} %solve_window.5.refs_3_), custom_call_target="tpu_custom_call" | custom-call | tf_op jit(solution)/shard_map/solve_window/pallas_call | solution.py:483
  35.7 3.7 %solve_window.7 = (f32[12,128,128]{2,1,0:T(8,128)S(1)}, f32[12,128,128]{2,1,0:T(8,128)S(1)}) custom-call(bf16[15,3,16,128]{3,2,1,0:T(8,128)(2,1)S(1)} %collective-permute-done.refs_0_, f32[32,128,128]{2,1,0:T(8,128)S(1)} %get-tuple-element.32.refs_1_, f32[32,32,128]{2,1,0:T(8,128)S(1)} %get-tuple-element.33.refs_2_, f32[24,128,128]{2,1,0:T(8,128)S(1)} %solve_window.6.refs_3_), custom_call_target="tpu_custom_call" | custom-call | tf_op jit(solution)/shard_map/solve_window/pallas_call | solution.py:483
  39.7 2.1 %collective-permute-done.8.other_ref = f32[12,128,128]{2,1,0:T(8,128)S(1)} collective-permute-done((f32[12,128,128]{2,1,0:T(8,128)S(1)}, f32[12,128,128]{2,1,0:T(8,128)S(1)}, u32[]{:S(2)}, u32[]{:S(2)}) %collective-permute-start.8) | collective-permute-done | bytes 786464 | tf_op jit(solution)/shard_map/ppermute | solution.py:710
  41.8 0.9 forward_x.1
  42.8 23.1 %all_to_all.10.got_ref = f32[32,40,128]{2,1,0:T(8,128)S(1)} all-to-all(f32[32,40,128]{2,1,0:T(8,128)S(1)} %bitcast.4), channel_id=1, replica_groups=mesh['orb'=8,'vec'=4] {'orb','vec'}, dimensions={0} | all-to-all | bytes 1310720 | tf_op jit(solution)/shard_map/all_to_all | solution.py:752
  66.0 3.2 %spectral.1 = f32[1024,128]{1,0:T(8,128)S(1)} custom-call(f32[96]{0:T(128)S(1)} %copy-done.7, f32[96,128]{1,0:T(8,128)S(1)} %copy-done.4, bf16[2,512,512]{2,1,0:T(8,128)(2,1)S(1)} %copy-done, bf16[2,288,320]{2,1,0:T(8,128)(2,1)S(1)} %copy-done.3, bf16[2,288,288]{2,1,0:T(8,128)(2,1)S(1)} %copy-done.2, bf16[2,512,384]{2,1,0:T(8,128)(2,1)S(1)} %copy-done.1, ...), custom_call_target="tpu_custom_call" | custom-call | tf_op jit(solution)/shard_map/spectral/pallas_call | solution.py:598
  69.2 18.7 %all_to_all.11 = f32[32,32,128]{2,1,0:T(8,128)S(1)} all-to-all(f32[32,32,128]{2,1,0:T(8,128)S(1)} %bitcast.5), channel_id=1, replica_groups=mesh['orb'=8,'vec'=4] {'orb','vec'}, dimensions={0} | all-to-all | bytes 1048576 | tf_op jit(solution)/shard_map/all_to_all | solution.py:754
  87.9 1.5 %back.1 = (f32[4,4]{1,0:T(4,128)}, f32[216,128]{1,0:T(8,128)S(1)}, f32[216,128]{1,0:T(8,128)S(1)}, f32[216,128]{1,0:T(8,128)S(1)}, f32[216,128]{1,0:T(8,128)S(1)}) custom-call(bf16[2,96,128]{2,1,0:T(8,128)(2,1)S(1)} %copy-done.5, f32[1024,128]{1,0:T(8,128)S(1)} %bitcast.6), custom_call_target="tpu_custom_call" | custom-call | tf_op jit(solution)/shard_map/back/pallas_call | solution.py:675
  89.6 1.5 %collective-permute-start.10 = (f32[216,128]{1,0:T(8,128)S(1)}, f32[216,128]{1,0:T(8,128)S(1)}, u32[]{:S(2)}, u32[]{:S(2)}) collective-permute-start(f32[216,128]{1,0:T(8,128)S(1)} %get-tuple-element.39), channel_id=1, source_target_pairs={{0,2},{1,3},{2,0},{3,1},{4,6},{5,7},{6,4},{7,5},{8,10},{9,11},{10,... | collective-permute-start | bytes 331784 | tf_op jit(solution)/shard_map/ppermute | solution.py:715
  91.1 1.4 %collective-permute-start.11 = (f32[216,128]{1,0:T(8,128)S(1)}, f32[216,128]{1,0:T(8,128)S(1)}, u32[]{:S(2)}, u32[]{:S(2)}) collective-permute-start(f32[216,128]{1,0:T(8,128)S(1)} %get-tuple-element.40), channel_id=1, source_target_pairs={{0,3},{1,0},{2,1},{3,2},{4,7},{5,4},{6,5},{7,6},{8,11},{9,8},{10,9... | collective-permute-start | bytes 331784 | tf_op jit(solution)/shard_map/ppermute | solution.py:715
  92.6 3.2 %collective-permute-done.9.refs_1_ = f32[216,128]{1,0:T(8,128)S(1)} collective-permute-done((f32[216,128]{1,0:T(8,128)S(1)}, f32[216,128]{1,0:T(8,128)S(1)}, u32[]{:S(2)}, u32[]{:S(2)}) %collective-permute-start.9) | collective-permute-done | bytes 110624 | tf_op jit(solution)/shard_map/ppermute | solution.py:715
  95.8 0.7 collective-permute-done.10.refs_2_
  97.0 0.8 assemble.1
  (30 shorter events, 2.4 us)
Async XLA Ops:
  3.8 10.4 %collective-permute-start.4 = (bf16[15,3,16,128]{3,2,1,0:T(8,128)(2,1)S(1)}, bf16[15,3,16,128]{3,2,1,0:T(8,128)(2,1)S(1)}, u32[]{:S(2)}, u32[]{:S(2)}) collective-permute-start(bf16[15,3,16,128]{3,2,1,0:T(8,128)(2,1)S(1)} %get-tuple-element.28), channel_id=1, source_target_pairs={{0,8},{4,12},{8,16},{12,20},{16,24},{20,28},{24,0},{28,4},{1,9},{5... | collective-permute-start | bytes 552968 | tf_op jit(solution)/shard_map/ppermute | solution.py:724
  6.8 7.0 %collective-permute-start.1 = (bf16[6,3,16,128]{3,2,1,0:T(8,128)(2,1)S(1)}, bf16[6,3,16,128]{3,2,1,0:T(8,128)(2,1)S(1)}, u32[]{:S(2)}, u32[]{:S(2)}) collective-permute-start(bf16[6,3,16,128]{3,2,1,0:T(8,128)(2,1)S(1)} %get-tuple-element.24), channel_id=1, source_target_pairs={{0,1},{1,2},{2,3},{3,0},{4,5},{5,6},{6,7},{7,4},{8,9},{9,10},{10,1... | collective-permute-start | bytes 221192 | tf_op jit(solution)/shard_map/ppermute | solution.py:715
  8.3 5.5 %collective-permute-start.2 = (bf16[6,3,16,128]{3,2,1,0:T(8,128)(2,1)S(1)}, bf16[6,3,16,128]{3,2,1,0:T(8,128)(2,1)S(1)}, u32[]{:S(2)}, u32[]{:S(2)}) collective-permute-start(bf16[6,3,16,128]{3,2,1,0:T(8,128)(2,1)S(1)} %get-tuple-element.25), channel_id=1, source_target_pairs={{0,2},{1,3},{2,0},{3,1},{4,6},{5,7},{6,4},{7,5},{8,10},{9,11},{10,... | collective-permute-start | bytes 221192 | tf_op jit(solution)/shard_map/ppermute | solution.py:715
  9.9 4.4 %collective-permute-start.3 = (bf16[6,3,16,128]{3,2,1,0:T(8,128)(2,1)S(1)}, bf16[6,3,16,128]{3,2,1,0:T(8,128)(2,1)S(1)}, u32[]{:S(2)}, u32[]{:S(2)}) collective-permute-start(bf16[6,3,16,128]{3,2,1,0:T(8,128)(2,1)S(1)} %get-tuple-element.26), channel_id=1, source_target_pairs={{0,3},{1,0},{2,1},{3,2},{4,7},{5,4},{6,5},{7,6},{8,11},{9,8},{10,9... | collective-permute-start | bytes 221192 | tf_op jit(solution)/shard_map/ppermute | solution.py:715
  11.3 10.2 %collective-permute-start.6 = (bf16[15,3,16,128]{3,2,1,0:T(8,128)(2,1)S(1)}, bf16[15,3,16,128]{3,2,1,0:T(8,128)(2,1)S(1)}, u32[]{:S(2)}, u32[]{:S(2)}) collective-permute-start(bf16[15,3,16,128]{3,2,1,0:T(8,128)(2,1)S(1)} %get-tuple-element.31), channel_id=1, source_target_pairs={{0,16},{4,20},{8,24},{12,28},{16,0},{20,4},{24,8},{28,12},{1,17},{... | collective-permute-start | bytes 552968 | tf_op jit(solution)/shard_map/ppermute | solution.py:724
  14.2 7.3 %collective-permute-start.5 = (bf16[5,2,3,16,128]{4,3,2,1,0:T(8,128)(2,1)S(1)}, bf16[5,2,3,16,128]{4,3,2,1,0:T(8,128)(2,1)S(1)}, u32[]{:S(2)}, u32[]{:S(2)}) collective-permute-start(bf16[5,2,3,16,128]{4,3,2,1,0:T(8,128)(2,1)S(1)} %get-tuple-element.30), channel_id=1, source_target_pairs={{4,8},{12,16},{20,24},{8,4},{16,12},{24,20},{0,0},{28,28},{5,9},{1... | collective-permute-start | bytes 368648 | tf_op jit(solution)/shard_map/ppermute | solution.py:734
  21.6 3.7 %collective-permute-start.7 = (bf16[5,8,3,16,128]{4,3,2,1,0:T(8,128)(2,1)S(1)}, bf16[5,8,3,16,128]{4,3,2,1,0:T(8,128)(2,1)S(1)}, u32[]{:S(2)}, u32[]{:S(2)}) collective-permute-start(bf16[5,8,3,16,128]{4,3,2,1,0:T(8,128)(2,1)S(1)} %with_edge.1.mine_ref), channel_id=1, source_target_pairs={{0,4},{4,0},{8,12},{12,8},{16,20},{20,16},{24,28},{28,24},{1,5},{5... | collective-permute-start | bytes 1474568 | tf_op jit(solution)/shard_map/ppermute | solution.py:710
  22.7 13.1 %collective-permute-start = (bf16[15,3,16,128]{3,2,1,0:T(8,128)(2,1)S(1)}, bf16[15,3,16,128]{3,2,1,0:T(8,128)(2,1)S(1)}, u32[]{:S(2)}, u32[]{:S(2)}) collective-permute-start(bf16[15,3,16,128]{3,2,1,0:T(8,128)(2,1)S(1)} %get-tuple-element.22), channel_id=1, source_target_pairs={{0,24},{4,28},{8,0},{12,4},{16,8},{20,12},{24,16},{28,20},{1,25},{... | collective-permute-start | bytes 552968 | tf_op jit(solution)/shard_map/ppermute | solution.py:724
  35.7 6.1 %copy-start.6 = (bf16[2,96,128]{2,1,0:T(8,128)(2,1)S(1)}, bf16[2,96,128]{2,1,0:T(8,128)(2,1)}, u32[]{:S(2)}) copy-start(bf16[2,96,128]{2,1,0:T(8,128)(2,1)} %constant.16.clone.basis_ref) | copy-start | bytes 147460
  39.4 2.4 %collective-permute-start.8 = (f32[12,128,128]{2,1,0:T(8,128)S(1)}, f32[12,128,128]{2,1,0:T(8,128)S(1)}, u32[]{:S(2)}, u32[]{:S(2)}) collective-permute-start(f32[12,128,128]{2,1,0:T(8,128)S(1)} %get-tuple-element.36), channel_id=1, source_target_pairs={{0,4},{4,0},{8,12},{12,8},{16,20},{20,16},{24,28},{28,24},{1,5},{5... | collective-permute-start | bytes 2359304 | tf_op jit(solution)/shard_map/ppermute | solution.py:710
  41.8 24.1 %copy-start = (bf16[2,512,512]{2,1,0:T(8,128)(2,1)S(1)}, bf16[2,512,512]{2,1,0:T(8,128)(2,1)}, u32[]{:S(2)}) copy-start(bf16[2,512,512]{2,1,0:T(8,128)(2,1)} %constant.19.clone.wy_ref) | copy-start | bytes 3145732
  41.8 24.1 %copy-start.1 = (bf16[2,512,384]{2,1,0:T(8,128)(2,1)S(1)}, bf16[2,512,384]{2,1,0:T(8,128)(2,1)}, u32[]{:S(2)}) copy-start(bf16[2,512,384]{2,1,0:T(8,128)(2,1)} %constant.22.clone.wyb_ref) | copy-start | bytes 2359300
  41.8 24.1 %copy-start.2 = (bf16[2,288,288]{2,1,0:T(8,128)(2,1)S(1)}, bf16[2,288,288]{2,1,0:T(8,128)(2,1)}, u32[]{:S(2)}) copy-start(bf16[2,288,288]{2,1,0:T(8,128)(2,1)} %constant.21.clone.kzb_ref) | copy-start | bytes 995332
  41.8 24.1 %copy-start.3 = (bf16[2,288,320]{2,1,0:T(8,128)(2,1)S(1)}, bf16[2,288,320]{2,1,0:T(8,128)(2,1)}, u32[]{:S(2)}) copy-start(bf16[2,288,320]{2,1,0:T(8,128)(2,1)} %constant.20.clone.kz_ref) | copy-start | bytes 1105924
  41.8 24.1 %copy-start.4 = (f32[96,128]{1,0:T(8,128)S(1)}, f32[96,128]{1,0:T(8,128)}, u32[]{:S(2)}) copy-start(f32[96,128]{1,0:T(8,128)} %constant.18.clone.muzy_ref) | copy-start | bytes 147460
  41.8 24.1 %copy-start.7 = (f32[96]{0:T(128)S(1)}, f32[96]{0:T(128)}, u32[]{:S(2)}) copy-start(f32[96]{0:T(128)} %constant.17.clone.mux_ref) | copy-start | bytes 1156
  65.9 21.9 %copy-start.5 = (bf16[2,96,128]{2,1,0:T(8,128)(2,1)S(1)}, bf16[2,96,128]{2,1,0:T(8,128)(2,1)}, u32[]{:S(2)}) copy-start(bf16[2,96,128]{2,1,0:T(8,128)(2,1)} %constant.23.clone.basis_ref) | copy-start | bytes 147460
  89.4 6.4 %collective-permute-start.9 = (f32[216,128]{1,0:T(8,128)S(1)}, f32[216,128]{1,0:T(8,128)S(1)}, u32[]{:S(2)}, u32[]{:S(2)}) collective-permute-start(f32[216,128]{1,0:T(8,128)S(1)} %get-tuple-element.38), channel_id=1, source_target_pairs={{0,1},{1,2},{2,3},{3,0},{4,5},{5,6},{6,7},{7,4},{8,9},{9,10},{10,1... | collective-permute-start | bytes 331784 | tf_op jit(solution)/shard_map/ppermute | solution.py:715
  89.6 6.9 %collective-permute-start.10 = (f32[216,128]{1,0:T(8,128)S(1)}, f32[216,128]{1,0:T(8,128)S(1)}, u32[]{:S(2)}, u32[]{:S(2)}) collective-permute-start(f32[216,128]{1,0:T(8,128)S(1)} %get-tuple-element.39), channel_id=1, source_target_pairs={{0,2},{1,3},{2,0},{3,1},{4,6},{5,7},{6,4},{7,5},{8,10},{9,11},{10,... | collective-permute-start | bytes 331784 | tf_op jit(solution)/shard_map/ppermute | solution.py:715
  91.1 5.9 %collective-permute-start.11 = (f32[216,128]{1,0:T(8,128)S(1)}, f32[216,128]{1,0:T(8,128)S(1)}, u32[]{:S(2)}, u32[]{:S(2)}) collective-permute-start(f32[216,128]{1,0:T(8,128)S(1)} %get-tuple-element.40), channel_id=1, source_target_pairs={{0,3},{1,0},{2,1},{3,2},{4,7},{5,4},{6,5},{7,6},{8,11},{9,8},{10,9... | collective-permute-start | bytes 331784 | tf_op jit(solution)/shard_map/ppermute | solution.py:715

commit v3 on v2

--- a/solution.py
+++ b/solution.py
@@ -19,6 +19,13 @@
 F32 = jnp.float32
 LANES = 128
 WEIGHTS = [1.0 / (1.0 + 0.8 * math.cos(math.pi * (2 * s + 1) / (2 * STEPS))) for s in range(STEPS)]
+
+SCALES = [WEIGHTS[0]]
+for weight_ in WEIGHTS[1:]:
+    SCALES.append((1.0 - weight_) * SCALES[-1])
+COEFFICIENTS = [None] + [
+    (1.0, WEIGHTS[s] / SCALES[s], WEIGHTS[s] * SCALES[s - 1] / SCALES[s]) for s in range(1, STEPS)
+]
 
 
 def neighbours(field):
@@ -415,50 +422,51 @@
             there = jnp.where((z >= 0) & (z < NZ), 1.0, 0.0)
             psi = jnp.concatenate([rows[i][zz * SUB : (zz + 1) * SUB] for i in range(GROUP)], 0)
             h = inside * there / (d_ref[w] - energy)
-            psi_s[w] = psi
+            psi_s[w] = SCALES[STEPS - 1] * psi
             h_s[w] = h
             scaled = -2.0 * psi * h
             for k in range(vec):
                 rows_k = pl.ds(k * ROWS, ROWS)
-                c = scaled * v_ref[w, rows_k, :]
-                c_s[w, rows_k, :] = c
-                u_a[w, rows_k, :] = WEIGHTS[0] * c
+                c_s[w, rows_k, :] = scaled * v_ref[w, rows_k, :]
         return carry
 
     lax.fori_loop(0, psi_ref.shape[0], begin, 0, unroll=5)
 
-    def stepped(src, w, weight):
+    def stepped(src, w, step):
         u = src[w]
         high, low = split(u)
         x = jnp.dot(jnp.concatenate([high, low], 1), beside, preferred_element_type=F32)
         near = x + (src[w - 1] + src[w + 1])
-        h = h_s[w]
+        own, given, around = COEFFICIENTS[step]
+        h = around * h_s[w]
         new = []
         for k in range(vec):
             rows = [u[k * ROWS + i * SUB : k * ROWS + (i + 1) * SUB] for i in range(GROUP)]
             north = jnp.concatenate([pltpu.roll(rows[-1], 1, 0)] + rows[:-1], 0)
             south = jnp.concatenate(rows[1:] + [pltpu.roll(rows[0], SUB - 1, 0)], 0)
             at_k = slice(k * ROWS, (k + 1) * ROWS)
-            total = near[at_k] + (north + south)
-            change = c_s[w, at_k, :] + h * total
-            new.append((1.0 - weight) * u[at_k] + weight * change)
+            change = h * (near[at_k] + (north + south))
+            if src is c_s:
+                new.append((own + given) * u[at_k] + change)
+            else:
+                new.append((u[at_k] + given * c_s[w, at_k, :]) + change)
         return new
 
-    src, dst = u_a, u_b
+    src, dst = c_s, u_a
     for step in range(1, STEPS - 1):
         low = GROUP - HALO + step
 
         def middle(w, carry, src=src, dst=dst, step=step):
-            dst[w] = jnp.concatenate(stepped(src, w, WEIGHTS[step]), 0)
+            dst[w] = jnp.concatenate(stepped(src, w, step), 0)
             return carry
 
         lax.fori_loop(low, planes - low, middle, 0, unroll=True)
-        src, dst = dst, src
+        src, dst = dst, (u_b if dst is u_a else u_a)
 
     def end(p, carry, out, start, src=src):
         w = GROUP + start + p
         psi = psi_s[w]
-        total = jnp.concatenate([psi * new for new in stepped(src, w, WEIGHTS[STEPS - 1])], 0)
+        total = jnp.concatenate([psi * new for new in stepped(src, w, STEPS - 1)], 0)
         if not first:
             total = total + sum_ref[start + p]
         out[p] = total
@@ -723,16 +731,16 @@
         perm = [(2 * a + c, 2 * ((a + r) % chips) + c) for a in range(chips) for c in range(2)]
         return lax.ppermute(psis[r], "orb", perm)
 
-    order = [1, *range(2, chips - 1), chips - 1]
+    order = [1, chips - 1, *range(2, chips - 1)]
     for r in order:
         psis[r] = to_chip(r)
     for n in range(1, vec):
         parts[n] = shift(parts[n], "vec", n)
     arrived = [psis[r] for r in order]
-    own, edge = edges(parts, arrived[:-2])
+    own, edge = edges(parts, [])
     near = [(o, o + 1) for o in range(1, orb - 1, 2)] + [(o + 1, o) for o in range(1, orb - 1, 2)]
     edge = lax.ppermute(edge, "orb", near + [(0, 0), (orb - 1, orb - 1)])
-    mine = with_edge(own, edge, arrived[-2:-1])
+    mine = with_edge(own, edge, arrived[:2])
     v, d = potential_rows(mine, swap_cores(mine, orb), vec, [])
     total = None
     for r in [0] + order:

time: 98 us -> 93.7 us (0.956)
  Pallas kernels: 23.2 us -> 21.3 us
  starting transfers between devices: 17.9 us -> 16.4 us
  blocking collectives: 41.8 us -> 40.6 us
    ppermute x3, starting transfers between devices: 8.27 us -> 5.37 us  [to_chip(): return lax.ppermute(psis[r], 'orb', perm)]
    pallas_call x4, Pallas kernels: 13.8 us -> 12 us  [solve_window(): pl.pallas_call(functools.partial(solve_kernel, vec, first, last), out_sha...]
    ppermute x6, starting transfers between devices: 7.6 us -> 9.1 us  [shift(): return lax.ppermute(x, axis, [(i, (i + count) % n) for i in range(n)])]
    all_to_all x2, blocking collectives: 41.8 us -> 40.6 us  [block_body(): got = lax.all_to_all(sent, both, 0, 0, tiled=True)]
  transfers between devices with their start and end apart: 12 -> 12, of which waited for: 6 -> 7; matrix products, arithmetic and copies ran while one was open for 0% -> 0% of each run, Pallas kernels for 11% -> 10%
where the time goes in v3:
time: 93.7 us; the launch traced here: 93.4 us
  blocking collectives  40.6 us (43%)
  Pallas kernels  21.3 us (23%)
  starting transfers between devices  16.4 us (18%)
  waiting for transfers between devices  13.6 us (15%)
  between operations  1.45 us (2%)
    all_to_all x2, blocking collectives, block_body(): got = lax.all_to_all(sent, both, 0, 0, tiled=True)  40.6 us
    pallas_call x4, Pallas kernels, solve_window(): pl.pallas_call(functools.partial(solve_kernel, vec, first, last), out_sha...  12 us
    ppermute x6, starting transfers between devices, shift(): return lax.ppermute(x, axis, [(i, (i + count) % n) for i in range(n)])  9.1 us
    ppermute x3, waiting for transfers between devices, to_chip(): return lax.ppermute(psis[r], 'orb', perm)  6.91 us
    ppermute x3, starting transfers between devices, to_chip(): return lax.ppermute(psis[r], 'orb', perm)  5.37 us
    ppermute x6, waiting for transfers between devices, shift(): return lax.ppermute(x, axis, [(i, (i + count) % n) for i in range(n)])  4.43 us
    pallas_call x1, Pallas kernels, spectral(): pl.pallas_call(functools.partial(spectral_kernel, orb, vec), out_shape=ja...  3.2 us
    pallas_call x1, Pallas kernels, windows(): pl.pallas_call(functools.partial(windows_kernel, orb, vec), out_shape=out...  2.48 us
  transfers between devices with their start and end apart: 12, of which 7 were waited for; matrix products, arithmetic and copies ran while one was open for 0% of the time, Pallas kernels for 10%

profile of v3, /device:TPU:0, one launch (start us, length us, event | category | flops | bytes accessed | tf_op | source)
XLA Modules:
  0.0 93.4 jit_solution(968055973388328451)
XLA Ops:
  1.3 2.5 %windows.1 = (bf16[15,3,16,128]{3,2,1,0:T(8,128)(2,1)S(1)}, bf16[15,3,16,128]{3,2,1,0:T(8,128)(2,1)S(1)}, bf16[15,3,16,128]{3,2,1,0:T(8,128)(2,1)S(1)}, bf16[15,...) custom-call(f32[1]{0:T(128)S(6)} %copy.16.energy_ref, ...), custom_call_target="tpu_custom_call" | custom-call | tf_op jit(solution)/shard_map/windows/pallas_call | solution.py:290
  3.8 3.0 %collective-permute-start.1 = (bf16[6,3,16,128]{3,2,1,0:T(8,128)(2,1)S(1)}, bf16[6,3,16,128]{3,2,1,0:T(8,128)(2,1)S(1)}, u32[]{:S(2)}, u32[]{:S(2)}) collective-permute-start(bf16[6,3,16,128]{3,2,1,0:T(8,128)(2,1)S(1)} %get-tuple-element.24), channel_id=1, source_target_pairs={{0,1},{1,2},{2,3},{3,0},{4,5},{5,6},{6,7},{7,4},{8,9},{9,10},{10,1... | collective-permute-start | bytes 221192 | tf_op jit(solution)/shard_map/ppermute | solution.py:723
  6.8 1.5 %collective-permute-start.2 = (bf16[6,3,16,128]{3,2,1,0:T(8,128)(2,1)S(1)}, bf16[6,3,16,128]{3,2,1,0:T(8,128)(2,1)S(1)}, u32[]{:S(2)}, u32[]{:S(2)}) collective-permute-start(bf16[6,3,16,128]{3,2,1,0:T(8,128)(2,1)S(1)} %get-tuple-element.25), channel_id=1, source_target_pairs={{0,2},{1,3},{2,0},{3,1},{4,6},{5,7},{6,4},{7,5},{8,10},{9,11},{10,... | collective-permute-start | bytes 221192 | tf_op jit(solution)/shard_map/ppermute | solution.py:723
  8.3 1.4 %collective-permute-start.3 = (bf16[6,3,16,128]{3,2,1,0:T(8,128)(2,1)S(1)}, bf16[6,3,16,128]{3,2,1,0:T(8,128)(2,1)S(1)}, u32[]{:S(2)}, u32[]{:S(2)}) collective-permute-start(bf16[6,3,16,128]{3,2,1,0:T(8,128)(2,1)S(1)} %get-tuple-element.26), channel_id=1, source_target_pairs={{0,3},{1,0},{2,1},{3,2},{4,7},{5,4},{6,5},{7,6},{8,11},{9,8},{10,9... | collective-permute-start | bytes 221192 | tf_op jit(solution)/shard_map/ppermute | solution.py:723
  9.7 1.6 %collective-permute-start.5 = (bf16[15,3,16,128]{3,2,1,0:T(8,128)(2,1)S(1)}, bf16[15,3,16,128]{3,2,1,0:T(8,128)(2,1)S(1)}, u32[]{:S(2)}, u32[]{:S(2)}) collective-permute-start(bf16[15,3,16,128]{3,2,1,0:T(8,128)(2,1)S(1)} %get-tuple-element.30), channel_id=1, source_target_pairs={{0,8},{4,12},{8,16},{12,20},{16,24},{20,28},{24,0},{28,4},{1,9},{5... | collective-permute-start | bytes 552968 | tf_op jit(solution)/shard_map/ppermute | solution.py:732
  11.3 2.2 %collective-permute-start.6 = (bf16[15,3,16,128]{3,2,1,0:T(8,128)(2,1)S(1)}, bf16[15,3,16,128]{3,2,1,0:T(8,128)(2,1)S(1)}, u32[]{:S(2)}, u32[]{:S(2)}) collective-permute-start(bf16[15,3,16,128]{3,2,1,0:T(8,128)(2,1)S(1)} %get-tuple-element.31), channel_id=1, source_target_pairs={{0,24},{4,28},{8,0},{12,4},{16,8},{20,12},{24,16},{28,20},{1,25},{... | collective-permute-start | bytes 552968 | tf_op jit(solution)/shard_map/ppermute | solution.py:732
  14.3 4.8 %collective-permute-done.5.refs_0_ = bf16[15,3,16,128]{3,2,1,0:T(8,128)(2,1)S(1)} collective-permute-done((bf16[15,3,16,128]{3,2,1,0:T(8,128)(2,1)S(1)}, bf16[15,3,16,128]{3,2,1,0:T(8,128)(2,1)S(1)}, u32[]{:S(2)}, u32[]{:S(2)}) %collective-permute-start.5) | collective-permute-done | bytes 184352 | tf_op jit(solution)/shard_map/ppermute | solution.py:732
  19.1 1.4 %collective-permute-done.6.refs_1_.refs_0_ = bf16[15,3,16,128]{3,2,1,0:T(8,128)(2,1)S(1)} collective-permute-done((bf16[15,3,16,128]{3,2,1,0:T(8,128)(2,1)S(1)}, bf16[15,3,16,128]{3,2,1,0:T(8,128)(2,1)S(1)}, u32[]{:S(2)}, u32[]{:S(2)}) %collective-permute-start.6) | collective-permute-done | bytes 184352 | tf_op jit(solution)/shard_map/ppermute | solution.py:732
  20.6 1.2 %collective-permute-start.7 = (bf16[5,8,3,16,128]{4,3,2,1,0:T(8,128)(2,1)S(1)}, bf16[5,8,3,16,128]{4,3,2,1,0:T(8,128)(2,1)S(1)}, u32[]{:S(2)}, u32[]{:S(2)}) collective-permute-start(bf16[5,8,3,16,128]{4,3,2,1,0:T(8,128)(2,1)S(1)} %with_edge.1.mine_ref), channel_id=1, source_target_pairs={{0,4},{4,0},{8,12},{12,8},{16,20},{20,16},{24,28},{28,24},{1,5},{5... | collective-permute-start | bytes 1474568 | tf_op jit(solution)/shard_map/ppermute | solution.py:718
  21.8 1.6 %collective-permute-start = (bf16[15,3,16,128]{3,2,1,0:T(8,128)(2,1)S(1)}, bf16[15,3,16,128]{3,2,1,0:T(8,128)(2,1)S(1)}, u32[]{:S(2)}, u32[]{:S(2)}) collective-permute-start(bf16[15,3,16,128]{3,2,1,0:T(8,128)(2,1)S(1)} %get-tuple-element.22), channel_id=1, source_target_pairs={{0,16},{4,20},{8,24},{12,28},{16,0},{20,4},{24,8},{28,12},{1,17},{... | collective-permute-start | bytes 552968 | tf_op jit(solution)/shard_map/ppermute | solution.py:732
  23.6 2.9 %solve_window.4.refs_3_ = f32[24,128,128]{2,1,0:T(8,128)S(1)} custom-call(bf16[15,3,16,128]{3,2,1,0:T(8,128)(2,1)S(1)} %get-tuple-element.34.refs_0_, f32[32,128,128]{2,1,0:T(8,128)S(1)} %get-tuple-element.32.refs_1_, f32[32,32,128]{2,1,0:T(8,128)S(1)} %get-tuple-element.33.refs_2_), custom_call_target="tpu_custom_call" | custom-call | tf_op jit(solution)/shard_map/solve_window/pallas_call | solution.py:491
  26.5 3.0 %solve_window.5.refs_3_ = f32[24,128,128]{2,1,0:T(8,128)S(1)} custom-call(bf16[15,3,16,128]{3,2,1,0:T(8,128)(2,1)S(1)} %collective-permute-done.5.refs_0_, f32[32,128,128]{2,1,0:T(8,128)S(1)} %get-tuple-element.32.refs_1_, f32[32,32,128]{2,1,0:T(8,128)S(1)} %get-tuple-element.33.refs_2_, f32[24,128,128]{2,1,0:T(8,128)S(1)} %solve_window.4.refs_3_), custom_call_target="tpu_custom_call" | custom-call | tf_op jit(solution)/shard_map/solve_window/pallas_call | solution.py:491
  29.5 3.0 %solve_window.6.refs_3_ = f32[24,128,128]{2,1,0:T(8,128)S(1)} custom-call(bf16[15,3,16,128]{3,2,1,0:T(8,128)(2,1)S(1)} %collective-permute-done.6.refs_1_.refs_0_, f32[32,128,128]{2,1,0:T(8,128)S(1)} %get-tuple-element.32.refs_1_, f32[32,32,128]{2,1,0:T(8,128)S(1)} %get-tuple-element.33.refs_2_, f32[24,128,128]{2,1,0:T(8,128)S(1)} %solve_window.5.refs_3_), custom_call_target="tpu_custom_call" | custom-call | tf_op jit(solution)/shard_map/solve_window/pallas_call | solution.py:491
  33.2 3.1 %solve_window.7 = (f32[12,128,128]{2,1,0:T(8,128)S(1)}, f32[12,128,128]{2,1,0:T(8,128)S(1)}) custom-call(bf16[15,3,16,128]{3,2,1,0:T(8,128)(2,1)S(1)} %collective-permute-done.refs_0_, f32[32,128,128]{2,1,0:T(8,128)S(1)} %get-tuple-element.32.refs_1_, f32[32,32,128]{2,1,0:T(8,128)S(1)} %get-tuple-element.33.refs_2_, f32[24,128,128]{2,1,0:T(8,128)S(1)} %solve_window.6.refs_3_), custom_call_target="tpu_custom_call" | custom-call | tf_op jit(solution)/shard_map/solve_window/pallas_call | solution.py:491
  36.4 2.3 %collective-permute-done.8.other_ref = f32[12,128,128]{2,1,0:T(8,128)S(1)} collective-permute-done((f32[12,128,128]{2,1,0:T(8,128)S(1)}, f32[12,128,128]{2,1,0:T(8,128)S(1)}, u32[]{:S(2)}, u32[]{:S(2)}) %collective-permute-start.8) | collective-permute-done | bytes 786464 | tf_op jit(solution)/shard_map/ppermute | solution.py:718
  38.7 0.9 %forward_x.1 = f32[1280,128]{1,0:T(8,128)S(1)} custom-call(bf16[2,96,128]{2,1,0:T(8,128)(2,1)S(1)} %copy-done.6, f32[12,128,128]{2,1,0:T(8,128)S(1)} %get-tuple-element.35.own_ref, f32[12,128,128]{2,1,0:T(8,128)S(1)} %collective-permute-done.8.other_ref), custom_call_target="tpu_custom_call" | custom-call | tf_op jit(solution)/shard_map/forward_x/pallas_call | solution.py:520
  39.7 21.9 %all_to_all.10.got_ref = f32[32,40,128]{2,1,0:T(8,128)S(1)} all-to-all(f32[32,40,128]{2,1,0:T(8,128)S(1)} %bitcast.4), channel_id=1, replica_groups=mesh['orb'=8,'vec'=4] {'orb','vec'}, dimensions={0} | all-to-all | bytes 1310720 | tf_op jit(solution)/shard_map/all_to_all | solution.py:760
  61.6 3.2 %spectral.1 = f32[1024,128]{1,0:T(8,128)S(1)} custom-call(f32[96]{0:T(128)S(1)} %copy-done.7, f32[96,128]{1,0:T(8,128)S(1)} %copy-done.4, bf16[2,512,512]{2,1,0:T(8,128)(2,1)S(1)} %copy-done, bf16[2,288,320]{2,1,0:T(8,128)(2,1)S(1)} %copy-done.3, bf16[2,288,288]{2,1,0:T(8,128)(2,1)S(1)} %copy-done.2, bf16[2,512,384]{2,1,0:T(8,128)(2,1)S(1)} %copy-done.1, ...), custom_call_target="tpu_custom_call" | custom-call | tf_op jit(solution)/shard_map/spectral/pallas_call | solution.py:606
  64.8 18.7 %all_to_all.11 = f32[32,32,128]{2,1,0:T(8,128)S(1)} all-to-all(f32[32,32,128]{2,1,0:T(8,128)S(1)} %bitcast.5), channel_id=1, replica_groups=mesh['orb'=8,'vec'=4] {'orb','vec'}, dimensions={0} | all-to-all | bytes 1048576 | tf_op jit(solution)/shard_map/all_to_all | solution.py:762
  83.5 1.5 %back.1 = (f32[4,4]{1,0:T(4,128)}, f32[216,128]{1,0:T(8,128)S(1)}, f32[216,128]{1,0:T(8,128)S(1)}, f32[216,128]{1,0:T(8,128)S(1)}, f32[216,128]{1,0:T(8,128)S(1)}) custom-call(bf16[2,96,128]{2,1,0:T(8,128)(2,1)S(1)} %copy-done.5, f32[1024,128]{1,0:T(8,128)S(1)} %bitcast.6), custom_call_target="tpu_custom_call" | custom-call | tf_op jit(solution)/shard_map/back/pallas_call | solution.py:683
  85.3 1.5 %collective-permute-start.10 = (f32[216,128]{1,0:T(8,128)S(1)}, f32[216,128]{1,0:T(8,128)S(1)}, u32[]{:S(2)}, u32[]{:S(2)}) collective-permute-start(f32[216,128]{1,0:T(8,128)S(1)} %get-tuple-element.39), channel_id=1, source_target_pairs={{0,2},{1,3},{2,0},{3,1},{4,6},{5,7},{6,4},{7,5},{8,10},{9,11},{10,... | collective-permute-start | bytes 331784 | tf_op jit(solution)/shard_map/ppermute | solution.py:723
  86.8 1.4 %collective-permute-start.11 = (f32[216,128]{1,0:T(8,128)S(1)}, f32[216,128]{1,0:T(8,128)S(1)}, u32[]{:S(2)}, u32[]{:S(2)}) collective-permute-start(f32[216,128]{1,0:T(8,128)S(1)} %get-tuple-element.40), channel_id=1, source_target_pairs={{0,3},{1,0},{2,1},{3,2},{4,7},{5,4},{6,5},{7,6},{8,11},{9,8},{10,9... | collective-permute-start | bytes 331784 | tf_op jit(solution)/shard_map/ppermute | solution.py:723
  88.2 3.2 %collective-permute-done.9.refs_1_ = f32[216,128]{1,0:T(8,128)S(1)} collective-permute-done((f32[216,128]{1,0:T(8,128)S(1)}, f32[216,128]{1,0:T(8,128)S(1)}, u32[]{:S(2)}, u32[]{:S(2)}) %collective-permute-start.9) | collective-permute-done | bytes 110624 | tf_op jit(solution)/shard_map/ppermute | solution.py:723
  92.6 0.8 assemble.1
  (30 shorter events, 3.3 us)
Async XLA Ops:
  3.8 9.8 %collective-permute-start.1 = (bf16[6,3,16,128]{3,2,1,0:T(8,128)(2,1)S(1)}, bf16[6,3,16,128]{3,2,1,0:T(8,128)(2,1)S(1)}, u32[]{:S(2)}, u32[]{:S(2)}) collective-permute-start(bf16[6,3,16,128]{3,2,1,0:T(8,128)(2,1)S(1)} %get-tuple-element.24), channel_id=1, source_target_pairs={{0,1},{1,2},{2,3},{3,0},{4,5},{5,6},{6,7},{7,4},{8,9},{9,10},{10,1... | collective-permute-start | bytes 221192 | tf_op jit(solution)/shard_map/ppermute | solution.py:723
  6.8 6.8 %collective-permute-start.2 = (bf16[6,3,16,128]{3,2,1,0:T(8,128)(2,1)S(1)}, bf16[6,3,16,128]{3,2,1,0:T(8,128)(2,1)S(1)}, u32[]{:S(2)}, u32[]{:S(2)}) collective-permute-start(bf16[6,3,16,128]{3,2,1,0:T(8,128)(2,1)S(1)} %get-tuple-element.25), channel_id=1, source_target_pairs={{0,2},{1,3},{2,0},{3,1},{4,6},{5,7},{6,4},{7,5},{8,10},{9,11},{10,... | collective-permute-start | bytes 221192 | tf_op jit(solution)/shard_map/ppermute | solution.py:723
  8.3 5.3 %collective-permute-start.3 = (bf16[6,3,16,128]{3,2,1,0:T(8,128)(2,1)S(1)}, bf16[6,3,16,128]{3,2,1,0:T(8,128)(2,1)S(1)}, u32[]{:S(2)}, u32[]{:S(2)}) collective-permute-start(bf16[6,3,16,128]{3,2,1,0:T(8,128)(2,1)S(1)} %get-tuple-element.26), channel_id=1, source_target_pairs={{0,3},{1,0},{2,1},{3,2},{4,7},{5,4},{6,5},{7,6},{8,11},{9,8},{10,9... | collective-permute-start | bytes 221192 | tf_op jit(solution)/shard_map/ppermute | solution.py:723
  9.7 9.4 %collective-permute-start.5 = (bf16[15,3,16,128]{3,2,1,0:T(8,128)(2,1)S(1)}, bf16[15,3,16,128]{3,2,1,0:T(8,128)(2,1)S(1)}, u32[]{:S(2)}, u32[]{:S(2)}) collective-permute-start(bf16[15,3,16,128]{3,2,1,0:T(8,128)(2,1)S(1)} %get-tuple-element.30), channel_id=1, source_target_pairs={{0,8},{4,12},{8,16},{12,20},{16,24},{20,28},{24,0},{28,4},{1,9},{5... | collective-permute-start | bytes 552968 | tf_op jit(solution)/shard_map/ppermute | solution.py:732
  11.3 9.2 %collective-permute-start.6 = (bf16[15,3,16,128]{3,2,1,0:T(8,128)(2,1)S(1)}, bf16[15,3,16,128]{3,2,1,0:T(8,128)(2,1)S(1)}, u32[]{:S(2)}, u32[]{:S(2)}) collective-permute-start(bf16[15,3,16,128]{3,2,1,0:T(8,128)(2,1)S(1)} %get-tuple-element.31), channel_id=1, source_target_pairs={{0,24},{4,28},{8,0},{12,4},{16,8},{20,12},{24,16},{28,20},{1,25},{... | collective-permute-start | bytes 552968 | tf_op jit(solution)/shard_map/ppermute | solution.py:732
  13.6 6.9 %collective-permute-start.4 = (bf16[5,2,3,16,128]{4,3,2,1,0:T(8,128)(2,1)S(1)}, bf16[5,2,3,16,128]{4,3,2,1,0:T(8,128)(2,1)S(1)}, u32[]{:S(2)}, u32[]{:S(2)}) collective-permute-start(bf16[5,2,3,16,128]{4,3,2,1,0:T(8,128)(2,1)S(1)} %get-tuple-element.29), channel_id=1, source_target_pairs={{4,8},{12,16},{20,24},{8,4},{16,12},{24,20},{0,0},{28,28},{5,9},{1... | collective-permute-start | bytes 368648 | tf_op jit(solution)/shard_map/ppermute | solution.py:742
  20.6 2.8 %collective-permute-start.7 = (bf16[5,8,3,16,128]{4,3,2,1,0:T(8,128)(2,1)S(1)}, bf16[5,8,3,16,128]{4,3,2,1,0:T(8,128)(2,1)S(1)}, u32[]{:S(2)}, u32[]{:S(2)}) collective-permute-start(bf16[5,8,3,16,128]{4,3,2,1,0:T(8,128)(2,1)S(1)} %with_edge.1.mine_ref), channel_id=1, source_target_pairs={{0,4},{4,0},{8,12},{12,8},{16,20},{20,16},{24,28},{28,24},{1,5},{5... | collective-permute-start | bytes 1474568 | tf_op jit(solution)/shard_map/ppermute | solution.py:718
  21.8 11.5 %collective-permute-start = (bf16[15,3,16,128]{3,2,1,0:T(8,128)(2,1)S(1)}, bf16[15,3,16,128]{3,2,1,0:T(8,128)(2,1)S(1)}, u32[]{:S(2)}, u32[]{:S(2)}) collective-permute-start(bf16[15,3,16,128]{3,2,1,0:T(8,128)(2,1)S(1)} %get-tuple-element.22), channel_id=1, source_target_pairs={{0,16},{4,20},{8,24},{12,28},{16,0},{20,4},{24,8},{28,12},{1,17},{... | collective-permute-start | bytes 552968 | tf_op jit(solution)/shard_map/ppermute | solution.py:732
  32.5 6.1 %copy-start.6 = (bf16[2,96,128]{2,1,0:T(8,128)(2,1)S(1)}, bf16[2,96,128]{2,1,0:T(8,128)(2,1)}, u32[]{:S(2)}) copy-start(bf16[2,96,128]{2,1,0:T(8,128)(2,1)} %constant.16.clone.basis_ref) | copy-start | bytes 147460
  36.3 2.4 %collective-permute-start.8 = (f32[12,128,128]{2,1,0:T(8,128)S(1)}, f32[12,128,128]{2,1,0:T(8,128)S(1)}, u32[]{:S(2)}, u32[]{:S(2)}) collective-permute-start(f32[12,128,128]{2,1,0:T(8,128)S(1)} %get-tuple-element.36), channel_id=1, source_target_pairs={{0,4},{4,0},{8,12},{12,8},{16,20},{20,16},{24,28},{28,24},{1,5},{5... | collective-permute-start | bytes 2359304 | tf_op jit(solution)/shard_map/ppermute | solution.py:718
  38.7 22.9 %copy-start = (bf16[2,512,512]{2,1,0:T(8,128)(2,1)S(1)}, bf16[2,512,512]{2,1,0:T(8,128)(2,1)}, u32[]{:S(2)}) copy-start(bf16[2,512,512]{2,1,0:T(8,128)(2,1)} %constant.19.clone.wy_ref) | copy-start | bytes 3145732
  38.7 22.9 %copy-start.1 = (bf16[2,512,384]{2,1,0:T(8,128)(2,1)S(1)}, bf16[2,512,384]{2,1,0:T(8,128)(2,1)}, u32[]{:S(2)}) copy-start(bf16[2,512,384]{2,1,0:T(8,128)(2,1)} %constant.22.clone.wyb_ref) | copy-start | bytes 2359300
  38.7 22.9 %copy-start.2 = (bf16[2,288,288]{2,1,0:T(8,128)(2,1)S(1)}, bf16[2,288,288]{2,1,0:T(8,128)(2,1)}, u32[]{:S(2)}) copy-start(bf16[2,288,288]{2,1,0:T(8,128)(2,1)} %constant.21.clone.kzb_ref) | copy-start | bytes 995332
  38.7 22.9 %copy-start.3 = (bf16[2,288,320]{2,1,0:T(8,128)(2,1)S(1)}, bf16[2,288,320]{2,1,0:T(8,128)(2,1)}, u32[]{:S(2)}) copy-start(bf16[2,288,320]{2,1,0:T(8,128)(2,1)} %constant.20.clone.kz_ref) | copy-start | bytes 1105924
  38.7 22.9 %copy-start.4 = (f32[96,128]{1,0:T(8,128)S(1)}, f32[96,128]{1,0:T(8,128)}, u32[]{:S(2)}) copy-start(f32[96,128]{1,0:T(8,128)} %constant.18.clone.muzy_ref) | copy-start | bytes 147460
  38.7 22.9 %copy-start.7 = (f32[96]{0:T(128)S(1)}, f32[96]{0:T(128)}, u32[]{:S(2)}) copy-start(f32[96]{0:T(128)} %constant.17.clone.mux_ref) | copy-start | bytes 1156
  61.6 21.9 %copy-start.5 = (bf16[2,96,128]{2,1,0:T(8,128)(2,1)S(1)}, bf16[2,96,128]{2,1,0:T(8,128)(2,1)}, u32[]{:S(2)}) copy-start(bf16[2,96,128]{2,1,0:T(8,128)(2,1)} %constant.23.clone.basis_ref) | copy-start | bytes 147460
  85.1 6.4 %collective-permute-start.9 = (f32[216,128]{1,0:T(8,128)S(1)}, f32[216,128]{1,0:T(8,128)S(1)}, u32[]{:S(2)}, u32[]{:S(2)}) collective-permute-start(f32[216,128]{1,0:T(8,128)S(1)} %get-tuple-element.38), channel_id=1, source_target_pairs={{0,1},{1,2},{2,3},{3,0},{4,5},{5,6},{6,7},{7,4},{8,9},{9,10},{10,1... | collective-permute-start | bytes 331784 | tf_op jit(solution)/shard_map/ppermute | solution.py:723
  85.3 6.9 %collective-permute-start.10 = (f32[216,128]{1,0:T(8,128)S(1)}, f32[216,128]{1,0:T(8,128)S(1)}, u32[]{:S(2)}, u32[]{:S(2)}) collective-permute-start(f32[216,128]{1,0:T(8,128)S(1)} %get-tuple-element.39), channel_id=1, source_target_pairs={{0,2},{1,3},{2,0},{3,1},{4,6},{5,7},{6,4},{7,5},{8,10},{9,11},{10,... | collective-permute-start | bytes 331784 | tf_op jit(solution)/shard_map/ppermute | solution.py:723
  86.8 5.9 %collective-permute-start.11 = (f32[216,128]{1,0:T(8,128)S(1)}, f32[216,128]{1,0:T(8,128)S(1)}, u32[]{:S(2)}, u32[]{:S(2)}) collective-permute-start(f32[216,128]{1,0:T(8,128)S(1)} %get-tuple-element.40), channel_id=1, source_target_pairs={{0,3},{1,0},{2,1},{3,2},{4,7},{5,4},{6,5},{7,6},{8,11},{9,8},{10,9... | collective-permute-start | bytes 331784 | tf_op jit(solution)/shard_map/ppermute | solution.py:723

commit v4 on v3

--- a/solution.py
+++ b/solution.py
@@ -140,6 +140,7 @@
 ROWS = GROUP * SUB
 WTILES = TILES * SUB
 HALO = STEPS - 1
+TAILS = 4
 
 
 def fits(orb, vec, norb, nv):
@@ -157,6 +158,8 @@
         and NX % (orb * vec) == 0
         and NZ % (orb * vec) == 0
         and STEPS <= GROUP
+        and NZ // orb == TAILS * TILES
+        and vec == GROUP
     )
 
 
@@ -390,15 +393,16 @@
     )(mine, other, *arrived)
 
 
-def solve_kernel(vec, first, last, *refs):
+def solve_kernel(vec, first, part, *refs):
     psi_ref, v_ref, d_ref = refs[:3]
     refs = refs[3:]
     sum_ref = None if first else refs[0]
-    outs = refs[0 if first else 1 : -5]
-    psi_s, h_s, c_s, u_a, u_b = refs[-5:]
+    out_ref, psi_s, h_s, c_s, u_a, u_b = refs[-6:]
     planes = d_ref.shape[0]
     depth = (planes - 2 * GROUP) // 2
     core = lax.axis_index("orb") % 2
+    begins = {None: 0, "own": core * depth, "other": (1 - core) * depth}[part]
+    count = 2 * depth if part is None else depth
     top = (lax.axis_index("orb") // 2) * 2 * depth - GROUP
     top_row = lax.axis_index("vec") * (ROWS - 2 * GROUP) - GROUP
     lane = lax.broadcasted_iota(jnp.int32, (SUB, LANES), 1)
@@ -415,9 +419,9 @@
     beside = jnp.where((at == to - 1) | (at == to + 1), 1.0, 0.0).astype(BF16)
 
     def begin(pair, carry):
-        rows = to_rows([psi_ref[pair, i].astype(F32) for i in range(TILES)])
+        rows = to_rows([psi_ref[begins // 2 + pair, i].astype(F32) for i in range(TILES)])
         for zz in range(2):
-            w = GROUP - HALO + 2 * pair + zz
+            w = GROUP - HALO + begins + 2 * pair + zz
             z = top + w
             there = jnp.where((z >= 0) & (z < NZ), 1.0, 0.0)
             psi = jnp.concatenate([rows[i][zz * SUB : (zz + 1) * SUB] for i in range(GROUP)], 0)
@@ -430,7 +434,7 @@
                 c_s[w, rows_k, :] = scaled * v_ref[w, rows_k, :]
         return carry
 
-    lax.fori_loop(0, psi_ref.shape[0], begin, 0, unroll=5)
+    lax.fori_loop(0, (count + 2 * HALO) // 2, begin, 0, unroll=3)
 
     def stepped(src, w, step):
         u = src[w]
@@ -456,67 +460,68 @@
     for step in range(1, STEPS - 1):
         low = GROUP - HALO + step
 
-        def middle(w, carry, src=src, dst=dst, step=step):
+        def middle(p, carry, src=src, dst=dst, step=step, low=low):
+            w = begins + low + p
             dst[w] = jnp.concatenate(stepped(src, w, step), 0)
             return carry
 
-        lax.fori_loop(low, planes - low, middle, 0, unroll=True)
+        lax.fori_loop(0, count + 2 * (HALO - step), middle, 0, unroll=True)
         src, dst = dst, (u_b if dst is u_a else u_a)
 
-    def end(p, carry, out, start, src=src):
-        w = GROUP + start + p
+    def end(p, carry, src=src):
+        w = GROUP + begins + p
         psi = psi_s[w]
         total = jnp.concatenate([psi * new for new in stepped(src, w, STEPS - 1)], 0)
         if not first:
-            total = total + sum_ref[start + p]
-        out[p] = total
+            total = total + sum_ref[begins + p]
+        out_ref[p] = total
         return carry
 
-    if last:
-        lax.fori_loop(0, depth, functools.partial(end, out=outs[1], start=(1 - core) * depth), 0, unroll=True)
-        lax.fori_loop(0, depth, functools.partial(end, out=outs[0], start=core * depth), 0, unroll=True)
-    else:
-        lax.fori_loop(0, 2 * depth, functools.partial(end, out=outs[0], start=0), 0, unroll=True)
-
-
-def solve_window(psi, v, d, total, vec, last):
+    lax.fori_loop(0, count, end, 0, unroll=True)
+
+
+def solve_window(psi, v, d, total, vec, part=None):
     planes = d.shape[0]
     depth = (planes - 2 * GROUP) // 2
-    first = total is None
-    if last:
-        outs = [jax.ShapeDtypeStruct((depth, LANES, LANES), F32)] * 2
-    else:
-        outs = [jax.ShapeDtypeStruct((2 * depth, LANES, LANES), F32)]
-    args = (psi, v, d) if first else (psi, v, d, total)
-    got = pl.pallas_call(
-        functools.partial(solve_kernel, vec, first, last),
-        out_shape=outs,
+    args = (psi, v, d) if total is None else (psi, v, d, total)
+    return pl.pallas_call(
+        functools.partial(solve_kernel, vec, total is None, part),
+        out_shape=jax.ShapeDtypeStruct((2 * depth if part is None else depth, LANES, LANES), F32),
         in_specs=[pl.BlockSpec(memory_space=pltpu.VMEM)] * len(args),
-        out_specs=[pl.BlockSpec(memory_space=pltpu.VMEM)] * len(outs),
+        out_specs=pl.BlockSpec(memory_space=pltpu.VMEM),
         scratch_shapes=[pltpu.VMEM((planes, ROWS, LANES), F32)] * 2
         + [pltpu.VMEM((planes, vec * ROWS, LANES), F32)] * 3,
         compiler_params=pltpu.CompilerParams(vmem_limit_bytes=32 << 20),
         name="solve_window",
     )(*args)
-    return got if last else got[0]
 
 
 def forward_x_kernel(ndev, basis_ref, own_ref, other_ref, out_ref):
-    depth = own_ref.shape[0]
-    parts = NX // ndev
+    depth = own_ref.shape[0] // LANES
+    inner = depth - depth // TAILS
     rows = out_ref.shape[0] // ndev
+    vecrows = LANES // SUB
     basis = (basis_ref[0], basis_ref[1])
+    lane = lax.broadcasted_iota(jnp.int32, (NX, LANES), 1)
+    pad = jnp.zeros((LANES - (SUB - 2) * vecrows, LANES), F32)
+    got = []
     for z in range(depth):
-        chi = split(own_ref[z] + other_ref[z])
-        got = dot3(basis, chi, ((1,), (1,)))
-        for part in range(parts):
-            out_ref[pl.ds(part * depth + z, ndev, rows), :] = got[part * ndev : (part + 1) * ndev]
-    for row in range(parts * depth, rows):
+        groups = [pl.ds(z * LANES + g, vecrows, SUB) for g in range(1, SUB - 1)]
+        chi = jnp.concatenate([own_ref[g, :] + other_ref[g, :] for g in groups] + [pad], 0)
+        got.append(dot3(basis, split(chi), ((1,), (1,))))
+    for z in range(inner):
+        whole, third = inner + z // TILES, z % TILES
+        tail = pltpu.roll(got[whole], LANES - LANES // TAILS * (third + 1), 1)
+        row = jnp.where(lane < LANES - LANES // TAILS, got[z], tail)
+        for part in range(NX // ndev):
+            out_ref[pl.ds(part * inner + z, ndev, rows), :] = row[part * ndev : (part + 1) * ndev]
+    for row in range(NX // ndev * inner, rows):
         out_ref[pl.ds(row, ndev, rows), :] = jnp.zeros((ndev, LANES), F32)
 
 
 def forward_x(own, other, basis, ndev):
-    rows = -(-(NX // ndev) * own.shape[0] // SUB) * SUB
+    depth = own.shape[0]
+    rows = -(-(NX // ndev) * (depth - depth // TAILS) // 8) * 8
     out = pl.pallas_call(
         functools.partial(forward_x_kernel, ndev),
         out_shape=jax.ShapeDtypeStruct((ndev * rows, LANES), F32),
@@ -524,24 +529,34 @@
         out_specs=pl.BlockSpec(memory_space=pltpu.VMEM),
         compiler_params=pltpu.CompilerParams(vmem_limit_bytes=24 << 20),
         name="forward_x",
-    )(basis, own, other)
+    )(basis, own.reshape(-1, LANES), other.reshape(-1, LANES))
     return out.reshape(ndev, rows, LANES)
 
 
-def spectral_kernel(orb, vec, mux_ref, muzy_ref, wy_ref, kz_ref, kzb_ref, wyb_ref, got_ref, out_ref):
+def spectral_kernel(orb, vec, rows, mux_ref, muzy_ref, wy_ref, kz_ref, kzb_ref, wyb_ref, got_ref, out_ref, tail_ref):
     ndev = orb * vec
     parts = NX // ndev
     me = lax.axis_index("orb") * vec + lax.axis_index("vec")
-    rows = got_ref.shape[1]
+    quarter = NZ // orb // TAILS
+    tails = tail_ref.shape[0] // orb
+    tail_ref[...] = jnp.zeros_like(tail_ref)
+    lane = lax.broadcasted_iota(jnp.int32, (parts * quarter, LANES), 1)
+    for o in range(orb):
+        for v in range(vec):
+            third = [got_ref[pl.ds((o * vec + v) * rows + p, parts * quarter, TILES), :] for p in range(TILES)]
+            tail = pltpu.roll(third[0], LANES // TAILS, 1)
+            for p in range(1, TILES):
+                tail = jnp.where(lane >= p * LANES // TAILS, pltpu.roll(third[p], (p + 1) * LANES // TAILS, 1), tail)
+            tail_ref[o * tails : o * tails + parts * quarter, v * LANES : (v + 1) * LANES] = tail
     x = jnp.concatenate(
         [
-            jnp.concatenate([got_ref[o * vec + v] for o in range(orb)], 0)
+            jnp.concatenate([got_ref[(o * vec + v) * rows : (o * vec + v + 1) * rows] for o in range(orb)], 0)
             for v in range(vec)
         ],
         1,
     )
     mm = ((1,), (0,))
-    t = dot3(split(x), (wy_ref[0], wy_ref[1]), mm)
+    t = dot3(split(jnp.concatenate([x, tail_ref[...]], 0)), (wy_ref[0], wy_ref[1]), mm)
     t = dot3((kz_ref[0], kz_ref[1]), split(t), mm)
     scale = jnp.concatenate(
         [
@@ -558,59 +573,65 @@
             entry = jnp.sum(jnp.sum(fields[k] * fields[l], axis=0, keepdims=True), axis=1, keepdims=True)
             gram = jnp.where(lane == k * vec + l, entry, gram)
     t = jnp.concatenate(fields, 1)
-    t = dot3((kzb_ref[0], kzb_ref[1]), split(t), mm)
+    t = jnp.concatenate(
+        [dot3((kzb_ref[0], kzb_ref[1]), split(t[part * NZ : (part + 1) * NZ]), mm) for part in range(parts)], 0
+    )
     t = dot3(split(t), (wyb_ref[0], wyb_ref[1]), mm)
     rows = out_ref.shape[0] // ndev
-    groups = t.shape[0] // ndev
-    for r in range(groups):
-        for yt in range(TILES):
-            out_ref[pl.ds(r * TILES + yt, ndev, rows), :] = t[
-                r * ndev : (r + 1) * ndev, yt * LANES : (yt + 1) * LANES
-            ]
-    out_ref[pl.ds(groups * TILES, ndev, rows), :] = jnp.broadcast_to(gram, (ndev, LANES))
+    zs = NZ // ndev
+    for part in range(parts):
+        for z in range(zs):
+            for yt in range(TILES):
+                out_ref[pl.ds((z * parts + part) * TILES + yt, ndev, rows), :] = t[
+                    (part * zs + z) * ndev : (part * zs + z + 1) * ndev, yt * LANES : (yt + 1) * LANES
+                ]
+    out_ref[pl.ds(zs * parts * TILES, ndev, rows), :] = jnp.broadcast_to(gram, (ndev, LANES))
 
 
 def spectral(got, orb, vec):
     ndev = orb * vec
     parts, zs = NX // ndev, NZ // ndev
     depth = NZ // orb
+    quarter = depth // TAILS
+    inner = depth - quarter
     strip = ROWS - 2 * GROUP
     rows_in = got.shape[1]
-    rows_out = -(-(parts * zs * TILES + 1) // SUB) * SUB
+    tails = -(-parts * quarter // 8) * 8
+    rows_out = -(-(parts * zs * TILES + 1) // 8) * 8
     sy, sz = np_basis(NY), np_basis(NZ)
-    wy = np.zeros((vec, vec, GROUP, SUB, vec, LANES))
+    wy = np.zeros((vec, LANES, vec, LANES))
     wyb = np.zeros((vec, LANES, TILES, vec, GROUP, SUB))
     for k in range(vec):
         for i in range(GROUP):
             for g in range(SUB):
                 for v in range(vec):
-                    row = v * strip - GROUP + GROUP * g + i
-                    if v * strip <= row < (v + 1) * strip:
-                        wy[v, k, i, g, k, :NY] = sy[row]
+                    if g < SUB - 2:
+                        wy[v, (g * vec + k) * GROUP + i, k, :NY] = sy[v * strip + GROUP * g + i]
                 for yt in range(TILES):
                     wyb[k, :NY, yt, k, i, g] = sy[yt * ROWS + GROUP * g + i]
     wy = wy.reshape(vec * LANES, vec * LANES)
     wyb = wyb.reshape(vec * LANES, TILES * LANES)
     kz = np.zeros((parts, NZ, orb, rows_in))
-    kzb = np.zeros((zs, parts, ndev, parts, NZ))
+    kzt = np.zeros((parts, NZ, orb, tails))
     for part in range(parts):
         for o in range(orb):
-            kz[part, :, o, part * depth : (part + 1) * depth] = sz[:, o * depth : (o + 1) * depth]
-        for z in range(zs):
-            kzb[z, part, :, part, :] = sz[z::zs]
-    kz = kz.reshape(parts * NZ, orb * rows_in)
-    kzb = kzb.reshape(zs * parts * ndev, parts * NZ)
+            mine = sz[:, o * depth : (o + 1) * depth]
+            kz[part, :, o, part * inner : (part + 1) * inner] = mine[:, :inner]
+            kzt[part, :, o, part * quarter : (part + 1) * quarter] = mine[:, inner:]
+    kz = np.concatenate([kz.reshape(parts * NZ, -1), kzt.reshape(parts * NZ, -1)], 1)
+    kzb = np.concatenate([sz[z::zs] for z in range(zs)])
     muzy = np.ones((NZ, LANES), np.float32)
     muzy[:, :NY] = np_eigen(NZ)[:, None] + np_eigen(NY)[None, :]
     mux = np_eigen(NX).astype(np.float32)
     out = pl.pallas_call(
-        functools.partial(spectral_kernel, orb, vec),
+        functools.partial(spectral_kernel, orb, vec, rows_in),
         out_shape=jax.ShapeDtypeStruct((ndev * rows_out, LANES), F32),
         in_specs=[pl.BlockSpec(memory_space=pltpu.SMEM)] + [pl.BlockSpec(memory_space=pltpu.VMEM)] * 6,
         out_specs=pl.BlockSpec(memory_space=pltpu.VMEM),
+        scratch_shapes=[pltpu.VMEM((orb * tails, vec * LANES), F32)],
         compiler_params=pltpu.CompilerParams(vmem_limit_bytes=32 << 20),
         name="spectral",
-    )(mux, muzy, np_split(wy), np_split(kz), np_split(kzb), np_split(wyb), got)
+    )(mux, muzy, np_split(wy), np_split(kz), np_split(kzb), np_split(wyb), got.reshape(-1, LANES))
     return out.reshape(ndev, rows_out, LANES)
 
 
@@ -743,9 +764,11 @@
     mine = with_edge(own, edge, arrived[:2])
     v, d = potential_rows(mine, swap_cores(mine, orb), vec, [])
     total = None
-    for r in [0] + order:
-        total = solve_window(psis[r], v, d, total, vec, r == order[-1])
-    return total[0], swap_cores(total[1], orb)
+    for r in [0] + order[:-1]:
+        total = solve_window(psis[r], v, d, total, vec)
+    last = psis[order[-1]]
+    other = swap_cores(solve_window(last, v, d, total, vec, "other"), orb)
+    return solve_window(last, v, d, total, vec, "own"), other
 
 
 def block_body(orbitals, energies, trial_potential, local_potential):

time: 93.7 us -> 89.8 us (0.958)
  blocking collectives: 40.6 us -> 37.8 us
  waiting for transfers between devices: 13.6 us -> 11.4 us
  Pallas kernels: 21.3 us -> 22.5 us
    all_to_all x2, blocking collectives: 40.6 us -> 37.8 us  [block_body(): got = lax.all_to_all(sent, both, 0, 0, tiled=True)]
    ppermute x2, waiting for transfers between devices: 2.27 us -> 0.44 us  [swap_cores(): return lax.ppermute(x, 'orb', [(o, o ^ 1) for o in range(orb)])]
    pallas_call x5 -> x6, Pallas kernels: 15.2 us -> 16 us  [the longest x5 12.9 us: solve_window(): pl.pallas_call(functools.partial(solve_kernel, vec, total is None, part),...]
  transfers between devices with their start and end apart: 12 -> 12, of which waited for: 7 -> 7; matrix products, arithmetic and copies ran while one was open for 0% -> 0% of each run, Pallas kernels for 10% -> 13%
where the time goes in v4:
time: 89.8 us; the launch traced here: 89.6 us
  blocking collectives  37.8 us (42%)
  Pallas kernels  22.5 us (25%)
  starting transfers between devices  16.4 us (18%)
  waiting for transfers between devices  11.4 us (13%)
  between operations  1.44 us (2%)
    all_to_all x2, blocking collectives, block_body(): got = lax.all_to_all(sent, both, 0, 0, tiled=True)  37.8 us
    pallas_call x5, Pallas kernels, solve_window(): pl.pallas_call(functools.partial(solve_kernel, vec, total is None, part),...  12.9 us
    ppermute x6, starting transfers between devices, shift(): return lax.ppermute(x, axis, [(i, (i + count) % n) for i in range(n)])  9.1 us
    ppermute x3, waiting for transfers between devices, to_chip(): return lax.ppermute(psis[r], 'orb', perm)  6.5 us
    ppermute x3, starting transfers between devices, to_chip(): return lax.ppermute(psis[r], 'orb', perm)  5.37 us
    ppermute x6, waiting for transfers between devices, shift(): return lax.ppermute(x, axis, [(i, (i + count) % n) for i in range(n)])  4.43 us
    pallas_call x1, Pallas kernels, spectral(): pl.pallas_call(functools.partial(spectral_kernel, orb, vec, rows_in), out...  3.11 us
    pallas_call x1, Pallas kernels, windows(): pl.pallas_call(functools.partial(windows_kernel, orb, vec), out_shape=out...  2.48 us
  transfers between devices with their start and end apart: 12, of which 7 were waited for; matrix products, arithmetic and copies ran while one was open for 0% of the time, Pallas kernels for 13%

profile of v4, /device:TPU:0, one launch (start us, length us, event | category | flops | bytes accessed | tf_op | source)
XLA Modules:
  0.0 89.6 jit_solution(311810913048571199)
XLA Ops:
  1.3 2.5 %windows.1 = (bf16[15,3,16,128]{3,2,1,0:T(8,128)(2,1)S(1)}, bf16[15,3,16,128]{3,2,1,0:T(8,128)(2,1)S(1)}, bf16[15,3,16,128]{3,2,1,0:T(8,128)(2,1)S(1)}, bf16[15,...) custom-call(f32[1]{0:T(128)S(6)} %copy.16.energy_ref, ...), custom_call_target="tpu_custom_call" | custom-call | tf_op jit(solution)/shard_map/windows/pallas_call | solution.py:293
  3.8 3.0 %collective-permute-start.1 = (bf16[6,3,16,128]{3,2,1,0:T(8,128)(2,1)S(1)}, bf16[6,3,16,128]{3,2,1,0:T(8,128)(2,1)S(1)}, u32[]{:S(2)}, u32[]{:S(2)}) collective-permute-start(bf16[6,3,16,128]{3,2,1,0:T(8,128)(2,1)S(1)} %get-tuple-element.22), channel_id=1, source_target_pairs={{0,1},{1,2},{2,3},{3,0},{4,5},{5,6},{6,7},{7,4},{8,9},{9,10},{10,1... | collective-permute-start | bytes 221192 | tf_op jit(solution)/shard_map/ppermute | solution.py:744
  6.8 1.5 %collective-permute-start.2 = (bf16[6,3,16,128]{3,2,1,0:T(8,128)(2,1)S(1)}, bf16[6,3,16,128]{3,2,1,0:T(8,128)(2,1)S(1)}, u32[]{:S(2)}, u32[]{:S(2)}) collective-permute-start(bf16[6,3,16,128]{3,2,1,0:T(8,128)(2,1)S(1)} %get-tuple-element.23), channel_id=1, source_target_pairs={{0,2},{1,3},{2,0},{3,1},{4,6},{5,7},{6,4},{7,5},{8,10},{9,11},{10,... | collective-permute-start | bytes 221192 | tf_op jit(solution)/shard_map/ppermute | solution.py:744
  8.3 1.4 %collective-permute-start.3 = (bf16[6,3,16,128]{3,2,1,0:T(8,128)(2,1)S(1)}, bf16[6,3,16,128]{3,2,1,0:T(8,128)(2,1)S(1)}, u32[]{:S(2)}, u32[]{:S(2)}) collective-permute-start(bf16[6,3,16,128]{3,2,1,0:T(8,128)(2,1)S(1)} %get-tuple-element.24), channel_id=1, source_target_pairs={{0,3},{1,0},{2,1},{3,2},{4,7},{5,4},{6,5},{7,6},{8,11},{9,8},{10,9... | collective-permute-start | bytes 221192 | tf_op jit(solution)/shard_map/ppermute | solution.py:744
  9.7 1.6 %collective-permute-start.5 = (bf16[15,3,16,128]{3,2,1,0:T(8,128)(2,1)S(1)}, bf16[15,3,16,128]{3,2,1,0:T(8,128)(2,1)S(1)}, u32[]{:S(2)}, u32[]{:S(2)}) collective-permute-start(bf16[15,3,16,128]{3,2,1,0:T(8,128)(2,1)S(1)} %get-tuple-element.28), channel_id=1, source_target_pairs={{0,8},{4,12},{8,16},{12,20},{16,24},{20,28},{24,0},{28,4},{1,9},{5... | collective-permute-start | bytes 552968 | tf_op jit(solution)/shard_map/ppermute | solution.py:753
  11.3 2.2 %collective-permute-start.6 = (bf16[15,3,16,128]{3,2,1,0:T(8,128)(2,1)S(1)}, bf16[15,3,16,128]{3,2,1,0:T(8,128)(2,1)S(1)}, u32[]{:S(2)}, u32[]{:S(2)}) collective-permute-start(bf16[15,3,16,128]{3,2,1,0:T(8,128)(2,1)S(1)} %get-tuple-element.29), channel_id=1, source_target_pairs={{0,24},{4,28},{8,0},{12,4},{16,8},{20,12},{24,16},{28,20},{1,25},{... | collective-permute-start | bytes 552968 | tf_op jit(solution)/shard_map/ppermute | solution.py:753
  14.3 4.8 %collective-permute-done.5.refs_0_ = bf16[15,3,16,128]{3,2,1,0:T(8,128)(2,1)S(1)} collective-permute-done((bf16[15,3,16,128]{3,2,1,0:T(8,128)(2,1)S(1)}, bf16[15,3,16,128]{3,2,1,0:T(8,128)(2,1)S(1)}, u32[]{:S(2)}, u32[]{:S(2)}) %collective-permute-start.5) | collective-permute-done | bytes 184352 | tf_op jit(solution)/shard_map/ppermute | solution.py:753
  19.1 1.4 %collective-permute-done.6.refs_1_.refs_0_ = bf16[15,3,16,128]{3,2,1,0:T(8,128)(2,1)S(1)} collective-permute-done((bf16[15,3,16,128]{3,2,1,0:T(8,128)(2,1)S(1)}, bf16[15,3,16,128]{3,2,1,0:T(8,128)(2,1)S(1)}, u32[]{:S(2)}, u32[]{:S(2)}) %collective-permute-start.6) | collective-permute-done | bytes 184352 | tf_op jit(solution)/shard_map/ppermute | solution.py:753
  20.6 1.2 %collective-permute-start.7 = (bf16[5,8,3,16,128]{4,3,2,1,0:T(8,128)(2,1)S(1)}, bf16[5,8,3,16,128]{4,3,2,1,0:T(8,128)(2,1)S(1)}, u32[]{:S(2)}, u32[]{:S(2)}) collective-permute-start(bf16[5,8,3,16,128]{4,3,2,1,0:T(8,128)(2,1)S(1)} %with_edge.1.mine_ref), channel_id=1, source_target_pairs={{0,4},{4,0},{8,12},{12,8},{16,20},{20,16},{24,28},{28,24},{1,5},{5... | collective-permute-start | bytes 1474568 | tf_op jit(solution)/shard_map/ppermute | solution.py:739
  21.8 1.6 %collective-permute-start = (bf16[15,3,16,128]{3,2,1,0:T(8,128)(2,1)S(1)}, bf16[15,3,16,128]{3,2,1,0:T(8,128)(2,1)S(1)}, u32[]{:S(2)}, u32[]{:S(2)}) collective-permute-start(bf16[15,3,16,128]{3,2,1,0:T(8,128)(2,1)S(1)} %get-tuple-element.20), channel_id=1, source_target_pairs={{0,16},{4,20},{8,24},{12,28},{16,0},{20,4},{24,8},{28,12},{1,17},{... | collective-permute-start | bytes 552968 | tf_op jit(solution)/shard_map/ppermute | solution.py:753
  23.6 3.0 %solve_window.5.refs_3_ = f32[24,128,128]{2,1,0:T(8,128)S(1)} custom-call(bf16[15,3,16,128]{3,2,1,0:T(8,128)(2,1)S(1)} %get-tuple-element.32.refs_0_, f32[32,128,128]{2,1,0:T(8,128)S(1)} %get-tuple-element.30.refs_1_, f32[32,32,128]{2,1,0:T(8,128)S(1)} %get-tuple-element.31.refs_2_), custom_call_target="tpu_custom_call" | custom-call | tf_op jit(solution)/shard_map/solve_window/pallas_call | solution.py:487
  26.7 3.1 %solve_window.6.refs_3_ = f32[24,128,128]{2,1,0:T(8,128)S(1)} custom-call(bf16[15,3,16,128]{3,2,1,0:T(8,128)(2,1)S(1)} %collective-permute-done.5.refs_0_, f32[32,128,128]{2,1,0:T(8,128)S(1)} %get-tuple-element.30.refs_1_, f32[32,32,128]{2,1,0:T(8,128)S(1)} %get-tuple-element.31.refs_2_, f32[24,128,128]{2,1,0:T(8,128)S(1)} %solve_window.5.refs_3_), custom_call_target="tpu_custom_call" | custom-call | tf_op jit(solution)/shard_map/solve_window/pallas_call | solution.py:487
  29.8 3.1 %solve_window.7.refs_3_ = f32[24,128,128]{2,1,0:T(8,128)S(1)} custom-call(bf16[15,3,16,128]{3,2,1,0:T(8,128)(2,1)S(1)} %collective-permute-done.6.refs_1_.refs_0_, f32[32,128,128]{2,1,0:T(8,128)S(1)} %get-tuple-element.30.refs_1_, f32[32,32,128]{2,1,0:T(8,128)S(1)} %get-tuple-element.31.refs_2_, f32[24,128,128]{2,1,0:T(8,128)S(1)} %solve_window.6.refs_3_), custom_call_target="tpu_custom_call" | custom-call | tf_op jit(solution)/shard_map/solve_window/pallas_call | solution.py:487
  33.2 1.8 %solve_window.9 = f32[12,128,128]{2,1,0:T(8,128)S(1)} custom-call(bf16[15,3,16,128]{3,2,1,0:T(8,128)(2,1)S(1)} %collective-permute-done.refs_0_, f32[32,128,128]{2,1,0:T(8,128)S(1)} %get-tuple-element.30.refs_1_, f32[32,32,128]{2,1,0:T(8,128)S(1)} %get-tuple-element.31.refs_2_, f32[24,128,128]{2,1,0:T(8,128)S(1)} %solve_window.7.refs_3_), custom_call_target="tpu_custom_call" | custom-call | tf_op jit(solution)/shard_map/solve_window/pallas_call | solution.py:487
  35.2 1.8 %solve_window.8 = f32[12,128,128]{2,1,0:T(8,128)S(1)} custom-call(bf16[15,3,16,128]{3,2,1,0:T(8,128)(2,1)S(1)} %collective-permute-done.refs_0_, f32[32,128,128]{2,1,0:T(8,128)S(1)} %get-tuple-element.30.refs_1_, f32[32,32,128]{2,1,0:T(8,128)S(1)} %get-tuple-element.31.refs_2_, f32[24,128,128]{2,1,0:T(8,128)S(1)} %solve_window.7.refs_3_), custom_call_target="tpu_custom_call" | custom-call | tf_op jit(solution)/shard_map/solve_window/pallas_call | solution.py:487
  37.5 1.2 %forward_x.1 = f32[1024,128]{1,0:T(8,128)S(1)} custom-call(bf16[2,96,128]{2,1,0:T(8,128)(2,1)S(1)} %copy-done.6, f32[1536,128]{1,0:T(8,128)S(1)} %bitcast.7, f32[1536,128]{1,0:T(8,128)S(1)} %bitcast.12), custom_call_target="tpu_custom_call" | custom-call | tf_op jit(solution)/shard_map/forward_x/pallas_call | solution.py:525
  38.7 19.3 %all_to_all.10 = f32[32,32,128]{2,1,0:T(8,128)S(1)} all-to-all(f32[32,32,128]{2,1,0:T(8,128)S(1)} %bitcast.11), channel_id=1, replica_groups=mesh['orb'=8,'vec'=4] {'orb','vec'}, dimensions={0} | all-to-all | bytes 1048576 | tf_op jit(solution)/shard_map/all_to_all | solution.py:783
  58.1 3.1 %spectral.1 = f32[1024,128]{1,0:T(8,128)S(1)} custom-call(f32[96]{0:T(128)S(1)} %copy-done.7, f32[96,128]{1,0:T(8,128)S(1)} %copy-done.5, bf16[2,512,512]{2,1,0:T(8,128)(2,1)S(1)} %copy-done, bf16[2,288,384]{2,1,0:T(8,128)(2,1)S(1)} %copy-done.2, bf16[2,96,96]{2,1,0:T(8,128)(2,1)S(1)} %copy-done.4, bf16[2,512,384]{2,1,0:T(8,128)(2,1)S(1)} %copy-done.1, ...), custom_call_target="tpu_custom_call" | custom-call | tf_op jit(solution)/shard_map/spectral/pallas_call | solution.py:626
  61.2 18.4 %all_to_all.11 = f32[32,32,128]{2,1,0:T(8,128)S(1)} all-to-all(f32[32,32,128]{2,1,0:T(8,128)S(1)} %bitcast.10), channel_id=1, replica_groups=mesh['orb'=8,'vec'=4] {'orb','vec'}, dimensions={0} | all-to-all | bytes 1048576 | tf_op jit(solution)/shard_map/all_to_all | solution.py:785
  79.6 1.5 %back.1 = (f32[4,4]{1,0:T(4,128)}, f32[216,128]{1,0:T(8,128)S(1)}, f32[216,128]{1,0:T(8,128)S(1)}, f32[216,128]{1,0:T(8,128)S(1)}, f32[216,128]{1,0:T(8,128)S(1)}) custom-call(bf16[2,96,128]{2,1,0:T(8,128)(2,1)S(1)} %copy-done.3, f32[1024,128]{1,0:T(8,128)S(1)} %bitcast.8), custom_call_target="tpu_custom_call" | custom-call | tf_op jit(solution)/shard_map/back/pallas_call | solution.py:704
  81.4 1.5 %collective-permute-start.10 = (f32[216,128]{1,0:T(8,128)S(1)}, f32[216,128]{1,0:T(8,128)S(1)}, u32[]{:S(2)}, u32[]{:S(2)}) collective-permute-start(f32[216,128]{1,0:T(8,128)S(1)} %get-tuple-element.35), channel_id=1, source_target_pairs={{0,2},{1,3},{2,0},{3,1},{4,6},{5,7},{6,4},{7,5},{8,10},{9,11},{10,... | collective-permute-start | bytes 331784 | tf_op jit(solution)/shard_map/ppermute | solution.py:744
  82.9 1.4 %collective-permute-start.11 = (f32[216,128]{1,0:T(8,128)S(1)}, f32[216,128]{1,0:T(8,128)S(1)}, u32[]{:S(2)}, u32[]{:S(2)}) collective-permute-start(f32[216,128]{1,0:T(8,128)S(1)} %get-tuple-element.36), channel_id=1, source_target_pairs={{0,3},{1,0},{2,1},{3,2},{4,7},{5,4},{6,5},{7,6},{8,11},{9,8},{10,9... | collective-permute-start | bytes 331784 | tf_op jit(solution)/shard_map/ppermute | solution.py:744
  84.3 3.2 %collective-permute-done.9.refs_1_ = f32[216,128]{1,0:T(8,128)S(1)} collective-permute-done((f32[216,128]{1,0:T(8,128)S(1)}, f32[216,128]{1,0:T(8,128)S(1)}, u32[]{:S(2)}, u32[]{:S(2)}) %collective-permute-start.9) | collective-permute-done | bytes 110624 | tf_op jit(solution)/shard_map/ppermute | solution.py:744
  88.8 0.8 assemble.1
  (31 shorter events, 3.4 us)
Async XLA Ops:
  3.8 9.8 %collective-permute-start.1 = (bf16[6,3,16,128]{3,2,1,0:T(8,128)(2,1)S(1)}, bf16[6,3,16,128]{3,2,1,0:T(8,128)(2,1)S(1)}, u32[]{:S(2)}, u32[]{:S(2)}) collective-permute-start(bf16[6,3,16,128]{3,2,1,0:T(8,128)(2,1)S(1)} %get-tuple-element.22), channel_id=1, source_target_pairs={{0,1},{1,2},{2,3},{3,0},{4,5},{5,6},{6,7},{7,4},{8,9},{9,10},{10,1... | collective-permute-start | bytes 221192 | tf_op jit(solution)/shard_map/ppermute | solution.py:744
  6.8 6.8 %collective-permute-start.2 = (bf16[6,3,16,128]{3,2,1,0:T(8,128)(2,1)S(1)}, bf16[6,3,16,128]{3,2,1,0:T(8,128)(2,1)S(1)}, u32[]{:S(2)}, u32[]{:S(2)}) collective-permute-start(bf16[6,3,16,128]{3,2,1,0:T(8,128)(2,1)S(1)} %get-tuple-element.23), channel_id=1, source_target_pairs={{0,2},{1,3},{2,0},{3,1},{4,6},{5,7},{6,4},{7,5},{8,10},{9,11},{10,... | collective-permute-start | bytes 221192 | tf_op jit(solution)/shard_map/ppermute | solution.py:744
  8.3 5.3 %collective-permute-start.3 = (bf16[6,3,16,128]{3,2,1,0:T(8,128)(2,1)S(1)}, bf16[6,3,16,128]{3,2,1,0:T(8,128)(2,1)S(1)}, u32[]{:S(2)}, u32[]{:S(2)}) collective-permute-start(bf16[6,3,16,128]{3,2,1,0:T(8,128)(2,1)S(1)} %get-tuple-element.24), channel_id=1, source_target_pairs={{0,3},{1,0},{2,1},{3,2},{4,7},{5,4},{6,5},{7,6},{8,11},{9,8},{10,9... | collective-permute-start | bytes 221192 | tf_op jit(solution)/shard_map/ppermute | solution.py:744
  9.7 9.4 %collective-permute-start.5 = (bf16[15,3,16,128]{3,2,1,0:T(8,128)(2,1)S(1)}, bf16[15,3,16,128]{3,2,1,0:T(8,128)(2,1)S(1)}, u32[]{:S(2)}, u32[]{:S(2)}) collective-permute-start(bf16[15,3,16,128]{3,2,1,0:T(8,128)(2,1)S(1)} %get-tuple-element.28), channel_id=1, source_target_pairs={{0,8},{4,12},{8,16},{12,20},{16,24},{20,28},{24,0},{28,4},{1,9},{5... | collective-permute-start | bytes 552968 | tf_op jit(solution)/shard_map/ppermute | solution.py:753
  11.3 9.2 %collective-permute-start.6 = (bf16[15,3,16,128]{3,2,1,0:T(8,128)(2,1)S(1)}, bf16[15,3,16,128]{3,2,1,0:T(8,128)(2,1)S(1)}, u32[]{:S(2)}, u32[]{:S(2)}) collective-permute-start(bf16[15,3,16,128]{3,2,1,0:T(8,128)(2,1)S(1)} %get-tuple-element.29), channel_id=1, source_target_pairs={{0,24},{4,28},{8,0},{12,4},{16,8},{20,12},{24,16},{28,20},{1,25},{... | collective-permute-start | bytes 552968 | tf_op jit(solution)/shard_map/ppermute | solution.py:753
  13.6 6.9 %collective-permute-start.4 = (bf16[5,2,3,16,128]{4,3,2,1,0:T(8,128)(2,1)S(1)}, bf16[5,2,3,16,128]{4,3,2,1,0:T(8,128)(2,1)S(1)}, u32[]{:S(2)}, u32[]{:S(2)}) collective-permute-start(bf16[5,2,3,16,128]{4,3,2,1,0:T(8,128)(2,1)S(1)} %get-tuple-element.27), channel_id=1, source_target_pairs={{4,8},{12,16},{20,24},{8,4},{16,12},{24,20},{0,0},{28,28},{5,9},{1... | collective-permute-start | bytes 368648 | tf_op jit(solution)/shard_map/ppermute | solution.py:763
  20.6 2.8 %collective-permute-start.7 = (bf16[5,8,3,16,128]{4,3,2,1,0:T(8,128)(2,1)S(1)}, bf16[5,8,3,16,128]{4,3,2,1,0:T(8,128)(2,1)S(1)}, u32[]{:S(2)}, u32[]{:S(2)}) collective-permute-start(bf16[5,8,3,16,128]{4,3,2,1,0:T(8,128)(2,1)S(1)} %with_edge.1.mine_ref), channel_id=1, source_target_pairs={{0,4},{4,0},{8,12},{12,8},{16,20},{20,16},{24,28},{28,24},{1,5},{5... | collective-permute-start | bytes 1474568 | tf_op jit(solution)/shard_map/ppermute | solution.py:739
  21.8 11.5 %collective-permute-start = (bf16[15,3,16,128]{3,2,1,0:T(8,128)(2,1)S(1)}, bf16[15,3,16,128]{3,2,1,0:T(8,128)(2,1)S(1)}, u32[]{:S(2)}, u32[]{:S(2)}) collective-permute-start(bf16[15,3,16,128]{3,2,1,0:T(8,128)(2,1)S(1)} %get-tuple-element.20), channel_id=1, source_target_pairs={{0,16},{4,20},{8,24},{12,28},{16,0},{20,4},{24,8},{28,12},{1,17},{... | collective-permute-start | bytes 552968 | tf_op jit(solution)/shard_map/ppermute | solution.py:753
  35.1 2.4 %copy-start.6 = (bf16[2,96,128]{2,1,0:T(8,128)(2,1)S(1)}, bf16[2,96,128]{2,1,0:T(8,128)(2,1)}, u32[]{:S(2)}) copy-start(bf16[2,96,128]{2,1,0:T(8,128)(2,1)} %constant.16.clone.basis_ref) | copy-start | bytes 147460
  35.1 2.4 %collective-permute-start.8 = (f32[12,128,128]{2,1,0:T(8,128)S(1)}, f32[12,128,128]{2,1,0:T(8,128)S(1)}, u32[]{:S(2)}, u32[]{:S(2)}) collective-permute-start(f32[12,128,128]{2,1,0:T(8,128)S(1)} %solve_window.9), channel_id=1, source_target_pairs={{0,4},{4,0},{8,12},{12,8},{16,20},{20,16},{24,28},{28,24},{1,5},{5... | collective-permute-start | bytes 2359304 | tf_op jit(solution)/shard_map/ppermute | solution.py:739
  37.4 20.6 %copy-start = (bf16[2,512,512]{2,1,0:T(8,128)(2,1)S(1)}, bf16[2,512,512]{2,1,0:T(8,128)(2,1)}, u32[]{:S(2)}) copy-start(bf16[2,512,512]{2,1,0:T(8,128)(2,1)} %constant.19.clone.wy_ref) | copy-start | bytes 3145732
  37.4 20.6 %copy-start.1 = (bf16[2,512,384]{2,1,0:T(8,128)(2,1)S(1)}, bf16[2,512,384]{2,1,0:T(8,128)(2,1)}, u32[]{:S(2)}) copy-start(bf16[2,512,384]{2,1,0:T(8,128)(2,1)} %constant.22.clone.wyb_ref) | copy-start | bytes 2359300
  37.4 20.6 %copy-start.2 = (bf16[2,288,384]{2,1,0:T(8,128)(2,1)S(1)}, bf16[2,288,384]{2,1,0:T(8,128)(2,1)}, u32[]{:S(2)}) copy-start(bf16[2,288,384]{2,1,0:T(8,128)(2,1)} %constant.20.clone.kz_ref) | copy-start | bytes 1327108
  37.4 20.6 %copy-start.4 = (bf16[2,96,96]{2,1,0:T(8,128)(2,1)S(1)}, bf16[2,96,96]{2,1,0:T(8,128)(2,1)}, u32[]{:S(2)}) copy-start(bf16[2,96,96]{2,1,0:T(8,128)(2,1)} %constant.21.clone.kzb_ref) | copy-start | bytes 110596
  37.4 20.6 %copy-start.5 = (f32[96,128]{1,0:T(8,128)S(1)}, f32[96,128]{1,0:T(8,128)}, u32[]{:S(2)}) copy-start(f32[96,128]{1,0:T(8,128)} %constant.18.clone.muzy_ref) | copy-start | bytes 147460
  37.5 20.6 %copy-start.7 = (f32[96]{0:T(128)S(1)}, f32[96]{0:T(128)}, u32[]{:S(2)}) copy-start(f32[96]{0:T(128)} %constant.17.clone.mux_ref) | copy-start | bytes 1156
  58.1 21.6 %copy-start.3 = (bf16[2,96,128]{2,1,0:T(8,128)(2,1)S(1)}, bf16[2,96,128]{2,1,0:T(8,128)(2,1)}, u32[]{:S(2)}) copy-start(bf16[2,96,128]{2,1,0:T(8,128)(2,1)} %constant.23.clone.basis_ref) | copy-start | bytes 147460
  81.2 6.4 %collective-permute-start.9 = (f32[216,128]{1,0:T(8,128)S(1)}, f32[216,128]{1,0:T(8,128)S(1)}, u32[]{:S(2)}, u32[]{:S(2)}) collective-permute-start(f32[216,128]{1,0:T(8,128)S(1)} %get-tuple-element.34), channel_id=1, source_target_pairs={{0,1},{1,2},{2,3},{3,0},{4,5},{5,6},{6,7},{7,4},{8,9},{9,10},{10,1... | collective-permute-start | bytes 331784 | tf_op jit(solution)/shard_map/ppermute | solution.py:744
  81.4 6.9 %collective-permute-start.10 = (f32[216,128]{1,0:T(8,128)S(1)}, f32[216,128]{1,0:T(8,128)S(1)}, u32[]{:S(2)}, u32[]{:S(2)}) collective-permute-start(f32[216,128]{1,0:T(8,128)S(1)} %get-tuple-element.35), channel_id=1, source_target_pairs={{0,2},{1,3},{2,0},{3,1},{4,6},{5,7},{6,4},{7,5},{8,10},{9,11},{10,... | collective-permute-start | bytes 331784 | tf_op jit(solution)/shard_map/ppermute | solution.py:744
  82.9 5.9 %collective-permute-start.11 = (f32[216,128]{1,0:T(8,128)S(1)}, f32[216,128]{1,0:T(8,128)S(1)}, u32[]{:S(2)}, u32[]{:S(2)}) collective-permute-start(f32[216,128]{1,0:T(8,128)S(1)} %get-tuple-element.36), channel_id=1, source_target_pairs={{0,3},{1,0},{2,1},{3,2},{4,7},{5,4},{6,5},{7,6},{8,11},{9,8},{10,9... | collective-permute-start | bytes 331784 | tf_op jit(solution)/shard_map/ppermute | solution.py:744

commit v5 on v4

--- a/solution.py
+++ b/solution.py
@@ -236,8 +236,8 @@
     lax.fori_loop(0, pairs, one, 0)
 
 
-def windows_kernel(orb, vec, energy_ref, psi_any, v_any, pot_any, *refs):
-    outs, (planes_ref, more_ref, psi_ref, v_ref, pot_ref, sem) = refs[:-6], refs[-6:]
+def windows_kernel(orb, vec, energy_any, psi_any, v_any, pot_any, *refs):
+    outs, (planes_ref, more_ref, psi_ref, v_ref, pot_ref, energy_ref, sem) = refs[:-7], refs[-7:]
     chips = orb // 2
     slab = NZ // chips
     depth = v_ref.shape[0]
@@ -249,10 +249,11 @@
         pltpu.make_async_copy(v_any.at[0], v_ref, sem.at[0]),
         pltpu.make_async_copy(pot_any.at[:, lanes], pot_ref, sem.at[1]),
         pltpu.make_async_copy(psi_any.at[0, :, lanes], psi_ref, sem.at[2]),
+        pltpu.make_async_copy(energy_any, energy_ref, sem.at[3]),
     ]
     for copy in copies:
         copy.start()
-    for copy in copies:
+    for copy in copies[:2]:
         copy.wait()
     for n in range(vec + 1):
         for t in range(WTILES):
@@ -266,6 +267,8 @@
     zero = jnp.zeros((HALO * WTILES, LANES), F32)
     planes_ref[: HALO * WTILES, :] = zero
     planes_ref[(NZ + HALO) * WTILES :, :] = zero
+    for copy in copies[2:]:
+        copy.wait()
     for t in range(WTILES):
         row = HALO * WTILES + (t % TILES) * SUB + t // TILES
         planes_ref[pl.ds(row, NZ, WTILES), :] = psi_ref[:, tile_lanes(strip, t, start)].astype(F32)
@@ -293,7 +296,7 @@
     got = pl.pallas_call(
         functools.partial(windows_kernel, orb, vec),
         out_shape=outs,
-        in_specs=[pl.BlockSpec(memory_space=pltpu.SMEM)] + [pl.BlockSpec(memory_space=pltpu.HBM)] * 3,
+        in_specs=[pl.BlockSpec(memory_space=pl.ANY)] + [pl.BlockSpec(memory_space=pltpu.HBM)] * 3,
         out_specs=[pl.BlockSpec(memory_space=pltpu.VMEM)] * len(outs),
         scratch_shapes=[
             pltpu.VMEM(((NZ + 2 * HALO) * WTILES, LANES), F32),
@@ -301,7 +304,8 @@
             pltpu.VMEM((NZ, WTILES * LANES), BF16),
             pltpu.VMEM((depth, NY * NX), BF16),
             pltpu.VMEM((depth, WTILES * LANES), BF16),
-            pltpu.SemaphoreType.DMA((3,)),
+            pltpu.SMEM((1,), F32),
+            pltpu.SemaphoreType.DMA((4,)),
         ],
         compiler_params=pltpu.CompilerParams(vmem_limit_bytes=24 << 20),
         name="windows",
@@ -515,13 +519,11 @@
         row = jnp.where(lane < LANES - LANES // TAILS, got[z], tail)
         for part in range(NX // ndev):
             out_ref[pl.ds(part * inner + z, ndev, rows), :] = row[part * ndev : (part + 1) * ndev]
-    for row in range(NX // ndev * inner, rows):
-        out_ref[pl.ds(row, ndev, rows), :] = jnp.zeros((ndev, LANES), F32)
 
 
 def forward_x(own, other, basis, ndev):
     depth = own.shape[0]
-    rows = -(-(NX // ndev) * (depth - depth // TAILS) // 8) * 8
+    rows = -(-(NX // ndev) * (depth - depth // TAILS) // 4) * 4
     out = pl.pallas_call(
         functools.partial(forward_x_kernel, ndev),
         out_shape=jax.ShapeDtypeStruct((ndev * rows, LANES), F32),
@@ -530,33 +532,28 @@
         compiler_params=pltpu.CompilerParams(vmem_limit_bytes=24 << 20),
         name="forward_x",
     )(basis, own.reshape(-1, LANES), other.reshape(-1, LANES))
-    return out.reshape(ndev, rows, LANES)
-
-
-def spectral_kernel(orb, vec, rows, mux_ref, muzy_ref, wy_ref, kz_ref, kzb_ref, wyb_ref, got_ref, out_ref, tail_ref):
+    return out.reshape(ndev, rows // 4, 4, LANES)
+
+
+def spectral_kernel(orb, vec, rows, mux_ref, muzy_ref, wy_ref, kz_ref, kzb_ref, wyb_ref, got_ref, out_ref):
     ndev = orb * vec
     parts = NX // ndev
     me = lax.axis_index("orb") * vec + lax.axis_index("vec")
-    quarter = NZ // orb // TAILS
-    tails = tail_ref.shape[0] // orb
-    tail_ref[...] = jnp.zeros_like(tail_ref)
-    lane = lax.broadcasted_iota(jnp.int32, (parts * quarter, LANES), 1)
-    for o in range(orb):
-        for v in range(vec):
-            third = [got_ref[pl.ds((o * vec + v) * rows + p, parts * quarter, TILES), :] for p in range(TILES)]
-            tail = pltpu.roll(third[0], LANES // TAILS, 1)
+    inner = NZ // orb - NZ // orb // TAILS
+    lane = lax.broadcasted_iota(jnp.int32, (orb, LANES), 1)
+    strips = []
+    for v in range(vec):
+        main = [got_ref[pl.ds(v * rows + r, orb, vec * rows), :] for r in range(parts * inner)]
+        tails = []
+        for r in range(0, parts * inner, TILES):
+            tail = pltpu.roll(main[r], LANES // TAILS, 1)
             for p in range(1, TILES):
-                tail = jnp.where(lane >= p * LANES // TAILS, pltpu.roll(third[p], (p + 1) * LANES // TAILS, 1), tail)
-            tail_ref[o * tails : o * tails + parts * quarter, v * LANES : (v + 1) * LANES] = tail
-    x = jnp.concatenate(
-        [
-            jnp.concatenate([got_ref[(o * vec + v) * rows : (o * vec + v + 1) * rows] for o in range(orb)], 0)
-            for v in range(vec)
-        ],
-        1,
-    )
+                third = pltpu.roll(main[r + p], (p + 1) * LANES // TAILS, 1)
+                tail = jnp.where(lane >= p * LANES // TAILS, third, tail)
+            tails.append(tail)
+        strips.append(jnp.concatenate(main + tails, 0))
     mm = ((1,), (0,))
-    t = dot3(split(jnp.concatenate([x, tail_ref[...]], 0)), (wy_ref[0], wy_ref[1]), mm)
+    t = dot3(split(jnp.concatenate(strips, 1)), (wy_ref[0], wy_ref[1]), mm)
     t = dot3((kz_ref[0], kz_ref[1]), split(t), mm)
     scale = jnp.concatenate(
         [
@@ -595,9 +592,8 @@
     quarter = depth // TAILS
     inner = depth - quarter
     strip = ROWS - 2 * GROUP
-    rows_in = got.shape[1]
-    tails = -(-parts * quarter // 8) * 8
-    rows_out = -(-(parts * zs * TILES + 1) // 8) * 8
+    rows_in = got.shape[1] * got.shape[2]
+    rows_out = -(-(parts * zs * TILES + 1) // 4) * 4
     sy, sz = np_basis(NY), np_basis(NZ)
     wy = np.zeros((vec, LANES, vec, LANES))
     wyb = np.zeros((vec, LANES, TILES, vec, GROUP, SUB))
@@ -611,13 +607,13 @@
                     wyb[k, :NY, yt, k, i, g] = sy[yt * ROWS + GROUP * g + i]
     wy = wy.reshape(vec * LANES, vec * LANES)
     wyb = wyb.reshape(vec * LANES, TILES * LANES)
-    kz = np.zeros((parts, NZ, orb, rows_in))
-    kzt = np.zeros((parts, NZ, orb, tails))
+    kz = np.zeros((parts, NZ, parts, inner, orb))
+    kzt = np.zeros((parts, NZ, parts, quarter, orb))
     for part in range(parts):
         for o in range(orb):
             mine = sz[:, o * depth : (o + 1) * depth]
-            kz[part, :, o, part * inner : (part + 1) * inner] = mine[:, :inner]
-            kzt[part, :, o, part * quarter : (part + 1) * quarter] = mine[:, inner:]
+            kz[part, :, part, :, o] = mine[:, :inner]
+            kzt[part, :, part, :, o] = mine[:, inner:]
     kz = np.concatenate([kz.reshape(parts * NZ, -1), kzt.reshape(parts * NZ, -1)], 1)
     kzb = np.concatenate([sz[z::zs] for z in range(zs)])
     muzy = np.ones((NZ, LANES), np.float32)
@@ -628,11 +624,10 @@
         out_shape=jax.ShapeDtypeStruct((ndev * rows_out, LANES), F32),
         in_specs=[pl.BlockSpec(memory_space=pltpu.SMEM)] + [pl.BlockSpec(memory_space=pltpu.VMEM)] * 6,
         out_specs=pl.BlockSpec(memory_space=pltpu.VMEM),
-        scratch_shapes=[pltpu.VMEM((orb * tails, vec * LANES), F32)],
         compiler_params=pltpu.CompilerParams(vmem_limit_bytes=32 << 20),
         name="spectral",
     )(mux, muzy, np_split(wy), np_split(kz), np_split(kzb), np_split(wyb), got.reshape(-1, LANES))
-    return out.reshape(ndev, rows_out, LANES)
+    return out.reshape(ndev, rows_out // 4, 4, LANES)
 
 
 def back_kernel(ndev, vec, basis_ref, got_ref, factor_ref, *outs):
@@ -713,12 +708,17 @@
 
 
 def assemble_kernel(vec, *refs):
-    gots, out_ref = refs[:vec], refs[vec]
-    line = lax.axis_index("vec")
+    gots, (out_any, sem) = refs[:vec], refs[vec:]
+    strip = lax.axis_index("vec")
     rows = gots[0].shape[0]
+    copies = []
     for s in range(vec):
-        start = pl.multiple_of(lax.rem(line - s + vec, vec) * rows, 8)
-        out_ref[pl.ds(start, rows), :] = gots[s][...]
+        start = pl.multiple_of(lax.rem(strip - s + vec, vec) * rows, 8)
+        copies.append(pltpu.make_async_copy(gots[s], out_any.at[pl.ds(start, rows)], sem.at[s]))
+    for copy in copies:
+        copy.start()
+    for copy in copies:
+        copy.wait()
 
 
 def assemble(gots):
@@ -728,7 +728,8 @@
         functools.partial(assemble_kernel, vec),
         out_shape=jax.ShapeDtypeStruct((rows, LANES), F32),
         in_specs=[pl.BlockSpec(memory_space=pltpu.VMEM)] * vec,
-        out_specs=pl.BlockSpec(memory_space=pltpu.VMEM),
+        out_specs=pl.BlockSpec(memory_space=pltpu.HBM),
+        scratch_shapes=[pltpu.SemaphoreType.DMA((vec,))],
         compiler_params=pltpu.CompilerParams(vmem_limit_bytes=24 << 20),
         name="assemble",
     )(*gots)

time: 89.8 us -> 86.2 us (0.960)
  blocking collectives: 37.8 us -> 35.1 us
  Pallas kernels: 22.5 us -> 21.6 us
    all_to_all x2, blocking collectives: 37.8 us -> 35.1 us  [block_body(): got = lax.all_to_all(sent, both, 0, 0, tiled=True)]
where the time goes in v5:
time: 86.2 us; the launch traced here: 86 us
  blocking collectives  35.1 us (41%)
  Pallas kernels  21.6 us (25%)
  starting transfers between devices  16.3 us (19%)
  waiting for transfers between devices  11.3 us (13%)
  between operations  1.62 us (2%)
    all_to_all x2, blocking collectives, block_body(): got = lax.all_to_all(sent, both, 0, 0, tiled=True)  35.1 us
    pallas_call x5, Pallas kernels, solve_window(): pl.pallas_call(functools.partial(solve_kernel, vec, total is None, part),...  12.9 us
    ppermute x6, starting transfers between devices, shift(): return lax.ppermute(x, axis, [(i, (i + count) % n) for i in range(n)])  8.97 us
    ppermute x3, waiting for transfers between devices, to_chip(): return lax.ppermute(psis[r], 'orb', perm)  6.51 us
    ppermute x3, starting transfers between devices, to_chip(): return lax.ppermute(psis[r], 'orb', perm)  5.37 us
    ppermute x6, waiting for transfers between devices, shift(): return lax.ppermute(x, axis, [(i, (i + count) % n) for i in range(n)])  4.45 us
    pallas_call x1, Pallas kernels, spectral(): pl.pallas_call(functools.partial(spectral_kernel, orb, vec, rows_in), out...  2.76 us
    pallas_call x1, Pallas kernels, windows(): pl.pallas_call(functools.partial(windows_kernel, orb, vec), out_shape=out...  2.27 us
  transfers between devices with their start and end apart: 12, of which 7 were waited for; matrix products, arithmetic and copies ran while one was open for 0% of the time, Pallas kernels for 13%

profile of v5, /device:TPU:0, one launch (start us, length us, event | category | flops | bytes accessed | tf_op | source)
XLA Modules:
  0.0 86.0 jit_solution(5524452564717674905)
XLA Ops:
  1.3 2.3 %windows.1 = (bf16[15,3,16,128]{3,2,1,0:T(8,128)(2,1)S(1)}, bf16[15,3,16,128]{3,2,1,0:T(8,128)(2,1)S(1)}, bf16[15,3,16,128]{3,2,1,0:T(8,128)(2,1)S(1)}, bf16[15,...) custom-call(f32[1]{0:T(128)S(6)} %copy.16.energy_any, ...), custom_call_target="tpu_custom_call" | custom-call | tf_op jit(solution)/shard_map/windows/pallas_call | solution.py:296
  3.6 3.0 %collective-permute-start.1 = (bf16[6,3,16,128]{3,2,1,0:T(8,128)(2,1)S(1)}, bf16[6,3,16,128]{3,2,1,0:T(8,128)(2,1)S(1)}, u32[]{:S(2)}, u32[]{:S(2)}) collective-permute-start(bf16[6,3,16,128]{3,2,1,0:T(8,128)(2,1)S(1)} %get-tuple-element.22), channel_id=1, source_target_pairs={{0,1},{1,2},{2,3},{3,0},{4,5},{5,6},{6,7},{7,4},{8,9},{9,10},{10,1... | collective-permute-start | bytes 221192 | tf_op jit(solution)/shard_map/ppermute | solution.py:745
  6.5 1.5 %collective-permute-start.2 = (bf16[6,3,16,128]{3,2,1,0:T(8,128)(2,1)S(1)}, bf16[6,3,16,128]{3,2,1,0:T(8,128)(2,1)S(1)}, u32[]{:S(2)}, u32[]{:S(2)}) collective-permute-start(bf16[6,3,16,128]{3,2,1,0:T(8,128)(2,1)S(1)} %get-tuple-element.23), channel_id=1, source_target_pairs={{0,2},{1,3},{2,0},{3,1},{4,6},{5,7},{6,4},{7,5},{8,10},{9,11},{10,... | collective-permute-start | bytes 221192 | tf_op jit(solution)/shard_map/ppermute | solution.py:745
  8.1 1.4 %collective-permute-start.3 = (bf16[6,3,16,128]{3,2,1,0:T(8,128)(2,1)S(1)}, bf16[6,3,16,128]{3,2,1,0:T(8,128)(2,1)S(1)}, u32[]{:S(2)}, u32[]{:S(2)}) collective-permute-start(bf16[6,3,16,128]{3,2,1,0:T(8,128)(2,1)S(1)} %get-tuple-element.24), channel_id=1, source_target_pairs={{0,3},{1,0},{2,1},{3,2},{4,7},{5,4},{6,5},{7,6},{8,11},{9,8},{10,9... | collective-permute-start | bytes 221192 | tf_op jit(solution)/shard_map/ppermute | solution.py:745
  9.5 1.6 %collective-permute-start.5 = (bf16[15,3,16,128]{3,2,1,0:T(8,128)(2,1)S(1)}, bf16[15,3,16,128]{3,2,1,0:T(8,128)(2,1)S(1)}, u32[]{:S(2)}, u32[]{:S(2)}) collective-permute-start(bf16[15,3,16,128]{3,2,1,0:T(8,128)(2,1)S(1)} %get-tuple-element.28), channel_id=1, source_target_pairs={{0,8},{4,12},{8,16},{12,20},{16,24},{20,28},{24,0},{28,4},{1,9},{5... | collective-permute-start | bytes 552968 | tf_op jit(solution)/shard_map/ppermute | solution.py:754
  11.1 2.2 %collective-permute-start.6 = (bf16[15,3,16,128]{3,2,1,0:T(8,128)(2,1)S(1)}, bf16[15,3,16,128]{3,2,1,0:T(8,128)(2,1)S(1)}, u32[]{:S(2)}, u32[]{:S(2)}) collective-permute-start(bf16[15,3,16,128]{3,2,1,0:T(8,128)(2,1)S(1)} %get-tuple-element.29), channel_id=1, source_target_pairs={{0,24},{4,28},{8,0},{12,4},{16,8},{20,12},{24,16},{28,20},{1,25},{... | collective-permute-start | bytes 552968 | tf_op jit(solution)/shard_map/ppermute | solution.py:754
  14.1 4.8 %collective-permute-done.5.refs_0_ = bf16[15,3,16,128]{3,2,1,0:T(8,128)(2,1)S(1)} collective-permute-done((bf16[15,3,16,128]{3,2,1,0:T(8,128)(2,1)S(1)}, bf16[15,3,16,128]{3,2,1,0:T(8,128)(2,1)S(1)}, u32[]{:S(2)}, u32[]{:S(2)}) %collective-permute-start.5) | collective-permute-done | bytes 184352 | tf_op jit(solution)/shard_map/ppermute | solution.py:754
  18.9 1.4 %collective-permute-done.6.refs_1_.refs_0_ = bf16[15,3,16,128]{3,2,1,0:T(8,128)(2,1)S(1)} collective-permute-done((bf16[15,3,16,128]{3,2,1,0:T(8,128)(2,1)S(1)}, bf16[15,3,16,128]{3,2,1,0:T(8,128)(2,1)S(1)}, u32[]{:S(2)}, u32[]{:S(2)}) %collective-permute-start.6) | collective-permute-done | bytes 184352 | tf_op jit(solution)/shard_map/ppermute | solution.py:754
  20.3 1.2 %collective-permute-start.7 = (bf16[5,8,3,16,128]{4,3,2,1,0:T(8,128)(2,1)S(1)}, bf16[5,8,3,16,128]{4,3,2,1,0:T(8,128)(2,1)S(1)}, u32[]{:S(2)}, u32[]{:S(2)}) collective-permute-start(bf16[5,8,3,16,128]{4,3,2,1,0:T(8,128)(2,1)S(1)} %with_edge.1.mine_ref), channel_id=1, source_target_pairs={{0,4},{4,0},{8,12},{12,8},{16,20},{20,16},{24,28},{28,24},{1,5},{5... | collective-permute-start | bytes 1474568 | tf_op jit(solution)/shard_map/ppermute | solution.py:740
  21.5 1.6 %collective-permute-start = (bf16[15,3,16,128]{3,2,1,0:T(8,128)(2,1)S(1)}, bf16[15,3,16,128]{3,2,1,0:T(8,128)(2,1)S(1)}, u32[]{:S(2)}, u32[]{:S(2)}) collective-permute-start(bf16[15,3,16,128]{3,2,1,0:T(8,128)(2,1)S(1)} %get-tuple-element.20), channel_id=1, source_target_pairs={{0,16},{4,20},{8,24},{12,28},{16,0},{20,4},{24,8},{28,12},{1,17},{... | collective-permute-start | bytes 552968 | tf_op jit(solution)/shard_map/ppermute | solution.py:754
  23.4 3.0 %solve_window.5.refs_3_ = f32[24,128,128]{2,1,0:T(8,128)S(1)} custom-call(bf16[15,3,16,128]{3,2,1,0:T(8,128)(2,1)S(1)} %get-tuple-element.32.refs_0_, f32[32,128,128]{2,1,0:T(8,128)S(1)} %get-tuple-element.30.refs_1_, f32[32,32,128]{2,1,0:T(8,128)S(1)} %get-tuple-element.31.refs_2_), custom_call_target="tpu_custom_call" | custom-call | tf_op jit(solution)/shard_map/solve_window/pallas_call | solution.py:491
  26.4 3.1 %solve_window.6.refs_3_ = f32[24,128,128]{2,1,0:T(8,128)S(1)} custom-call(bf16[15,3,16,128]{3,2,1,0:T(8,128)(2,1)S(1)} %collective-permute-done.5.refs_0_, f32[32,128,128]{2,1,0:T(8,128)S(1)} %get-tuple-element.30.refs_1_, f32[32,32,128]{2,1,0:T(8,128)S(1)} %get-tuple-element.31.refs_2_, f32[24,128,128]{2,1,0:T(8,128)S(1)} %solve_window.5.refs_3_), custom_call_target="tpu_custom_call" | custom-call | tf_op jit(solution)/shard_map/solve_window/pallas_call | solution.py:491
  29.6 3.1 %solve_window.7.refs_3_ = f32[24,128,128]{2,1,0:T(8,128)S(1)} custom-call(bf16[15,3,16,128]{3,2,1,0:T(8,128)(2,1)S(1)} %collective-permute-done.6.refs_1_.refs_0_, f32[32,128,128]{2,1,0:T(8,128)S(1)} %get-tuple-element.30.refs_1_, f32[32,32,128]{2,1,0:T(8,128)S(1)} %get-tuple-element.31.refs_2_, f32[24,128,128]{2,1,0:T(8,128)S(1)} %solve_window.6.refs_3_), custom_call_target="tpu_custom_call" | custom-call | tf_op jit(solution)/shard_map/solve_window/pallas_call | solution.py:491
  33.0 1.8 %solve_window.9 = f32[12,128,128]{2,1,0:T(8,128)S(1)} custom-call(bf16[15,3,16,128]{3,2,1,0:T(8,128)(2,1)S(1)} %collective-permute-done.refs_0_, f32[32,128,128]{2,1,0:T(8,128)S(1)} %get-tuple-element.30.refs_1_, f32[32,32,128]{2,1,0:T(8,128)S(1)} %get-tuple-element.31.refs_2_, f32[24,128,128]{2,1,0:T(8,128)S(1)} %solve_window.7.refs_3_), custom_call_target="tpu_custom_call" | custom-call | tf_op jit(solution)/shard_map/solve_window/pallas_call | solution.py:491
  35.0 1.8 %solve_window.8 = f32[12,128,128]{2,1,0:T(8,128)S(1)} custom-call(bf16[15,3,16,128]{3,2,1,0:T(8,128)(2,1)S(1)} %collective-permute-done.refs_0_, f32[32,128,128]{2,1,0:T(8,128)S(1)} %get-tuple-element.30.refs_1_, f32[32,32,128]{2,1,0:T(8,128)S(1)} %get-tuple-element.31.refs_2_, f32[24,128,128]{2,1,0:T(8,128)S(1)} %solve_window.7.refs_3_), custom_call_target="tpu_custom_call" | custom-call | tf_op jit(solution)/shard_map/solve_window/pallas_call | solution.py:491
  37.2 1.0 %forward_x.1 = f32[896,128]{1,0:T(8,128)S(1)} custom-call(bf16[2,96,128]{2,1,0:T(8,128)(2,1)S(1)} %copy-done.6, f32[1536,128]{1,0:T(8,128)S(1)} %bitcast.7, f32[1536,128]{1,0:T(8,128)S(1)} %bitcast.12), custom_call_target="tpu_custom_call" | custom-call | tf_op jit(solution)/shard_map/forward_x/pallas_call | solution.py:527
  38.2 18.1 %all_to_all.10 = f32[32,7,4,128]{3,2,1,0:T(4,128)S(1)} all-to-all(f32[32,7,4,128]{3,2,1,0:T(4,128)S(1)} %bitcast.11), channel_id=1, replica_groups=mesh['orb'=8,'vec'=4] {'orb','vec'}, dimensions={0} | all-to-all | bytes 917504 | tf_op jit(solution)/shard_map/all_to_all | solution.py:784
  56.3 2.8 %spectral.1 = f32[896,128]{1,0:T(8,128)S(1)} custom-call(f32[96]{0:T(128)S(1)} %copy-done.7, f32[96,128]{1,0:T(8,128)S(1)} %copy-done.5, bf16[2,512,512]{2,1,0:T(8,128)(2,1)S(1)} %copy-done, bf16[2,288,288]{2,1,0:T(8,128)(2,1)S(1)} %copy-done.2, bf16[2,96,96]{2,1,0:T(8,128)(2,1)S(1)} %copy-done.4, bf16[2,512,384]{2,1,0:T(8,128)(2,1)S(1)} %copy-done.1, ...), custom_call_target="tpu_custom_call" | custom-call | tf_op jit(solution)/shard_map/spectral/pallas_call | solution.py:622
  59.1 17.0 %all_to_all.11 = f32[32,7,4,128]{3,2,1,0:T(4,128)S(1)} all-to-all(f32[32,7,4,128]{3,2,1,0:T(4,128)S(1)} %bitcast.10), channel_id=1, replica_groups=mesh['orb'=8,'vec'=4] {'orb','vec'}, dimensions={0} | all-to-all | bytes 917504 | tf_op jit(solution)/shard_map/all_to_all | solution.py:786
  76.1 1.5 %back.1 = (f32[4,4]{1,0:T(4,128)}, f32[216,128]{1,0:T(8,128)S(1)}, f32[216,128]{1,0:T(8,128)S(1)}, f32[216,128]{1,0:T(8,128)S(1)}, f32[216,128]{1,0:T(8,128)S(1)}) custom-call(bf16[2,96,128]{2,1,0:T(8,128)(2,1)S(1)} %copy-done.3, f32[896,128]{1,0:T(8,128)S(1)} %bitcast.8), custom_call_target="tpu_custom_call" | custom-call | tf_op jit(solution)/shard_map/back/pallas_call | solution.py:699
  77.7 1.5 %collective-permute-start.10 = (f32[216,128]{1,0:T(8,128)S(1)}, f32[216,128]{1,0:T(8,128)S(1)}, u32[]{:S(2)}, u32[]{:S(2)}) collective-permute-start(f32[216,128]{1,0:T(8,128)S(1)} %get-tuple-element.35), channel_id=1, source_target_pairs={{0,2},{1,3},{2,0},{3,1},{4,6},{5,7},{6,4},{7,5},{8,10},{9,11},{10,... | collective-permute-start | bytes 331784 | tf_op jit(solution)/shard_map/ppermute | solution.py:745
  79.1 1.4 %collective-permute-start.11 = (f32[216,128]{1,0:T(8,128)S(1)}, f32[216,128]{1,0:T(8,128)S(1)}, u32[]{:S(2)}, u32[]{:S(2)}) collective-permute-start(f32[216,128]{1,0:T(8,128)S(1)} %get-tuple-element.36), channel_id=1, source_target_pairs={{0,3},{1,0},{2,1},{3,2},{4,7},{5,4},{6,5},{7,6},{8,11},{9,8},{10,9... | collective-permute-start | bytes 331784 | tf_op jit(solution)/shard_map/ppermute | solution.py:745
  80.6 3.4 %collective-permute-done.9.refs_1_ = f32[216,128]{1,0:T(8,128)S(1)} collective-permute-done((f32[216,128]{1,0:T(8,128)S(1)}, f32[216,128]{1,0:T(8,128)S(1)}, u32[]{:S(2)}, u32[]{:S(2)}) %collective-permute-start.9) | collective-permute-done | bytes 110624 | tf_op jit(solution)/shard_map/ppermute | solution.py:745
  85.0 0.8 assemble.1
  (31 shorter events, 3.1 us)
Async XLA Ops:
  3.6 9.8 %collective-permute-start.1 = (bf16[6,3,16,128]{3,2,1,0:T(8,128)(2,1)S(1)}, bf16[6,3,16,128]{3,2,1,0:T(8,128)(2,1)S(1)}, u32[]{:S(2)}, u32[]{:S(2)}) collective-permute-start(bf16[6,3,16,128]{3,2,1,0:T(8,128)(2,1)S(1)} %get-tuple-element.22), channel_id=1, source_target_pairs={{0,1},{1,2},{2,3},{3,0},{4,5},{5,6},{6,7},{7,4},{8,9},{9,10},{10,1... | collective-permute-start | bytes 221192 | tf_op jit(solution)/shard_map/ppermute | solution.py:745
  6.5 6.8 %collective-permute-start.2 = (bf16[6,3,16,128]{3,2,1,0:T(8,128)(2,1)S(1)}, bf16[6,3,16,128]{3,2,1,0:T(8,128)(2,1)S(1)}, u32[]{:S(2)}, u32[]{:S(2)}) collective-permute-start(bf16[6,3,16,128]{3,2,1,0:T(8,128)(2,1)S(1)} %get-tuple-element.23), channel_id=1, source_target_pairs={{0,2},{1,3},{2,0},{3,1},{4,6},{5,7},{6,4},{7,5},{8,10},{9,11},{10,... | collective-permute-start | bytes 221192 | tf_op jit(solution)/shard_map/ppermute | solution.py:745
  8.1 5.3 %collective-permute-start.3 = (bf16[6,3,16,128]{3,2,1,0:T(8,128)(2,1)S(1)}, bf16[6,3,16,128]{3,2,1,0:T(8,128)(2,1)S(1)}, u32[]{:S(2)}, u32[]{:S(2)}) collective-permute-start(bf16[6,3,16,128]{3,2,1,0:T(8,128)(2,1)S(1)} %get-tuple-element.24), channel_id=1, source_target_pairs={{0,3},{1,0},{2,1},{3,2},{4,7},{5,4},{6,5},{7,6},{8,11},{9,8},{10,9... | collective-permute-start | bytes 221192 | tf_op jit(solution)/shard_map/ppermute | solution.py:745
  9.5 9.4 %collective-permute-start.5 = (bf16[15,3,16,128]{3,2,1,0:T(8,128)(2,1)S(1)}, bf16[15,3,16,128]{3,2,1,0:T(8,128)(2,1)S(1)}, u32[]{:S(2)}, u32[]{:S(2)}) collective-permute-start(bf16[15,3,16,128]{3,2,1,0:T(8,128)(2,1)S(1)} %get-tuple-element.28), channel_id=1, source_target_pairs={{0,8},{4,12},{8,16},{12,20},{16,24},{20,28},{24,0},{28,4},{1,9},{5... | collective-permute-start | bytes 552968 | tf_op jit(solution)/shard_map/ppermute | solution.py:754
  11.1 9.2 %collective-permute-start.6 = (bf16[15,3,16,128]{3,2,1,0:T(8,128)(2,1)S(1)}, bf16[15,3,16,128]{3,2,1,0:T(8,128)(2,1)S(1)}, u32[]{:S(2)}, u32[]{:S(2)}) collective-permute-start(bf16[15,3,16,128]{3,2,1,0:T(8,128)(2,1)S(1)} %get-tuple-element.29), channel_id=1, source_target_pairs={{0,24},{4,28},{8,0},{12,4},{16,8},{20,12},{24,16},{28,20},{1,25},{... | collective-permute-start | bytes 552968 | tf_op jit(solution)/shard_map/ppermute | solution.py:754
  13.4 6.9 %collective-permute-start.4 = (bf16[5,2,3,16,128]{4,3,2,1,0:T(8,128)(2,1)S(1)}, bf16[5,2,3,16,128]{4,3,2,1,0:T(8,128)(2,1)S(1)}, u32[]{:S(2)}, u32[]{:S(2)}) collective-permute-start(bf16[5,2,3,16,128]{4,3,2,1,0:T(8,128)(2,1)S(1)} %get-tuple-element.27), channel_id=1, source_target_pairs={{4,8},{12,16},{20,24},{8,4},{16,12},{24,20},{0,0},{28,28},{5,9},{1... | collective-permute-start | bytes 368648 | tf_op jit(solution)/shard_map/ppermute | solution.py:764
  20.3 2.8 %collective-permute-start.7 = (bf16[5,8,3,16,128]{4,3,2,1,0:T(8,128)(2,1)S(1)}, bf16[5,8,3,16,128]{4,3,2,1,0:T(8,128)(2,1)S(1)}, u32[]{:S(2)}, u32[]{:S(2)}) collective-permute-start(bf16[5,8,3,16,128]{4,3,2,1,0:T(8,128)(2,1)S(1)} %with_edge.1.mine_ref), channel_id=1, source_target_pairs={{0,4},{4,0},{8,12},{12,8},{16,20},{20,16},{24,28},{28,24},{1,5},{5... | collective-permute-start | bytes 1474568 | tf_op jit(solution)/shard_map/ppermute | solution.py:740
  21.5 11.5 %collective-permute-start = (bf16[15,3,16,128]{3,2,1,0:T(8,128)(2,1)S(1)}, bf16[15,3,16,128]{3,2,1,0:T(8,128)(2,1)S(1)}, u32[]{:S(2)}, u32[]{:S(2)}) collective-permute-start(bf16[15,3,16,128]{3,2,1,0:T(8,128)(2,1)S(1)} %get-tuple-element.20), channel_id=1, source_target_pairs={{0,16},{4,20},{8,24},{12,28},{16,0},{20,4},{24,8},{28,12},{1,17},{... | collective-permute-start | bytes 552968 | tf_op jit(solution)/shard_map/ppermute | solution.py:754
  34.8 2.4 %copy-start.6 = (bf16[2,96,128]{2,1,0:T(8,128)(2,1)S(1)}, bf16[2,96,128]{2,1,0:T(8,128)(2,1)}, u32[]{:S(2)}) copy-start(bf16[2,96,128]{2,1,0:T(8,128)(2,1)} %constant.16.clone.basis_ref) | copy-start | bytes 147460
  34.8 2.4 %collective-permute-start.8 = (f32[12,128,128]{2,1,0:T(8,128)S(1)}, f32[12,128,128]{2,1,0:T(8,128)S(1)}, u32[]{:S(2)}, u32[]{:S(2)}) collective-permute-start(f32[12,128,128]{2,1,0:T(8,128)S(1)} %solve_window.9), channel_id=1, source_target_pairs={{0,4},{4,0},{8,12},{12,8},{16,20},{20,16},{24,28},{28,24},{1,5},{5... | collective-permute-start | bytes 2359304 | tf_op jit(solution)/shard_map/ppermute | solution.py:740
  36.8 19.4 %copy-start = (bf16[2,512,512]{2,1,0:T(8,128)(2,1)S(1)}, bf16[2,512,512]{2,1,0:T(8,128)(2,1)}, u32[]{:S(2)}) copy-start(bf16[2,512,512]{2,1,0:T(8,128)(2,1)} %constant.19.clone.wy_ref) | copy-start | bytes 3145732
  36.8 19.4 %copy-start.1 = (bf16[2,512,384]{2,1,0:T(8,128)(2,1)S(1)}, bf16[2,512,384]{2,1,0:T(8,128)(2,1)}, u32[]{:S(2)}) copy-start(bf16[2,512,384]{2,1,0:T(8,128)(2,1)} %constant.22.clone.wyb_ref) | copy-start | bytes 2359300
  36.8 19.4 %copy-start.2 = (bf16[2,288,288]{2,1,0:T(8,128)(2,1)S(1)}, bf16[2,288,288]{2,1,0:T(8,128)(2,1)}, u32[]{:S(2)}) copy-start(bf16[2,288,288]{2,1,0:T(8,128)(2,1)} %constant.20.clone.kz_ref) | copy-start | bytes 995332
  36.8 19.4 %copy-start.4 = (bf16[2,96,96]{2,1,0:T(8,128)(2,1)S(1)}, bf16[2,96,96]{2,1,0:T(8,128)(2,1)}, u32[]{:S(2)}) copy-start(bf16[2,96,96]{2,1,0:T(8,128)(2,1)} %constant.21.clone.kzb_ref) | copy-start | bytes 110596
  36.8 19.4 %copy-start.5 = (f32[96,128]{1,0:T(8,128)S(1)}, f32[96,128]{1,0:T(8,128)}, u32[]{:S(2)}) copy-start(f32[96,128]{1,0:T(8,128)} %constant.18.clone.muzy_ref) | copy-start | bytes 147460
  36.8 19.4 %copy-start.7 = (f32[96]{0:T(128)S(1)}, f32[96]{0:T(128)}, u32[]{:S(2)}) copy-start(f32[96]{0:T(128)} %constant.17.clone.mux_ref) | copy-start | bytes 1156
  56.3 19.8 %copy-start.3 = (bf16[2,96,128]{2,1,0:T(8,128)(2,1)S(1)}, bf16[2,96,128]{2,1,0:T(8,128)(2,1)}, u32[]{:S(2)}) copy-start(bf16[2,96,128]{2,1,0:T(8,128)(2,1)} %constant.23.clone.basis_ref) | copy-start | bytes 147460
  77.6 6.4 %collective-permute-start.9 = (f32[216,128]{1,0:T(8,128)S(1)}, f32[216,128]{1,0:T(8,128)S(1)}, u32[]{:S(2)}, u32[]{:S(2)}) collective-permute-start(f32[216,128]{1,0:T(8,128)S(1)} %get-tuple-element.34), channel_id=1, source_target_pairs={{0,1},{1,2},{2,3},{3,0},{4,5},{5,6},{6,7},{7,4},{8,9},{9,10},{10,1... | collective-permute-start | bytes 331784 | tf_op jit(solution)/shard_map/ppermute | solution.py:745
  77.7 7.0 %collective-permute-start.10 = (f32[216,128]{1,0:T(8,128)S(1)}, f32[216,128]{1,0:T(8,128)S(1)}, u32[]{:S(2)}, u32[]{:S(2)}) collective-permute-start(f32[216,128]{1,0:T(8,128)S(1)} %get-tuple-element.35), channel_id=1, source_target_pairs={{0,2},{1,3},{2,0},{3,1},{4,6},{5,7},{6,4},{7,5},{8,10},{9,11},{10,... | collective-permute-start | bytes 331784 | tf_op jit(solution)/shard_map/ppermute | solution.py:745
  79.1 5.9 %collective-permute-start.11 = (f32[216,128]{1,0:T(8,128)S(1)}, f32[216,128]{1,0:T(8,128)S(1)}, u32[]{:S(2)}, u32[]{:S(2)}) collective-permute-start(f32[216,128]{1,0:T(8,128)S(1)} %get-tuple-element.36), channel_id=1, source_target_pairs={{0,3},{1,0},{2,1},{3,2},{4,7},{5,4},{6,5},{7,6},{8,11},{9,8},{10,9... | collective-permute-start | bytes 331784 | tf_op jit(solution)/shard_map/ppermute | solution.py:745

commit v6 on v5

--- a/solution.py
+++ b/solution.py
@@ -178,6 +178,8 @@
     one = functools.partial(
         lax.dot_general, dimension_numbers=(dims, ((), ())), preferred_element_type=F32
     )
+    if dims[0] == (1,) and a[0].shape[1] == LANES:
+        return one(jnp.concatenate([a[0], a[0], a[1]], 1), jnp.concatenate([b[0], b[1], b[0]], dims[1][0]))
     return one(a[0], b[0]) + (one(a[0], b[1]) + one(a[1], b[0]))
 
 
@@ -438,7 +440,7 @@
                 c_s[w, rows_k, :] = scaled * v_ref[w, rows_k, :]
         return carry
 
-    lax.fori_loop(0, (count + 2 * HALO) // 2, begin, 0, unroll=3)
+    lax.fori_loop(0, (count + 2 * HALO) // 2, begin, 0, unroll=True)
 
     def stepped(src, w, step):
         u = src[w]

time: 86.2 us -> 85.6 us (level)
  Pallas kernels: 21.6 us -> 20.3 us
    pallas_call x5, Pallas kernels: 12.9 us -> 12 us  [solve_window(): pl.pallas_call(functools.partial(solve_kernel, vec, total is None, part),...]
where the time goes in v6:
time: 85.6 us; the launch traced here: 85.4 us
  blocking collectives  35.1 us (41%)
  Pallas kernels  20.3 us (24%)
  starting transfers between devices  16.3 us (19%)
  waiting for transfers between devices  12.1 us (14%)
  between operations  1.63 us (2%)
    all_to_all x2, blocking collectives, block_body(): got = lax.all_to_all(sent, both, 0, 0, tiled=True)  35.1 us
    pallas_call x5, Pallas kernels, solve_window(): pl.pallas_call(functools.partial(solve_kernel, vec, total is None, part),...  12 us
    ppermute x6, starting transfers between devices, shift(): return lax.ppermute(x, axis, [(i, (i + count) % n) for i in range(n)])  8.97 us
    ppermute x3, waiting for transfers between devices, to_chip(): return lax.ppermute(psis[r], 'orb', perm)  7.22 us
    ppermute x3, starting transfers between devices, to_chip(): return lax.ppermute(psis[r], 'orb', perm)  5.37 us
    ppermute x6, waiting for transfers between devices, shift(): return lax.ppermute(x, axis, [(i, (i + count) % n) for i in range(n)])  4.45 us
    pallas_call x1, Pallas kernels, spectral(): pl.pallas_call(functools.partial(spectral_kernel, orb, vec, rows_in), out...  2.75 us
    pallas_call x1, Pallas kernels, windows(): pl.pallas_call(functools.partial(windows_kernel, orb, vec), out_shape=out...  2.27 us
  transfers between devices with their start and end apart: 12, of which 7 were waited for; matrix products, arithmetic and copies ran while one was open for 0% of the time, Pallas kernels for 13%

profile of v6, /device:TPU:0, one launch (start us, length us, event | category | flops | bytes accessed | tf_op | source)
XLA Modules:
  0.0 85.4 jit_solution(11113862306785701320)
XLA Ops:
  1.3 2.3 %windows.1 = (bf16[15,3,16,128]{3,2,1,0:T(8,128)(2,1)S(1)}, bf16[15,3,16,128]{3,2,1,0:T(8,128)(2,1)S(1)}, bf16[15,3,16,128]{3,2,1,0:T(8,128)(2,1)S(1)}, bf16[15,...) custom-call(f32[1]{0:T(128)S(6)} %copy.16.energy_any, ...), custom_call_target="tpu_custom_call" | custom-call | tf_op jit(solution)/shard_map/windows/pallas_call | solution.py:298
  3.6 3.0 %collective-permute-start.1 = (bf16[6,3,16,128]{3,2,1,0:T(8,128)(2,1)S(1)}, bf16[6,3,16,128]{3,2,1,0:T(8,128)(2,1)S(1)}, u32[]{:S(2)}, u32[]{:S(2)}) collective-permute-start(bf16[6,3,16,128]{3,2,1,0:T(8,128)(2,1)S(1)} %get-tuple-element.22), channel_id=1, source_target_pairs={{0,1},{1,2},{2,3},{3,0},{4,5},{5,6},{6,7},{7,4},{8,9},{9,10},{10,1... | collective-permute-start | bytes 221192 | tf_op jit(solution)/shard_map/ppermute | solution.py:747
  6.5 1.5 %collective-permute-start.2 = (bf16[6,3,16,128]{3,2,1,0:T(8,128)(2,1)S(1)}, bf16[6,3,16,128]{3,2,1,0:T(8,128)(2,1)S(1)}, u32[]{:S(2)}, u32[]{:S(2)}) collective-permute-start(bf16[6,3,16,128]{3,2,1,0:T(8,128)(2,1)S(1)} %get-tuple-element.23), channel_id=1, source_target_pairs={{0,2},{1,3},{2,0},{3,1},{4,6},{5,7},{6,4},{7,5},{8,10},{9,11},{10,... | collective-permute-start | bytes 221192 | tf_op jit(solution)/shard_map/ppermute | solution.py:747
  8.1 1.4 %collective-permute-start.3 = (bf16[6,3,16,128]{3,2,1,0:T(8,128)(2,1)S(1)}, bf16[6,3,16,128]{3,2,1,0:T(8,128)(2,1)S(1)}, u32[]{:S(2)}, u32[]{:S(2)}) collective-permute-start(bf16[6,3,16,128]{3,2,1,0:T(8,128)(2,1)S(1)} %get-tuple-element.24), channel_id=1, source_target_pairs={{0,3},{1,0},{2,1},{3,2},{4,7},{5,4},{6,5},{7,6},{8,11},{9,8},{10,9... | collective-permute-start | bytes 221192 | tf_op jit(solution)/shard_map/ppermute | solution.py:747
  9.5 1.6 %collective-permute-start.5 = (bf16[15,3,16,128]{3,2,1,0:T(8,128)(2,1)S(1)}, bf16[15,3,16,128]{3,2,1,0:T(8,128)(2,1)S(1)}, u32[]{:S(2)}, u32[]{:S(2)}) collective-permute-start(bf16[15,3,16,128]{3,2,1,0:T(8,128)(2,1)S(1)} %get-tuple-element.28), channel_id=1, source_target_pairs={{0,8},{4,12},{8,16},{12,20},{16,24},{20,28},{24,0},{28,4},{1,9},{5... | collective-permute-start | bytes 552968 | tf_op jit(solution)/shard_map/ppermute | solution.py:756
  11.1 2.2 %collective-permute-start.6 = (bf16[15,3,16,128]{3,2,1,0:T(8,128)(2,1)S(1)}, bf16[15,3,16,128]{3,2,1,0:T(8,128)(2,1)S(1)}, u32[]{:S(2)}, u32[]{:S(2)}) collective-permute-start(bf16[15,3,16,128]{3,2,1,0:T(8,128)(2,1)S(1)} %get-tuple-element.29), channel_id=1, source_target_pairs={{0,24},{4,28},{8,0},{12,4},{16,8},{20,12},{24,16},{28,20},{1,25},{... | collective-permute-start | bytes 552968 | tf_op jit(solution)/shard_map/ppermute | solution.py:756
  14.1 4.8 %collective-permute-done.5.refs_0_ = bf16[15,3,16,128]{3,2,1,0:T(8,128)(2,1)S(1)} collective-permute-done((bf16[15,3,16,128]{3,2,1,0:T(8,128)(2,1)S(1)}, bf16[15,3,16,128]{3,2,1,0:T(8,128)(2,1)S(1)}, u32[]{:S(2)}, u32[]{:S(2)}) %collective-permute-start.5) | collective-permute-done | bytes 184352 | tf_op jit(solution)/shard_map/ppermute | solution.py:756
  18.9 1.4 %collective-permute-done.6.refs_1_.refs_0_ = bf16[15,3,16,128]{3,2,1,0:T(8,128)(2,1)S(1)} collective-permute-done((bf16[15,3,16,128]{3,2,1,0:T(8,128)(2,1)S(1)}, bf16[15,3,16,128]{3,2,1,0:T(8,128)(2,1)S(1)}, u32[]{:S(2)}, u32[]{:S(2)}) %collective-permute-start.6) | collective-permute-done | bytes 184352 | tf_op jit(solution)/shard_map/ppermute | solution.py:756
  20.3 1.2 %collective-permute-start.7 = (bf16[5,8,3,16,128]{4,3,2,1,0:T(8,128)(2,1)S(1)}, bf16[5,8,3,16,128]{4,3,2,1,0:T(8,128)(2,1)S(1)}, u32[]{:S(2)}, u32[]{:S(2)}) collective-permute-start(bf16[5,8,3,16,128]{4,3,2,1,0:T(8,128)(2,1)S(1)} %with_edge.1.mine_ref), channel_id=1, source_target_pairs={{0,4},{4,0},{8,12},{12,8},{16,20},{20,16},{24,28},{28,24},{1,5},{5... | collective-permute-start | bytes 1474568 | tf_op jit(solution)/shard_map/ppermute | solution.py:742
  21.5 1.6 %collective-permute-start = (bf16[15,3,16,128]{3,2,1,0:T(8,128)(2,1)S(1)}, bf16[15,3,16,128]{3,2,1,0:T(8,128)(2,1)S(1)}, u32[]{:S(2)}, u32[]{:S(2)}) collective-permute-start(bf16[15,3,16,128]{3,2,1,0:T(8,128)(2,1)S(1)} %get-tuple-element.20), channel_id=1, source_target_pairs={{0,16},{4,20},{8,24},{12,28},{16,0},{20,4},{24,8},{28,12},{1,17},{... | collective-permute-start | bytes 552968 | tf_op jit(solution)/shard_map/ppermute | solution.py:756
  23.4 2.8 %solve_window.5.refs_3_ = f32[24,128,128]{2,1,0:T(8,128)S(1)} custom-call(bf16[15,3,16,128]{3,2,1,0:T(8,128)(2,1)S(1)} %get-tuple-element.32.refs_0_, f32[32,128,128]{2,1,0:T(8,128)S(1)} %get-tuple-element.30.refs_1_, f32[32,32,128]{2,1,0:T(8,128)S(1)} %get-tuple-element.31.refs_2_), custom_call_target="tpu_custom_call" | custom-call | tf_op jit(solution)/shard_map/solve_window/pallas_call | solution.py:493
  26.2 2.9 %solve_window.6.refs_3_ = f32[24,128,128]{2,1,0:T(8,128)S(1)} custom-call(bf16[15,3,16,128]{3,2,1,0:T(8,128)(2,1)S(1)} %collective-permute-done.5.refs_0_, f32[32,128,128]{2,1,0:T(8,128)S(1)} %get-tuple-element.30.refs_1_, f32[32,32,128]{2,1,0:T(8,128)S(1)} %get-tuple-element.31.refs_2_, f32[24,128,128]{2,1,0:T(8,128)S(1)} %solve_window.5.refs_3_), custom_call_target="tpu_custom_call" | custom-call | tf_op jit(solution)/shard_map/solve_window/pallas_call | solution.py:493
  29.1 2.9 %solve_window.7.refs_3_ = f32[24,128,128]{2,1,0:T(8,128)S(1)} custom-call(bf16[15,3,16,128]{3,2,1,0:T(8,128)(2,1)S(1)} %collective-permute-done.6.refs_1_.refs_0_, f32[32,128,128]{2,1,0:T(8,128)S(1)} %get-tuple-element.30.refs_1_, f32[32,32,128]{2,1,0:T(8,128)S(1)} %get-tuple-element.31.refs_2_, f32[24,128,128]{2,1,0:T(8,128)S(1)} %solve_window.6.refs_3_), custom_call_target="tpu_custom_call" | custom-call | tf_op jit(solution)/shard_map/solve_window/pallas_call | solution.py:493
  32.0 1.0 %collective-permute-done.refs_0_ = bf16[15,3,16,128]{3,2,1,0:T(8,128)(2,1)S(1)} collective-permute-done((bf16[15,3,16,128]{3,2,1,0:T(8,128)(2,1)S(1)}, bf16[15,3,16,128]{3,2,1,0:T(8,128)(2,1)S(1)}, u32[]{:S(2)}, u32[]{:S(2)}) %collective-permute-start) | collective-permute-done | bytes 184352 | tf_op jit(solution)/shard_map/ppermute | solution.py:756
  33.0 1.6 %solve_window.9 = f32[12,128,128]{2,1,0:T(8,128)S(1)} custom-call(bf16[15,3,16,128]{3,2,1,0:T(8,128)(2,1)S(1)} %collective-permute-done.refs_0_, f32[32,128,128]{2,1,0:T(8,128)S(1)} %get-tuple-element.30.refs_1_, f32[32,32,128]{2,1,0:T(8,128)S(1)} %get-tuple-element.31.refs_2_, f32[24,128,128]{2,1,0:T(8,128)S(1)} %solve_window.7.refs_3_), custom_call_target="tpu_custom_call" | custom-call | tf_op jit(solution)/shard_map/solve_window/pallas_call | solution.py:493
  34.7 1.8 %solve_window.8 = f32[12,128,128]{2,1,0:T(8,128)S(1)} custom-call(bf16[15,3,16,128]{3,2,1,0:T(8,128)(2,1)S(1)} %collective-permute-done.refs_0_, f32[32,128,128]{2,1,0:T(8,128)S(1)} %get-tuple-element.30.refs_1_, f32[32,32,128]{2,1,0:T(8,128)S(1)} %get-tuple-element.31.refs_2_, f32[24,128,128]{2,1,0:T(8,128)S(1)} %solve_window.7.refs_3_), custom_call_target="tpu_custom_call" | custom-call | tf_op jit(solution)/shard_map/solve_window/pallas_call | solution.py:493
  37.6 18.1 %all_to_all.10 = f32[32,7,4,128]{3,2,1,0:T(4,128)S(1)} all-to-all(f32[32,7,4,128]{3,2,1,0:T(4,128)S(1)} %bitcast.11), channel_id=1, replica_groups=mesh['orb'=8,'vec'=4] {'orb','vec'}, dimensions={0} | all-to-all | bytes 917504 | tf_op jit(solution)/shard_map/all_to_all | solution.py:786
  55.7 2.8 %spectral.1 = f32[896,128]{1,0:T(8,128)S(1)} custom-call(f32[96]{0:T(128)S(1)} %copy-done.7, f32[96,128]{1,0:T(8,128)S(1)} %copy-done.5, bf16[2,512,512]{2,1,0:T(8,128)(2,1)S(1)} %copy-done, bf16[2,288,288]{2,1,0:T(8,128)(2,1)S(1)} %copy-done.2, bf16[2,96,96]{2,1,0:T(8,128)(2,1)S(1)} %copy-done.4, bf16[2,512,384]{2,1,0:T(8,128)(2,1)S(1)} %copy-done.1, ...), custom_call_target="tpu_custom_call" | custom-call | tf_op jit(solution)/shard_map/spectral/pallas_call | solution.py:624
  58.5 17.0 %all_to_all.11 = f32[32,7,4,128]{3,2,1,0:T(4,128)S(1)} all-to-all(f32[32,7,4,128]{3,2,1,0:T(4,128)S(1)} %bitcast.10), channel_id=1, replica_groups=mesh['orb'=8,'vec'=4] {'orb','vec'}, dimensions={0} | all-to-all | bytes 917504 | tf_op jit(solution)/shard_map/all_to_all | solution.py:788
  75.5 1.5 %back.1 = (f32[4,4]{1,0:T(4,128)}, f32[216,128]{1,0:T(8,128)S(1)}, f32[216,128]{1,0:T(8,128)S(1)}, f32[216,128]{1,0:T(8,128)S(1)}, f32[216,128]{1,0:T(8,128)S(1)}) custom-call(bf16[2,96,128]{2,1,0:T(8,128)(2,1)S(1)} %copy-done.3, f32[896,128]{1,0:T(8,128)S(1)} %bitcast.8), custom_call_target="tpu_custom_call" | custom-call | tf_op jit(solution)/shard_map/back/pallas_call | solution.py:701
  77.1 1.5 %collective-permute-start.10 = (f32[216,128]{1,0:T(8,128)S(1)}, f32[216,128]{1,0:T(8,128)S(1)}, u32[]{:S(2)}, u32[]{:S(2)}) collective-permute-start(f32[216,128]{1,0:T(8,128)S(1)} %get-tuple-element.35), channel_id=1, source_target_pairs={{0,2},{1,3},{2,0},{3,1},{4,6},{5,7},{6,4},{7,5},{8,10},{9,11},{10,... | collective-permute-start | bytes 331784 | tf_op jit(solution)/shard_map/ppermute | solution.py:747
  78.6 1.4 %collective-permute-start.11 = (f32[216,128]{1,0:T(8,128)S(1)}, f32[216,128]{1,0:T(8,128)S(1)}, u32[]{:S(2)}, u32[]{:S(2)}) collective-permute-start(f32[216,128]{1,0:T(8,128)S(1)} %get-tuple-element.36), channel_id=1, source_target_pairs={{0,3},{1,0},{2,1},{3,2},{4,7},{5,4},{6,5},{7,6},{8,11},{9,8},{10,9... | collective-permute-start | bytes 331784 | tf_op jit(solution)/shard_map/ppermute | solution.py:747
  80.1 3.4 %collective-permute-done.9.refs_1_ = f32[216,128]{1,0:T(8,128)S(1)} collective-permute-done((f32[216,128]{1,0:T(8,128)S(1)}, f32[216,128]{1,0:T(8,128)S(1)}, u32[]{:S(2)}, u32[]{:S(2)}) %collective-permute-start.9) | collective-permute-done | bytes 110624 | tf_op jit(solution)/shard_map/ppermute | solution.py:747
  84.5 0.8 assemble.1
  (31 shorter events, 3.4 us)
Async XLA Ops:
  3.6 9.8 %collective-permute-start.1 = (bf16[6,3,16,128]{3,2,1,0:T(8,128)(2,1)S(1)}, bf16[6,3,16,128]{3,2,1,0:T(8,128)(2,1)S(1)}, u32[]{:S(2)}, u32[]{:S(2)}) collective-permute-start(bf16[6,3,16,128]{3,2,1,0:T(8,128)(2,1)S(1)} %get-tuple-element.22), channel_id=1, source_target_pairs={{0,1},{1,2},{2,3},{3,0},{4,5},{5,6},{6,7},{7,4},{8,9},{9,10},{10,1... | collective-permute-start | bytes 221192 | tf_op jit(solution)/shard_map/ppermute | solution.py:747
  6.5 6.8 %collective-permute-start.2 = (bf16[6,3,16,128]{3,2,1,0:T(8,128)(2,1)S(1)}, bf16[6,3,16,128]{3,2,1,0:T(8,128)(2,1)S(1)}, u32[]{:S(2)}, u32[]{:S(2)}) collective-permute-start(bf16[6,3,16,128]{3,2,1,0:T(8,128)(2,1)S(1)} %get-tuple-element.23), channel_id=1, source_target_pairs={{0,2},{1,3},{2,0},{3,1},{4,6},{5,7},{6,4},{7,5},{8,10},{9,11},{10,... | collective-permute-start | bytes 221192 | tf_op jit(solution)/shard_map/ppermute | solution.py:747
  8.1 5.3 %collective-permute-start.3 = (bf16[6,3,16,128]{3,2,1,0:T(8,128)(2,1)S(1)}, bf16[6,3,16,128]{3,2,1,0:T(8,128)(2,1)S(1)}, u32[]{:S(2)}, u32[]{:S(2)}) collective-permute-start(bf16[6,3,16,128]{3,2,1,0:T(8,128)(2,1)S(1)} %get-tuple-element.24), channel_id=1, source_target_pairs={{0,3},{1,0},{2,1},{3,2},{4,7},{5,4},{6,5},{7,6},{8,11},{9,8},{10,9... | collective-permute-start | bytes 221192 | tf_op jit(solution)/shard_map/ppermute | solution.py:747
  9.5 9.4 %collective-permute-start.5 = (bf16[15,3,16,128]{3,2,1,0:T(8,128)(2,1)S(1)}, bf16[15,3,16,128]{3,2,1,0:T(8,128)(2,1)S(1)}, u32[]{:S(2)}, u32[]{:S(2)}) collective-permute-start(bf16[15,3,16,128]{3,2,1,0:T(8,128)(2,1)S(1)} %get-tuple-element.28), channel_id=1, source_target_pairs={{0,8},{4,12},{8,16},{12,20},{16,24},{20,28},{24,0},{28,4},{1,9},{5... | collective-permute-start | bytes 552968 | tf_op jit(solution)/shard_map/ppermute | solution.py:756
  11.1 9.2 %collective-permute-start.6 = (bf16[15,3,16,128]{3,2,1,0:T(8,128)(2,1)S(1)}, bf16[15,3,16,128]{3,2,1,0:T(8,128)(2,1)S(1)}, u32[]{:S(2)}, u32[]{:S(2)}) collective-permute-start(bf16[15,3,16,128]{3,2,1,0:T(8,128)(2,1)S(1)} %get-tuple-element.29), channel_id=1, source_target_pairs={{0,24},{4,28},{8,0},{12,4},{16,8},{20,12},{24,16},{28,20},{1,25},{... | collective-permute-start | bytes 552968 | tf_op jit(solution)/shard_map/ppermute | solution.py:756
  13.4 6.9 %collective-permute-start.4 = (bf16[5,2,3,16,128]{4,3,2,1,0:T(8,128)(2,1)S(1)}, bf16[5,2,3,16,128]{4,3,2,1,0:T(8,128)(2,1)S(1)}, u32[]{:S(2)}, u32[]{:S(2)}) collective-permute-start(bf16[5,2,3,16,128]{4,3,2,1,0:T(8,128)(2,1)S(1)} %get-tuple-element.27), channel_id=1, source_target_pairs={{4,8},{12,16},{20,24},{8,4},{16,12},{24,20},{0,0},{28,28},{5,9},{1... | collective-permute-start | bytes 368648 | tf_op jit(solution)/shard_map/ppermute | solution.py:766
  20.3 2.8 %collective-permute-start.7 = (bf16[5,8,3,16,128]{4,3,2,1,0:T(8,128)(2,1)S(1)}, bf16[5,8,3,16,128]{4,3,2,1,0:T(8,128)(2,1)S(1)}, u32[]{:S(2)}, u32[]{:S(2)}) collective-permute-start(bf16[5,8,3,16,128]{4,3,2,1,0:T(8,128)(2,1)S(1)} %with_edge.1.mine_ref), channel_id=1, source_target_pairs={{0,4},{4,0},{8,12},{12,8},{16,20},{20,16},{24,28},{28,24},{1,5},{5... | collective-permute-start | bytes 1474568 | tf_op jit(solution)/shard_map/ppermute | solution.py:742
  21.5 11.5 %collective-permute-start = (bf16[15,3,16,128]{3,2,1,0:T(8,128)(2,1)S(1)}, bf16[15,3,16,128]{3,2,1,0:T(8,128)(2,1)S(1)}, u32[]{:S(2)}, u32[]{:S(2)}) collective-permute-start(bf16[15,3,16,128]{3,2,1,0:T(8,128)(2,1)S(1)} %get-tuple-element.20), channel_id=1, source_target_pairs={{0,16},{4,20},{8,24},{12,28},{16,0},{20,4},{24,8},{28,12},{1,17},{... | collective-permute-start | bytes 552968 | tf_op jit(solution)/shard_map/ppermute | solution.py:756
  34.6 2.4 %copy-start.6 = (bf16[2,96,128]{2,1,0:T(8,128)(2,1)S(1)}, bf16[2,96,128]{2,1,0:T(8,128)(2,1)}, u32[]{:S(2)}) copy-start(bf16[2,96,128]{2,1,0:T(8,128)(2,1)} %constant.16.clone.basis_ref) | copy-start | bytes 147460
  34.7 2.4 %collective-permute-start.8 = (f32[12,128,128]{2,1,0:T(8,128)S(1)}, f32[12,128,128]{2,1,0:T(8,128)S(1)}, u32[]{:S(2)}, u32[]{:S(2)}) collective-permute-start(f32[12,128,128]{2,1,0:T(8,128)S(1)} %solve_window.9), channel_id=1, source_target_pairs={{0,4},{4,0},{8,12},{12,8},{16,20},{20,16},{24,28},{28,24},{1,5},{5... | collective-permute-start | bytes 2359304 | tf_op jit(solution)/shard_map/ppermute | solution.py:742
  36.5 19.2 %copy-start = (bf16[2,512,512]{2,1,0:T(8,128)(2,1)S(1)}, bf16[2,512,512]{2,1,0:T(8,128)(2,1)}, u32[]{:S(2)}) copy-start(bf16[2,512,512]{2,1,0:T(8,128)(2,1)} %constant.19.clone.wy_ref) | copy-start | bytes 3145732
  36.5 19.2 %copy-start.1 = (bf16[2,512,384]{2,1,0:T(8,128)(2,1)S(1)}, bf16[2,512,384]{2,1,0:T(8,128)(2,1)}, u32[]{:S(2)}) copy-start(bf16[2,512,384]{2,1,0:T(8,128)(2,1)} %constant.22.clone.wyb_ref) | copy-start | bytes 2359300
  36.6 19.1 %copy-start.2 = (bf16[2,288,288]{2,1,0:T(8,128)(2,1)S(1)}, bf16[2,288,288]{2,1,0:T(8,128)(2,1)}, u32[]{:S(2)}) copy-start(bf16[2,288,288]{2,1,0:T(8,128)(2,1)} %constant.20.clone.kz_ref) | copy-start | bytes 995332
  36.6 19.1 %copy-start.4 = (bf16[2,96,96]{2,1,0:T(8,128)(2,1)S(1)}, bf16[2,96,96]{2,1,0:T(8,128)(2,1)}, u32[]{:S(2)}) copy-start(bf16[2,96,96]{2,1,0:T(8,128)(2,1)} %constant.21.clone.kzb_ref) | copy-start | bytes 110596
  36.6 19.1 %copy-start.5 = (f32[96,128]{1,0:T(8,128)S(1)}, f32[96,128]{1,0:T(8,128)}, u32[]{:S(2)}) copy-start(f32[96,128]{1,0:T(8,128)} %constant.18.clone.muzy_ref) | copy-start | bytes 147460
  36.6 19.1 %copy-start.7 = (f32[96]{0:T(128)S(1)}, f32[96]{0:T(128)}, u32[]{:S(2)}) copy-start(f32[96]{0:T(128)} %constant.17.clone.mux_ref) | copy-start | bytes 1156
  55.7 19.8 %copy-start.3 = (bf16[2,96,128]{2,1,0:T(8,128)(2,1)S(1)}, bf16[2,96,128]{2,1,0:T(8,128)(2,1)}, u32[]{:S(2)}) copy-start(bf16[2,96,128]{2,1,0:T(8,128)(2,1)} %constant.23.clone.basis_ref) | copy-start | bytes 147460
  77.0 6.4 %collective-permute-start.9 = (f32[216,128]{1,0:T(8,128)S(1)}, f32[216,128]{1,0:T(8,128)S(1)}, u32[]{:S(2)}, u32[]{:S(2)}) collective-permute-start(f32[216,128]{1,0:T(8,128)S(1)} %get-tuple-element.34), channel_id=1, source_target_pairs={{0,1},{1,2},{2,3},{3,0},{4,5},{5,6},{6,7},{7,4},{8,9},{9,10},{10,1... | collective-permute-start | bytes 331784 | tf_op jit(solution)/shard_map/ppermute | solution.py:747
  77.1 7.0 %collective-permute-start.10 = (f32[216,128]{1,0:T(8,128)S(1)}, f32[216,128]{1,0:T(8,128)S(1)}, u32[]{:S(2)}, u32[]{:S(2)}) collective-permute-start(f32[216,128]{1,0:T(8,128)S(1)} %get-tuple-element.35), channel_id=1, source_target_pairs={{0,2},{1,3},{2,0},{3,1},{4,6},{5,7},{6,4},{7,5},{8,10},{9,11},{10,... | collective-permute-start | bytes 331784 | tf_op jit(solution)/shard_map/ppermute | solution.py:747
  78.6 5.9 %collective-permute-start.11 = (f32[216,128]{1,0:T(8,128)S(1)}, f32[216,128]{1,0:T(8,128)S(1)}, u32[]{:S(2)}, u32[]{:S(2)}) collective-permute-start(f32[216,128]{1,0:T(8,128)S(1)} %get-tuple-element.36), channel_id=1, source_target_pairs={{0,3},{1,0},{2,1},{3,2},{4,7},{5,4},{6,5},{7,6},{8,11},{9,8},{10,9... | collective-permute-start | bytes 331784 | tf_op jit(solution)/shard_map/ppermute | solution.py:747

commit v7 on v6

--- a/solution.py
+++ b/solution.py
@@ -239,7 +239,8 @@
 
 
 def windows_kernel(orb, vec, energy_any, psi_any, v_any, pot_any, *refs):
-    outs, (planes_ref, more_ref, psi_ref, v_ref, pot_ref, energy_ref, sem) = refs[:-7], refs[-7:]
+    outs, (planes_ref, more_ref, pot_rows_ref, psi_ref, v_ref, pot_ref, energy_ref, sem) = refs[:-8], refs[-8:]
+    tiles = NY * NX // LANES
     chips = orb // 2
     slab = NZ // chips
     depth = v_ref.shape[0]
@@ -255,17 +256,22 @@
     ]
     for copy in copies:
         copy.start()
+    more_ref[:SUB, :] = jnp.zeros((SUB, LANES), F32)
+    more_ref[SUB + depth * tiles :, :] = jnp.zeros((SUB, LANES), F32)
     for copy in copies[:2]:
         copy.wait()
-    for n in range(vec + 1):
-        for t in range(WTILES):
-            row = (n * depth) * WTILES + (t % TILES) * SUB + t // TILES
-            if n < vec:
-                tile = v_ref[:, tile_lanes(lax.rem(strip + n, vec), t)]
-            else:
-                tile = pot_ref[:, tile_lanes(strip, t, start)]
-            more_ref[pl.ds(row, depth, WTILES), :] = tile.astype(F32)
-        pack_planes(more_ref, n * depth, outs[chips + n], depth // 2)
+    for tile in range(tiles):
+        more_ref[pl.ds(SUB + tile, depth, tiles), :] = v_ref[:, tile * LANES : (tile + 1) * LANES].astype(F32)
+    for t in range(WTILES):
+        row = (t % TILES) * SUB + t // TILES
+        pot_rows_ref[pl.ds(row, depth, WTILES), :] = pot_ref[:, tile_lanes(strip, t, start)].astype(F32)
+    for n in range(vec):
+        first = SUB + first_tile(lax.rem(strip + n, vec))
+        for pair in range(depth // 2):
+            for i in range(TILES):
+                block = [more_ref[pl.ds(first + i + (2 * pair + zz) * tiles, SUB, TILES), :] for zz in range(2)]
+                outs[chips + n][pair, i] = jnp.concatenate(block, 0).astype(BF16)
+    pack_planes(pot_rows_ref, 0, outs[chips + vec], depth // 2)
     zero = jnp.zeros((HALO * WTILES, LANES), F32)
     planes_ref[: HALO * WTILES, :] = zero
     planes_ref[(NZ + HALO) * WTILES :, :] = zero
@@ -302,7 +308,8 @@
         out_specs=[pl.BlockSpec(memory_space=pltpu.VMEM)] * len(outs),
         scratch_shapes=[
             pltpu.VMEM(((NZ + 2 * HALO) * WTILES, LANES), F32),
-            pltpu.VMEM(((vec + 1) * depth * WTILES, LANES), F32),
+            pltpu.VMEM((depth * NY * NX // LANES + 2 * SUB, LANES), F32),
+            pltpu.VMEM((depth * WTILES, LANES), F32),
             pltpu.VMEM((NZ, WTILES * LANES), BF16),
             pltpu.VMEM((depth, NY * NX), BF16),
             pltpu.VMEM((depth, WTILES * LANES), BF16),

time: 85.6 us -> 85.4 us (level)
  no operation moved by 1% of the time
where the time goes in v7:
time: 85.4 us; the launch traced here: 85.2 us
  blocking collectives  35.1 us (41%)
  Pallas kernels  20 us (23%)
  starting transfers between devices  16.3 us (19%)
  waiting for transfers between devices  12.1 us (14%)
  between operations  1.63 us (2%)
    all_to_all x2, blocking collectives, block_body(): got = lax.all_to_all(sent, both, 0, 0, tiled=True)  35.1 us
    pallas_call x5, Pallas kernels, solve_window(): pl.pallas_call(functools.partial(solve_kernel, vec, total is None, part),...  12 us
    ppermute x6, starting transfers between devices, shift(): return lax.ppermute(x, axis, [(i, (i + count) % n) for i in range(n)])  8.97 us
    ppermute x3, waiting for transfers between devices, to_chip(): return lax.ppermute(psis[r], 'orb', perm)  7.22 us
    ppermute x3, starting transfers between devices, to_chip(): return lax.ppermute(psis[r], 'orb', perm)  5.37 us
    ppermute x6, waiting for transfers between devices, shift(): return lax.ppermute(x, axis, [(i, (i + count) % n) for i in range(n)])  4.45 us
    pallas_call x1, Pallas kernels, spectral(): pl.pallas_call(functools.partial(spectral_kernel, orb, vec, rows_in), out...  2.75 us
    pallas_call x1, Pallas kernels, windows(): pl.pallas_call(functools.partial(windows_kernel, orb, vec), out_shape=out...  2 us
  transfers between devices with their start and end apart: 12, of which 7 were waited for; matrix products, arithmetic and copies ran while one was open for 0% of the time, Pallas kernels for 13%

profile of v7, /device:TPU:0, one launch (start us, length us, event | category | flops | bytes accessed | tf_op | source)
XLA Modules:
  0.0 85.2 jit_solution(13744700908889179918)
XLA Ops:
  1.3 2.0 %windows.1 = (bf16[15,3,16,128]{3,2,1,0:T(8,128)(2,1)S(1)}, bf16[15,3,16,128]{3,2,1,0:T(8,128)(2,1)S(1)}, bf16[15,3,16,128]{3,2,1,0:T(8,128)(2,1)S(1)}, bf16[15,...) custom-call(f32[1]{0:T(128)S(6)} %copy.16.energy_any, ...), custom_call_target="tpu_custom_call" | custom-call | tf_op jit(solution)/shard_map/windows/pallas_call | solution.py:304
  3.3 3.0 %collective-permute-start.1 = (bf16[6,3,16,128]{3,2,1,0:T(8,128)(2,1)S(1)}, bf16[6,3,16,128]{3,2,1,0:T(8,128)(2,1)S(1)}, u32[]{:S(2)}, u32[]{:S(2)}) collective-permute-start(bf16[6,3,16,128]{3,2,1,0:T(8,128)(2,1)S(1)} %get-tuple-element.22), channel_id=1, source_target_pairs={{0,1},{1,2},{2,3},{3,0},{4,5},{5,6},{6,7},{7,4},{8,9},{9,10},{10,1... | collective-permute-start | bytes 221192 | tf_op jit(solution)/shard_map/ppermute | solution.py:754
  6.3 1.5 %collective-permute-start.2 = (bf16[6,3,16,128]{3,2,1,0:T(8,128)(2,1)S(1)}, bf16[6,3,16,128]{3,2,1,0:T(8,128)(2,1)S(1)}, u32[]{:S(2)}, u32[]{:S(2)}) collective-permute-start(bf16[6,3,16,128]{3,2,1,0:T(8,128)(2,1)S(1)} %get-tuple-element.23), channel_id=1, source_target_pairs={{0,2},{1,3},{2,0},{3,1},{4,6},{5,7},{6,4},{7,5},{8,10},{9,11},{10,... | collective-permute-start | bytes 221192 | tf_op jit(solution)/shard_map/ppermute | solution.py:754
  7.8 1.4 %collective-permute-start.3 = (bf16[6,3,16,128]{3,2,1,0:T(8,128)(2,1)S(1)}, bf16[6,3,16,128]{3,2,1,0:T(8,128)(2,1)S(1)}, u32[]{:S(2)}, u32[]{:S(2)}) collective-permute-start(bf16[6,3,16,128]{3,2,1,0:T(8,128)(2,1)S(1)} %get-tuple-element.24), channel_id=1, source_target_pairs={{0,3},{1,0},{2,1},{3,2},{4,7},{5,4},{6,5},{7,6},{8,11},{9,8},{10,9... | collective-permute-start | bytes 221192 | tf_op jit(solution)/shard_map/ppermute | solution.py:754
  9.2 1.6 %collective-permute-start.5 = (bf16[15,3,16,128]{3,2,1,0:T(8,128)(2,1)S(1)}, bf16[15,3,16,128]{3,2,1,0:T(8,128)(2,1)S(1)}, u32[]{:S(2)}, u32[]{:S(2)}) collective-permute-start(bf16[15,3,16,128]{3,2,1,0:T(8,128)(2,1)S(1)} %get-tuple-element.28), channel_id=1, source_target_pairs={{0,8},{4,12},{8,16},{12,20},{16,24},{20,28},{24,0},{28,4},{1,9},{5... | collective-permute-start | bytes 552968 | tf_op jit(solution)/shard_map/ppermute | solution.py:763
  10.8 2.2 %collective-permute-start.6 = (bf16[15,3,16,128]{3,2,1,0:T(8,128)(2,1)S(1)}, bf16[15,3,16,128]{3,2,1,0:T(8,128)(2,1)S(1)}, u32[]{:S(2)}, u32[]{:S(2)}) collective-permute-start(bf16[15,3,16,128]{3,2,1,0:T(8,128)(2,1)S(1)} %get-tuple-element.29), channel_id=1, source_target_pairs={{0,24},{4,28},{8,0},{12,4},{16,8},{20,12},{24,16},{28,20},{1,25},{... | collective-permute-start | bytes 552968 | tf_op jit(solution)/shard_map/ppermute | solution.py:763
  13.8 4.8 %collective-permute-done.5.refs_0_ = bf16[15,3,16,128]{3,2,1,0:T(8,128)(2,1)S(1)} collective-permute-done((bf16[15,3,16,128]{3,2,1,0:T(8,128)(2,1)S(1)}, bf16[15,3,16,128]{3,2,1,0:T(8,128)(2,1)S(1)}, u32[]{:S(2)}, u32[]{:S(2)}) %collective-permute-start.5) | collective-permute-done | bytes 184352 | tf_op jit(solution)/shard_map/ppermute | solution.py:763
  18.6 1.4 %collective-permute-done.6.refs_1_.refs_0_ = bf16[15,3,16,128]{3,2,1,0:T(8,128)(2,1)S(1)} collective-permute-done((bf16[15,3,16,128]{3,2,1,0:T(8,128)(2,1)S(1)}, bf16[15,3,16,128]{3,2,1,0:T(8,128)(2,1)S(1)}, u32[]{:S(2)}, u32[]{:S(2)}) %collective-permute-start.6) | collective-permute-done | bytes 184352 | tf_op jit(solution)/shard_map/ppermute | solution.py:763
  20.1 1.2 %collective-permute-start.7 = (bf16[5,8,3,16,128]{4,3,2,1,0:T(8,128)(2,1)S(1)}, bf16[5,8,3,16,128]{4,3,2,1,0:T(8,128)(2,1)S(1)}, u32[]{:S(2)}, u32[]{:S(2)}) collective-permute-start(bf16[5,8,3,16,128]{4,3,2,1,0:T(8,128)(2,1)S(1)} %with_edge.1.mine_ref), channel_id=1, source_target_pairs={{0,4},{4,0},{8,12},{12,8},{16,20},{20,16},{24,28},{28,24},{1,5},{5... | collective-permute-start | bytes 1474568 | tf_op jit(solution)/shard_map/ppermute | solution.py:749
  21.3 1.6 %collective-permute-start = (bf16[15,3,16,128]{3,2,1,0:T(8,128)(2,1)S(1)}, bf16[15,3,16,128]{3,2,1,0:T(8,128)(2,1)S(1)}, u32[]{:S(2)}, u32[]{:S(2)}) collective-permute-start(bf16[15,3,16,128]{3,2,1,0:T(8,128)(2,1)S(1)} %get-tuple-element.20), channel_id=1, source_target_pairs={{0,16},{4,20},{8,24},{12,28},{16,0},{20,4},{24,8},{28,12},{1,17},{... | collective-permute-start | bytes 552968 | tf_op jit(solution)/shard_map/ppermute | solution.py:763
  23.2 2.8 %solve_window.5.refs_3_ = f32[24,128,128]{2,1,0:T(8,128)S(1)} custom-call(bf16[15,3,16,128]{3,2,1,0:T(8,128)(2,1)S(1)} %get-tuple-element.32.refs_0_, f32[32,128,128]{2,1,0:T(8,128)S(1)} %get-tuple-element.30.refs_1_, f32[32,32,128]{2,1,0:T(8,128)S(1)} %get-tuple-element.31.refs_2_), custom_call_target="tpu_custom_call" | custom-call | tf_op jit(solution)/shard_map/solve_window/pallas_call | solution.py:500
  25.9 2.9 %solve_window.6.refs_3_ = f32[24,128,128]{2,1,0:T(8,128)S(1)} custom-call(bf16[15,3,16,128]{3,2,1,0:T(8,128)(2,1)S(1)} %collective-permute-done.5.refs_0_, f32[32,128,128]{2,1,0:T(8,128)S(1)} %get-tuple-element.30.refs_1_, f32[32,32,128]{2,1,0:T(8,128)S(1)} %get-tuple-element.31.refs_2_, f32[24,128,128]{2,1,0:T(8,128)S(1)} %solve_window.5.refs_3_), custom_call_target="tpu_custom_call" | custom-call | tf_op jit(solution)/shard_map/solve_window/pallas_call | solution.py:500
  28.8 2.9 %solve_window.7.refs_3_ = f32[24,128,128]{2,1,0:T(8,128)S(1)} custom-call(bf16[15,3,16,128]{3,2,1,0:T(8,128)(2,1)S(1)} %collective-permute-done.6.refs_1_.refs_0_, f32[32,128,128]{2,1,0:T(8,128)S(1)} %get-tuple-element.30.refs_1_, f32[32,32,128]{2,1,0:T(8,128)S(1)} %get-tuple-element.31.refs_2_, f32[24,128,128]{2,1,0:T(8,128)S(1)} %solve_window.6.refs_3_), custom_call_target="tpu_custom_call" | custom-call | tf_op jit(solution)/shard_map/solve_window/pallas_call | solution.py:500
  31.7 1.0 %collective-permute-done.refs_0_ = bf16[15,3,16,128]{3,2,1,0:T(8,128)(2,1)S(1)} collective-permute-done((bf16[15,3,16,128]{3,2,1,0:T(8,128)(2,1)S(1)}, bf16[15,3,16,128]{3,2,1,0:T(8,128)(2,1)S(1)}, u32[]{:S(2)}, u32[]{:S(2)}) %collective-permute-start) | collective-permute-done | bytes 184352 | tf_op jit(solution)/shard_map/ppermute | solution.py:763
  32.7 1.6 %solve_window.9 = f32[12,128,128]{2,1,0:T(8,128)S(1)} custom-call(bf16[15,3,16,128]{3,2,1,0:T(8,128)(2,1)S(1)} %collective-permute-done.refs_0_, f32[32,128,128]{2,1,0:T(8,128)S(1)} %get-tuple-element.30.refs_1_, f32[32,32,128]{2,1,0:T(8,128)S(1)} %get-tuple-element.31.refs_2_, f32[24,128,128]{2,1,0:T(8,128)S(1)} %solve_window.7.refs_3_), custom_call_target="tpu_custom_call" | custom-call | tf_op jit(solution)/shard_map/solve_window/pallas_call | solution.py:500
  34.5 1.8 %solve_window.8 = f32[12,128,128]{2,1,0:T(8,128)S(1)} custom-call(bf16[15,3,16,128]{3,2,1,0:T(8,128)(2,1)S(1)} %collective-permute-done.refs_0_, f32[32,128,128]{2,1,0:T(8,128)S(1)} %get-tuple-element.30.refs_1_, f32[32,32,128]{2,1,0:T(8,128)S(1)} %get-tuple-element.31.refs_2_, f32[24,128,128]{2,1,0:T(8,128)S(1)} %solve_window.7.refs_3_), custom_call_target="tpu_custom_call" | custom-call | tf_op jit(solution)/shard_map/solve_window/pallas_call | solution.py:500
  37.4 18.1 %all_to_all.10 = f32[32,7,4,128]{3,2,1,0:T(4,128)S(1)} all-to-all(f32[32,7,4,128]{3,2,1,0:T(4,128)S(1)} %bitcast.11), channel_id=1, replica_groups=mesh['orb'=8,'vec'=4] {'orb','vec'}, dimensions={0} | all-to-all | bytes 917504 | tf_op jit(solution)/shard_map/all_to_all | solution.py:793
  55.5 2.8 %spectral.1 = f32[896,128]{1,0:T(8,128)S(1)} custom-call(f32[96]{0:T(128)S(1)} %copy-done.7, f32[96,128]{1,0:T(8,128)S(1)} %copy-done.5, bf16[2,512,512]{2,1,0:T(8,128)(2,1)S(1)} %copy-done, bf16[2,288,288]{2,1,0:T(8,128)(2,1)S(1)} %copy-done.2, bf16[2,96,96]{2,1,0:T(8,128)(2,1)S(1)} %copy-done.4, bf16[2,512,384]{2,1,0:T(8,128)(2,1)S(1)} %copy-done.1, ...), custom_call_target="tpu_custom_call" | custom-call | tf_op jit(solution)/shard_map/spectral/pallas_call | solution.py:631
  58.2 17.0 %all_to_all.11 = f32[32,7,4,128]{3,2,1,0:T(4,128)S(1)} all-to-all(f32[32,7,4,128]{3,2,1,0:T(4,128)S(1)} %bitcast.10), channel_id=1, replica_groups=mesh['orb'=8,'vec'=4] {'orb','vec'}, dimensions={0} | all-to-all | bytes 917504 | tf_op jit(solution)/shard_map/all_to_all | solution.py:795
  75.3 1.5 %back.1 = (f32[4,4]{1,0:T(4,128)}, f32[216,128]{1,0:T(8,128)S(1)}, f32[216,128]{1,0:T(8,128)S(1)}, f32[216,128]{1,0:T(8,128)S(1)}, f32[216,128]{1,0:T(8,128)S(1)}) custom-call(bf16[2,96,128]{2,1,0:T(8,128)(2,1)S(1)} %copy-done.3, f32[896,128]{1,0:T(8,128)S(1)} %bitcast.8), custom_call_target="tpu_custom_call" | custom-call | tf_op jit(solution)/shard_map/back/pallas_call | solution.py:708
  76.8 1.5 %collective-permute-start.10 = (f32[216,128]{1,0:T(8,128)S(1)}, f32[216,128]{1,0:T(8,128)S(1)}, u32[]{:S(2)}, u32[]{:S(2)}) collective-permute-start(f32[216,128]{1,0:T(8,128)S(1)} %get-tuple-element.35), channel_id=1, source_target_pairs={{0,2},{1,3},{2,0},{3,1},{4,6},{5,7},{6,4},{7,5},{8,10},{9,11},{10,... | collective-permute-start | bytes 331784 | tf_op jit(solution)/shard_map/ppermute | solution.py:754
  78.3 1.4 %collective-permute-start.11 = (f32[216,128]{1,0:T(8,128)S(1)}, f32[216,128]{1,0:T(8,128)S(1)}, u32[]{:S(2)}, u32[]{:S(2)}) collective-permute-start(f32[216,128]{1,0:T(8,128)S(1)} %get-tuple-element.36), channel_id=1, source_target_pairs={{0,3},{1,0},{2,1},{3,2},{4,7},{5,4},{6,5},{7,6},{8,11},{9,8},{10,9... | collective-permute-start | bytes 331784 | tf_op jit(solution)/shard_map/ppermute | solution.py:754
  79.8 3.4 %collective-permute-done.9.refs_1_ = f32[216,128]{1,0:T(8,128)S(1)} collective-permute-done((f32[216,128]{1,0:T(8,128)S(1)}, f32[216,128]{1,0:T(8,128)S(1)}, u32[]{:S(2)}, u32[]{:S(2)}) %collective-permute-start.9) | collective-permute-done | bytes 110624 | tf_op jit(solution)/shard_map/ppermute | solution.py:754
  84.2 0.8 assemble.1
  (31 shorter events, 3.4 us)
Async XLA Ops:
  3.3 9.8 %collective-permute-start.1 = (bf16[6,3,16,128]{3,2,1,0:T(8,128)(2,1)S(1)}, bf16[6,3,16,128]{3,2,1,0:T(8,128)(2,1)S(1)}, u32[]{:S(2)}, u32[]{:S(2)}) collective-permute-start(bf16[6,3,16,128]{3,2,1,0:T(8,128)(2,1)S(1)} %get-tuple-element.22), channel_id=1, source_target_pairs={{0,1},{1,2},{2,3},{3,0},{4,5},{5,6},{6,7},{7,4},{8,9},{9,10},{10,1... | collective-permute-start | bytes 221192 | tf_op jit(solution)/shard_map/ppermute | solution.py:754
  6.3 6.8 %collective-permute-start.2 = (bf16[6,3,16,128]{3,2,1,0:T(8,128)(2,1)S(1)}, bf16[6,3,16,128]{3,2,1,0:T(8,128)(2,1)S(1)}, u32[]{:S(2)}, u32[]{:S(2)}) collective-permute-start(bf16[6,3,16,128]{3,2,1,0:T(8,128)(2,1)S(1)} %get-tuple-element.23), channel_id=1, source_target_pairs={{0,2},{1,3},{2,0},{3,1},{4,6},{5,7},{6,4},{7,5},{8,10},{9,11},{10,... | collective-permute-start | bytes 221192 | tf_op jit(solution)/shard_map/ppermute | solution.py:754
  7.8 5.3 %collective-permute-start.3 = (bf16[6,3,16,128]{3,2,1,0:T(8,128)(2,1)S(1)}, bf16[6,3,16,128]{3,2,1,0:T(8,128)(2,1)S(1)}, u32[]{:S(2)}, u32[]{:S(2)}) collective-permute-start(bf16[6,3,16,128]{3,2,1,0:T(8,128)(2,1)S(1)} %get-tuple-element.24), channel_id=1, source_target_pairs={{0,3},{1,0},{2,1},{3,2},{4,7},{5,4},{6,5},{7,6},{8,11},{9,8},{10,9... | collective-permute-start | bytes 221192 | tf_op jit(solution)/shard_map/ppermute | solution.py:754
  9.2 9.4 %collective-permute-start.5 = (bf16[15,3,16,128]{3,2,1,0:T(8,128)(2,1)S(1)}, bf16[15,3,16,128]{3,2,1,0:T(8,128)(2,1)S(1)}, u32[]{:S(2)}, u32[]{:S(2)}) collective-permute-start(bf16[15,3,16,128]{3,2,1,0:T(8,128)(2,1)S(1)} %get-tuple-element.28), channel_id=1, source_target_pairs={{0,8},{4,12},{8,16},{12,20},{16,24},{20,28},{24,0},{28,4},{1,9},{5... | collective-permute-start | bytes 552968 | tf_op jit(solution)/shard_map/ppermute | solution.py:763
  10.8 9.2 %collective-permute-start.6 = (bf16[15,3,16,128]{3,2,1,0:T(8,128)(2,1)S(1)}, bf16[15,3,16,128]{3,2,1,0:T(8,128)(2,1)S(1)}, u32[]{:S(2)}, u32[]{:S(2)}) collective-permute-start(bf16[15,3,16,128]{3,2,1,0:T(8,128)(2,1)S(1)} %get-tuple-element.29), channel_id=1, source_target_pairs={{0,24},{4,28},{8,0},{12,4},{16,8},{20,12},{24,16},{28,20},{1,25},{... | collective-permute-start | bytes 552968 | tf_op jit(solution)/shard_map/ppermute | solution.py:763
  13.1 6.9 %collective-permute-start.4 = (bf16[5,2,3,16,128]{4,3,2,1,0:T(8,128)(2,1)S(1)}, bf16[5,2,3,16,128]{4,3,2,1,0:T(8,128)(2,1)S(1)}, u32[]{:S(2)}, u32[]{:S(2)}) collective-permute-start(bf16[5,2,3,16,128]{4,3,2,1,0:T(8,128)(2,1)S(1)} %get-tuple-element.27), channel_id=1, source_target_pairs={{4,8},{12,16},{20,24},{8,4},{16,12},{24,20},{0,0},{28,28},{5,9},{1... | collective-permute-start | bytes 368648 | tf_op jit(solution)/shard_map/ppermute | solution.py:773
  20.1 2.8 %collective-permute-start.7 = (bf16[5,8,3,16,128]{4,3,2,1,0:T(8,128)(2,1)S(1)}, bf16[5,8,3,16,128]{4,3,2,1,0:T(8,128)(2,1)S(1)}, u32[]{:S(2)}, u32[]{:S(2)}) collective-permute-start(bf16[5,8,3,16,128]{4,3,2,1,0:T(8,128)(2,1)S(1)} %with_edge.1.mine_ref), channel_id=1, source_target_pairs={{0,4},{4,0},{8,12},{12,8},{16,20},{20,16},{24,28},{28,24},{1,5},{5... | collective-permute-start | bytes 1474568 | tf_op jit(solution)/shard_map/ppermute | solution.py:749
  21.3 11.5 %collective-permute-start = (bf16[15,3,16,128]{3,2,1,0:T(8,128)(2,1)S(1)}, bf16[15,3,16,128]{3,2,1,0:T(8,128)(2,1)S(1)}, u32[]{:S(2)}, u32[]{:S(2)}) collective-permute-start(bf16[15,3,16,128]{3,2,1,0:T(8,128)(2,1)S(1)} %get-tuple-element.20), channel_id=1, source_target_pairs={{0,16},{4,20},{8,24},{12,28},{16,0},{20,4},{24,8},{28,12},{1,17},{... | collective-permute-start | bytes 552968 | tf_op jit(solution)/shard_map/ppermute | solution.py:763
  34.4 2.4 %copy-start.6 = (bf16[2,96,128]{2,1,0:T(8,128)(2,1)S(1)}, bf16[2,96,128]{2,1,0:T(8,128)(2,1)}, u32[]{:S(2)}) copy-start(bf16[2,96,128]{2,1,0:T(8,128)(2,1)} %constant.16.clone.basis_ref) | copy-start | bytes 147460
  34.4 2.4 %collective-permute-start.8 = (f32[12,128,128]{2,1,0:T(8,128)S(1)}, f32[12,128,128]{2,1,0:T(8,128)S(1)}, u32[]{:S(2)}, u32[]{:S(2)}) collective-permute-start(f32[12,128,128]{2,1,0:T(8,128)S(1)} %solve_window.9), channel_id=1, source_target_pairs={{0,4},{4,0},{8,12},{12,8},{16,20},{20,16},{24,28},{28,24},{1,5},{5... | collective-permute-start | bytes 2359304 | tf_op jit(solution)/shard_map/ppermute | solution.py:749
  36.3 19.2 %copy-start = (bf16[2,512,512]{2,1,0:T(8,128)(2,1)S(1)}, bf16[2,512,512]{2,1,0:T(8,128)(2,1)}, u32[]{:S(2)}) copy-start(bf16[2,512,512]{2,1,0:T(8,128)(2,1)} %constant.19.clone.wy_ref) | copy-start | bytes 3145732
  36.3 19.2 %copy-start.1 = (bf16[2,512,384]{2,1,0:T(8,128)(2,1)S(1)}, bf16[2,512,384]{2,1,0:T(8,128)(2,1)}, u32[]{:S(2)}) copy-start(bf16[2,512,384]{2,1,0:T(8,128)(2,1)} %constant.22.clone.wyb_ref) | copy-start | bytes 2359300
  36.3 19.1 %copy-start.2 = (bf16[2,288,288]{2,1,0:T(8,128)(2,1)S(1)}, bf16[2,288,288]{2,1,0:T(8,128)(2,1)}, u32[]{:S(2)}) copy-start(bf16[2,288,288]{2,1,0:T(8,128)(2,1)} %constant.20.clone.kz_ref) | copy-start | bytes 995332
  36.3 19.1 %copy-start.4 = (bf16[2,96,96]{2,1,0:T(8,128)(2,1)S(1)}, bf16[2,96,96]{2,1,0:T(8,128)(2,1)}, u32[]{:S(2)}) copy-start(bf16[2,96,96]{2,1,0:T(8,128)(2,1)} %constant.21.clone.kzb_ref) | copy-start | bytes 110596
  36.3 19.1 %copy-start.5 = (f32[96,128]{1,0:T(8,128)S(1)}, f32[96,128]{1,0:T(8,128)}, u32[]{:S(2)}) copy-start(f32[96,128]{1,0:T(8,128)} %constant.18.clone.muzy_ref) | copy-start | bytes 147460
  36.3 19.1 %copy-start.7 = (f32[96]{0:T(128)S(1)}, f32[96]{0:T(128)}, u32[]{:S(2)}) copy-start(f32[96]{0:T(128)} %constant.17.clone.mux_ref) | copy-start | bytes 1156
  55.5 19.8 %copy-start.3 = (bf16[2,96,128]{2,1,0:T(8,128)(2,1)S(1)}, bf16[2,96,128]{2,1,0:T(8,128)(2,1)}, u32[]{:S(2)}) copy-start(bf16[2,96,128]{2,1,0:T(8,128)(2,1)} %constant.23.clone.basis_ref) | copy-start | bytes 147460
  76.7 6.4 %collective-permute-start.9 = (f32[216,128]{1,0:T(8,128)S(1)}, f32[216,128]{1,0:T(8,128)S(1)}, u32[]{:S(2)}, u32[]{:S(2)}) collective-permute-start(f32[216,128]{1,0:T(8,128)S(1)} %get-tuple-element.34), channel_id=1, source_target_pairs={{0,1},{1,2},{2,3},{3,0},{4,5},{5,6},{6,7},{7,4},{8,9},{9,10},{10,1... | collective-permute-start | bytes 331784 | tf_op jit(solution)/shard_map/ppermute | solution.py:754
  76.8 7.0 %collective-permute-start.10 = (f32[216,128]{1,0:T(8,128)S(1)}, f32[216,128]{1,0:T(8,128)S(1)}, u32[]{:S(2)}, u32[]{:S(2)}) collective-permute-start(f32[216,128]{1,0:T(8,128)S(1)} %get-tuple-element.35), channel_id=1, source_target_pairs={{0,2},{1,3},{2,0},{3,1},{4,6},{5,7},{6,4},{7,5},{8,10},{9,11},{10,... | collective-permute-start | bytes 331784 | tf_op jit(solution)/shard_map/ppermute | solution.py:754
  78.3 5.9 %collective-permute-start.11 = (f32[216,128]{1,0:T(8,128)S(1)}, f32[216,128]{1,0:T(8,128)S(1)}, u32[]{:S(2)}, u32[]{:S(2)}) collective-permute-start(f32[216,128]{1,0:T(8,128)S(1)} %get-tuple-element.36), channel_id=1, source_target_pairs={{0,3},{1,0},{2,1},{3,2},{4,7},{5,4},{6,5},{7,6},{8,11},{9,8},{10,9... | collective-permute-start | bytes 331784 | tf_op jit(solution)/shard_map/ppermute | solution.py:754

commit v8 on v7

--- a/solution.py
+++ b/solution.py
@@ -684,15 +684,15 @@
             line.append(value)
         coefficients.append(line)
     for z in range(zs):
+        columns = [
+            jnp.concatenate(
+                [got_ref[pl.ds((z * parts + part) * TILES + yt, ndev, rows), :] for part in range(parts)], 0
+            )
+            for yt in range(TILES)
+        ]
+        fields = dot3(split(jnp.concatenate(columns, 1)), basis, ((0,), (0,)))
         for yt in range(TILES):
-            x = jnp.concatenate(
-                [
-                    got_ref[pl.ds((z * parts + part) * TILES + yt, ndev, rows), :]
-                    for part in range(parts)
-                ],
-                0,
-            )
-            y = dot3(split(x), basis, ((0,), (0,)))
+            y = fields[yt * LANES : (yt + 1) * LANES]
             for s in range(vec):
                 mixed = coefficients[s][0] * y[:ROWS]
                 for k in range(1, vec):

time: 85.4 us -> 85.4 us (level)
  no operation moved by 1% of the time
where the time goes in v8:
time: 85.4 us; the launch traced here: 85.2 us
  blocking collectives  35.1 us (41%)
  Pallas kernels  20 us (23%)
  starting transfers between devices  16.3 us (19%)
  waiting for transfers between devices  12.1 us (14%)
  between operations  1.63 us (2%)
    all_to_all x2, blocking collectives, block_body(): got = lax.all_to_all(sent, both, 0, 0, tiled=True)  35.1 us
    pallas_call x5, Pallas kernels, solve_window(): pl.pallas_call(functools.partial(solve_kernel, vec, total is None, part),...  12 us
    ppermute x6, starting transfers between devices, shift(): return lax.ppermute(x, axis, [(i, (i + count) % n) for i in range(n)])  8.98 us
    ppermute x3, waiting for transfers between devices, to_chip(): return lax.ppermute(psis[r], 'orb', perm)  7.22 us
    ppermute x3, starting transfers between devices, to_chip(): return lax.ppermute(psis[r], 'orb', perm)  5.37 us
    ppermute x6, waiting for transfers between devices, shift(): return lax.ppermute(x, axis, [(i, (i + count) % n) for i in range(n)])  4.45 us
    pallas_call x1, Pallas kernels, spectral(): pl.pallas_call(functools.partial(spectral_kernel, orb, vec, rows_in), out...  2.75 us
    pallas_call x1, Pallas kernels, windows(): pl.pallas_call(functools.partial(windows_kernel, orb, vec), out_shape=out...  2 us
  transfers between devices with their start and end apart: 12, of which 7 were waited for; matrix products, arithmetic and copies ran while one was open for 0% of the time, Pallas kernels for 13%

profile of v8, /device:TPU:0, one launch (start us, length us, event | category | flops | bytes accessed | tf_op | source)
XLA Modules:
  0.0 85.2 jit_solution(5708732178317518341)
XLA Ops:
  1.3 2.0 %windows.1 = (bf16[15,3,16,128]{3,2,1,0:T(8,128)(2,1)S(1)}, bf16[15,3,16,128]{3,2,1,0:T(8,128)(2,1)S(1)}, bf16[15,3,16,128]{3,2,1,0:T(8,128)(2,1)S(1)}, bf16[15,...) custom-call(f32[1]{0:T(128)S(6)} %copy.16.energy_any, ...), custom_call_target="tpu_custom_call" | custom-call | tf_op jit(solution)/shard_map/windows/pallas_call | solution.py:304
  3.3 3.0 %collective-permute-start.1 = (bf16[6,3,16,128]{3,2,1,0:T(8,128)(2,1)S(1)}, bf16[6,3,16,128]{3,2,1,0:T(8,128)(2,1)S(1)}, u32[]{:S(2)}, u32[]{:S(2)}) collective-permute-start(bf16[6,3,16,128]{3,2,1,0:T(8,128)(2,1)S(1)} %get-tuple-element.22), channel_id=1, source_target_pairs={{0,1},{1,2},{2,3},{3,0},{4,5},{5,6},{6,7},{7,4},{8,9},{9,10},{10,1... | collective-permute-start | bytes 221192 | tf_op jit(solution)/shard_map/ppermute | solution.py:754
  6.3 1.5 %collective-permute-start.2 = (bf16[6,3,16,128]{3,2,1,0:T(8,128)(2,1)S(1)}, bf16[6,3,16,128]{3,2,1,0:T(8,128)(2,1)S(1)}, u32[]{:S(2)}, u32[]{:S(2)}) collective-permute-start(bf16[6,3,16,128]{3,2,1,0:T(8,128)(2,1)S(1)} %get-tuple-element.23), channel_id=1, source_target_pairs={{0,2},{1,3},{2,0},{3,1},{4,6},{5,7},{6,4},{7,5},{8,10},{9,11},{10,... | collective-permute-start | bytes 221192 | tf_op jit(solution)/shard_map/ppermute | solution.py:754
  7.8 1.4 %collective-permute-start.3 = (bf16[6,3,16,128]{3,2,1,0:T(8,128)(2,1)S(1)}, bf16[6,3,16,128]{3,2,1,0:T(8,128)(2,1)S(1)}, u32[]{:S(2)}, u32[]{:S(2)}) collective-permute-start(bf16[6,3,16,128]{3,2,1,0:T(8,128)(2,1)S(1)} %get-tuple-element.24), channel_id=1, source_target_pairs={{0,3},{1,0},{2,1},{3,2},{4,7},{5,4},{6,5},{7,6},{8,11},{9,8},{10,9... | collective-permute-start | bytes 221192 | tf_op jit(solution)/shard_map/ppermute | solution.py:754
  9.2 1.6 %collective-permute-start.5 = (bf16[15,3,16,128]{3,2,1,0:T(8,128)(2,1)S(1)}, bf16[15,3,16,128]{3,2,1,0:T(8,128)(2,1)S(1)}, u32[]{:S(2)}, u32[]{:S(2)}) collective-permute-start(bf16[15,3,16,128]{3,2,1,0:T(8,128)(2,1)S(1)} %get-tuple-element.28), channel_id=1, source_target_pairs={{0,8},{4,12},{8,16},{12,20},{16,24},{20,28},{24,0},{28,4},{1,9},{5... | collective-permute-start | bytes 552968 | tf_op jit(solution)/shard_map/ppermute | solution.py:763
  10.8 2.2 %collective-permute-start.6 = (bf16[15,3,16,128]{3,2,1,0:T(8,128)(2,1)S(1)}, bf16[15,3,16,128]{3,2,1,0:T(8,128)(2,1)S(1)}, u32[]{:S(2)}, u32[]{:S(2)}) collective-permute-start(bf16[15,3,16,128]{3,2,1,0:T(8,128)(2,1)S(1)} %get-tuple-element.29), channel_id=1, source_target_pairs={{0,24},{4,28},{8,0},{12,4},{16,8},{20,12},{24,16},{28,20},{1,25},{... | collective-permute-start | bytes 552968 | tf_op jit(solution)/shard_map/ppermute | solution.py:763
  13.8 4.8 %collective-permute-done.5.refs_0_ = bf16[15,3,16,128]{3,2,1,0:T(8,128)(2,1)S(1)} collective-permute-done((bf16[15,3,16,128]{3,2,1,0:T(8,128)(2,1)S(1)}, bf16[15,3,16,128]{3,2,1,0:T(8,128)(2,1)S(1)}, u32[]{:S(2)}, u32[]{:S(2)}) %collective-permute-start.5) | collective-permute-done | bytes 184352 | tf_op jit(solution)/shard_map/ppermute | solution.py:763
  18.6 1.4 %collective-permute-done.6.refs_1_.refs_0_ = bf16[15,3,16,128]{3,2,1,0:T(8,128)(2,1)S(1)} collective-permute-done((bf16[15,3,16,128]{3,2,1,0:T(8,128)(2,1)S(1)}, bf16[15,3,16,128]{3,2,1,0:T(8,128)(2,1)S(1)}, u32[]{:S(2)}, u32[]{:S(2)}) %collective-permute-start.6) | collective-permute-done | bytes 184352 | tf_op jit(solution)/shard_map/ppermute | solution.py:763
  20.1 1.2 %collective-permute-start.7 = (bf16[5,8,3,16,128]{4,3,2,1,0:T(8,128)(2,1)S(1)}, bf16[5,8,3,16,128]{4,3,2,1,0:T(8,128)(2,1)S(1)}, u32[]{:S(2)}, u32[]{:S(2)}) collective-permute-start(bf16[5,8,3,16,128]{4,3,2,1,0:T(8,128)(2,1)S(1)} %with_edge.1.mine_ref), channel_id=1, source_target_pairs={{0,4},{4,0},{8,12},{12,8},{16,20},{20,16},{24,28},{28,24},{1,5},{5... | collective-permute-start | bytes 1474568 | tf_op jit(solution)/shard_map/ppermute | solution.py:749
  21.3 1.6 %collective-permute-start = (bf16[15,3,16,128]{3,2,1,0:T(8,128)(2,1)S(1)}, bf16[15,3,16,128]{3,2,1,0:T(8,128)(2,1)S(1)}, u32[]{:S(2)}, u32[]{:S(2)}) collective-permute-start(bf16[15,3,16,128]{3,2,1,0:T(8,128)(2,1)S(1)} %get-tuple-element.20), channel_id=1, source_target_pairs={{0,16},{4,20},{8,24},{12,28},{16,0},{20,4},{24,8},{28,12},{1,17},{... | collective-permute-start | bytes 552968 | tf_op jit(solution)/shard_map/ppermute | solution.py:763
  23.2 2.8 %solve_window.5.refs_3_ = f32[24,128,128]{2,1,0:T(8,128)S(1)} custom-call(bf16[15,3,16,128]{3,2,1,0:T(8,128)(2,1)S(1)} %get-tuple-element.32.refs_0_, f32[32,128,128]{2,1,0:T(8,128)S(1)} %get-tuple-element.30.refs_1_, f32[32,32,128]{2,1,0:T(8,128)S(1)} %get-tuple-element.31.refs_2_), custom_call_target="tpu_custom_call" | custom-call | tf_op jit(solution)/shard_map/solve_window/pallas_call | solution.py:500
  25.9 2.9 %solve_window.6.refs_3_ = f32[24,128,128]{2,1,0:T(8,128)S(1)} custom-call(bf16[15,3,16,128]{3,2,1,0:T(8,128)(2,1)S(1)} %collective-permute-done.5.refs_0_, f32[32,128,128]{2,1,0:T(8,128)S(1)} %get-tuple-element.30.refs_1_, f32[32,32,128]{2,1,0:T(8,128)S(1)} %get-tuple-element.31.refs_2_, f32[24,128,128]{2,1,0:T(8,128)S(1)} %solve_window.5.refs_3_), custom_call_target="tpu_custom_call" | custom-call | tf_op jit(solution)/shard_map/solve_window/pallas_call | solution.py:500
  28.8 2.9 %solve_window.7.refs_3_ = f32[24,128,128]{2,1,0:T(8,128)S(1)} custom-call(bf16[15,3,16,128]{3,2,1,0:T(8,128)(2,1)S(1)} %collective-permute-done.6.refs_1_.refs_0_, f32[32,128,128]{2,1,0:T(8,128)S(1)} %get-tuple-element.30.refs_1_, f32[32,32,128]{2,1,0:T(8,128)S(1)} %get-tuple-element.31.refs_2_, f32[24,128,128]{2,1,0:T(8,128)S(1)} %solve_window.6.refs_3_), custom_call_target="tpu_custom_call" | custom-call | tf_op jit(solution)/shard_map/solve_window/pallas_call | solution.py:500
  31.7 1.0 %collective-permute-done.refs_0_ = bf16[15,3,16,128]{3,2,1,0:T(8,128)(2,1)S(1)} collective-permute-done((bf16[15,3,16,128]{3,2,1,0:T(8,128)(2,1)S(1)}, bf16[15,3,16,128]{3,2,1,0:T(8,128)(2,1)S(1)}, u32[]{:S(2)}, u32[]{:S(2)}) %collective-permute-start) | collective-permute-done | bytes 184352 | tf_op jit(solution)/shard_map/ppermute | solution.py:763
  32.7 1.6 %solve_window.9 = f32[12,128,128]{2,1,0:T(8,128)S(1)} custom-call(bf16[15,3,16,128]{3,2,1,0:T(8,128)(2,1)S(1)} %collective-permute-done.refs_0_, f32[32,128,128]{2,1,0:T(8,128)S(1)} %get-tuple-element.30.refs_1_, f32[32,32,128]{2,1,0:T(8,128)S(1)} %get-tuple-element.31.refs_2_, f32[24,128,128]{2,1,0:T(8,128)S(1)} %solve_window.7.refs_3_), custom_call_target="tpu_custom_call" | custom-call | tf_op jit(solution)/shard_map/solve_window/pallas_call | solution.py:500
  34.5 1.8 %solve_window.8 = f32[12,128,128]{2,1,0:T(8,128)S(1)} custom-call(bf16[15,3,16,128]{3,2,1,0:T(8,128)(2,1)S(1)} %collective-permute-done.refs_0_, f32[32,128,128]{2,1,0:T(8,128)S(1)} %get-tuple-element.30.refs_1_, f32[32,32,128]{2,1,0:T(8,128)S(1)} %get-tuple-element.31.refs_2_, f32[24,128,128]{2,1,0:T(8,128)S(1)} %solve_window.7.refs_3_), custom_call_target="tpu_custom_call" | custom-call | tf_op jit(solution)/shard_map/solve_window/pallas_call | solution.py:500
  37.4 18.1 %all_to_all.10 = f32[32,7,4,128]{3,2,1,0:T(4,128)S(1)} all-to-all(f32[32,7,4,128]{3,2,1,0:T(4,128)S(1)} %bitcast.11), channel_id=1, replica_groups=mesh['orb'=8,'vec'=4] {'orb','vec'}, dimensions={0} | all-to-all | bytes 917504 | tf_op jit(solution)/shard_map/all_to_all | solution.py:793
  55.5 2.8 %spectral.1 = f32[896,128]{1,0:T(8,128)S(1)} custom-call(f32[96]{0:T(128)S(1)} %copy-done.7, f32[96,128]{1,0:T(8,128)S(1)} %copy-done.5, bf16[2,512,512]{2,1,0:T(8,128)(2,1)S(1)} %copy-done, bf16[2,288,288]{2,1,0:T(8,128)(2,1)S(1)} %copy-done.2, bf16[2,96,96]{2,1,0:T(8,128)(2,1)S(1)} %copy-done.4, bf16[2,512,384]{2,1,0:T(8,128)(2,1)S(1)} %copy-done.1, ...), custom_call_target="tpu_custom_call" | custom-call | tf_op jit(solution)/shard_map/spectral/pallas_call | solution.py:631
  58.2 17.0 %all_to_all.11 = f32[32,7,4,128]{3,2,1,0:T(4,128)S(1)} all-to-all(f32[32,7,4,128]{3,2,1,0:T(4,128)S(1)} %bitcast.10), channel_id=1, replica_groups=mesh['orb'=8,'vec'=4] {'orb','vec'}, dimensions={0} | all-to-all | bytes 917504 | tf_op jit(solution)/shard_map/all_to_all | solution.py:795
  75.3 1.5 %back.1 = (f32[4,4]{1,0:T(4,128)}, f32[216,128]{1,0:T(8,128)S(1)}, f32[216,128]{1,0:T(8,128)S(1)}, f32[216,128]{1,0:T(8,128)S(1)}, f32[216,128]{1,0:T(8,128)S(1)}) custom-call(bf16[2,96,128]{2,1,0:T(8,128)(2,1)S(1)} %copy-done.3, f32[896,128]{1,0:T(8,128)S(1)} %bitcast.8), custom_call_target="tpu_custom_call" | custom-call | tf_op jit(solution)/shard_map/back/pallas_call | solution.py:708
  76.8 1.5 %collective-permute-start.10 = (f32[216,128]{1,0:T(8,128)S(1)}, f32[216,128]{1,0:T(8,128)S(1)}, u32[]{:S(2)}, u32[]{:S(2)}) collective-permute-start(f32[216,128]{1,0:T(8,128)S(1)} %get-tuple-element.35), channel_id=1, source_target_pairs={{0,2},{1,3},{2,0},{3,1},{4,6},{5,7},{6,4},{7,5},{8,10},{9,11},{10,... | collective-permute-start | bytes 331784 | tf_op jit(solution)/shard_map/ppermute | solution.py:754
  78.3 1.4 %collective-permute-start.11 = (f32[216,128]{1,0:T(8,128)S(1)}, f32[216,128]{1,0:T(8,128)S(1)}, u32[]{:S(2)}, u32[]{:S(2)}) collective-permute-start(f32[216,128]{1,0:T(8,128)S(1)} %get-tuple-element.36), channel_id=1, source_target_pairs={{0,3},{1,0},{2,1},{3,2},{4,7},{5,4},{6,5},{7,6},{8,11},{9,8},{10,9... | collective-permute-start | bytes 331784 | tf_op jit(solution)/shard_map/ppermute | solution.py:754
  79.8 3.4 %collective-permute-done.9.refs_1_ = f32[216,128]{1,0:T(8,128)S(1)} collective-permute-done((f32[216,128]{1,0:T(8,128)S(1)}, f32[216,128]{1,0:T(8,128)S(1)}, u32[]{:S(2)}, u32[]{:S(2)}) %collective-permute-start.9) | collective-permute-done | bytes 110624 | tf_op jit(solution)/shard_map/ppermute | solution.py:754
  84.2 0.8 assemble.1
  (31 shorter events, 3.4 us)
Async XLA Ops:
  3.3 9.8 %collective-permute-start.1 = (bf16[6,3,16,128]{3,2,1,0:T(8,128)(2,1)S(1)}, bf16[6,3,16,128]{3,2,1,0:T(8,128)(2,1)S(1)}, u32[]{:S(2)}, u32[]{:S(2)}) collective-permute-start(bf16[6,3,16,128]{3,2,1,0:T(8,128)(2,1)S(1)} %get-tuple-element.22), channel_id=1, source_target_pairs={{0,1},{1,2},{2,3},{3,0},{4,5},{5,6},{6,7},{7,4},{8,9},{9,10},{10,1... | collective-permute-start | bytes 221192 | tf_op jit(solution)/shard_map/ppermute | solution.py:754
  6.3 6.8 %collective-permute-start.2 = (bf16[6,3,16,128]{3,2,1,0:T(8,128)(2,1)S(1)}, bf16[6,3,16,128]{3,2,1,0:T(8,128)(2,1)S(1)}, u32[]{:S(2)}, u32[]{:S(2)}) collective-permute-start(bf16[6,3,16,128]{3,2,1,0:T(8,128)(2,1)S(1)} %get-tuple-element.23), channel_id=1, source_target_pairs={{0,2},{1,3},{2,0},{3,1},{4,6},{5,7},{6,4},{7,5},{8,10},{9,11},{10,... | collective-permute-start | bytes 221192 | tf_op jit(solution)/shard_map/ppermute | solution.py:754
  7.8 5.3 %collective-permute-start.3 = (bf16[6,3,16,128]{3,2,1,0:T(8,128)(2,1)S(1)}, bf16[6,3,16,128]{3,2,1,0:T(8,128)(2,1)S(1)}, u32[]{:S(2)}, u32[]{:S(2)}) collective-permute-start(bf16[6,3,16,128]{3,2,1,0:T(8,128)(2,1)S(1)} %get-tuple-element.24), channel_id=1, source_target_pairs={{0,3},{1,0},{2,1},{3,2},{4,7},{5,4},{6,5},{7,6},{8,11},{9,8},{10,9... | collective-permute-start | bytes 221192 | tf_op jit(solution)/shard_map/ppermute | solution.py:754
  9.2 9.4 %collective-permute-start.5 = (bf16[15,3,16,128]{3,2,1,0:T(8,128)(2,1)S(1)}, bf16[15,3,16,128]{3,2,1,0:T(8,128)(2,1)S(1)}, u32[]{:S(2)}, u32[]{:S(2)}) collective-permute-start(bf16[15,3,16,128]{3,2,1,0:T(8,128)(2,1)S(1)} %get-tuple-element.28), channel_id=1, source_target_pairs={{0,8},{4,12},{8,16},{12,20},{16,24},{20,28},{24,0},{28,4},{1,9},{5... | collective-permute-start | bytes 552968 | tf_op jit(solution)/shard_map/ppermute | solution.py:763
  10.8 9.2 %collective-permute-start.6 = (bf16[15,3,16,128]{3,2,1,0:T(8,128)(2,1)S(1)}, bf16[15,3,16,128]{3,2,1,0:T(8,128)(2,1)S(1)}, u32[]{:S(2)}, u32[]{:S(2)}) collective-permute-start(bf16[15,3,16,128]{3,2,1,0:T(8,128)(2,1)S(1)} %get-tuple-element.29), channel_id=1, source_target_pairs={{0,24},{4,28},{8,0},{12,4},{16,8},{20,12},{24,16},{28,20},{1,25},{... | collective-permute-start | bytes 552968 | tf_op jit(solution)/shard_map/ppermute | solution.py:763
  13.1 6.9 %collective-permute-start.4 = (bf16[5,2,3,16,128]{4,3,2,1,0:T(8,128)(2,1)S(1)}, bf16[5,2,3,16,128]{4,3,2,1,0:T(8,128)(2,1)S(1)}, u32[]{:S(2)}, u32[]{:S(2)}) collective-permute-start(bf16[5,2,3,16,128]{4,3,2,1,0:T(8,128)(2,1)S(1)} %get-tuple-element.27), channel_id=1, source_target_pairs={{4,8},{12,16},{20,24},{8,4},{16,12},{24,20},{0,0},{28,28},{5,9},{1... | collective-permute-start | bytes 368648 | tf_op jit(solution)/shard_map/ppermute | solution.py:773
  20.1 2.8 %collective-permute-start.7 = (bf16[5,8,3,16,128]{4,3,2,1,0:T(8,128)(2,1)S(1)}, bf16[5,8,3,16,128]{4,3,2,1,0:T(8,128)(2,1)S(1)}, u32[]{:S(2)}, u32[]{:S(2)}) collective-permute-start(bf16[5,8,3,16,128]{4,3,2,1,0:T(8,128)(2,1)S(1)} %with_edge.1.mine_ref), channel_id=1, source_target_pairs={{0,4},{4,0},{8,12},{12,8},{16,20},{20,16},{24,28},{28,24},{1,5},{5... | collective-permute-start | bytes 1474568 | tf_op jit(solution)/shard_map/ppermute | solution.py:749
  21.3 11.5 %collective-permute-start = (bf16[15,3,16,128]{3,2,1,0:T(8,128)(2,1)S(1)}, bf16[15,3,16,128]{3,2,1,0:T(8,128)(2,1)S(1)}, u32[]{:S(2)}, u32[]{:S(2)}) collective-permute-start(bf16[15,3,16,128]{3,2,1,0:T(8,128)(2,1)S(1)} %get-tuple-element.20), channel_id=1, source_target_pairs={{0,16},{4,20},{8,24},{12,28},{16,0},{20,4},{24,8},{28,12},{1,17},{... | collective-permute-start | bytes 552968 | tf_op jit(solution)/shard_map/ppermute | solution.py:763
  34.4 2.4 %copy-start.6 = (bf16[2,96,128]{2,1,0:T(8,128)(2,1)S(1)}, bf16[2,96,128]{2,1,0:T(8,128)(2,1)}, u32[]{:S(2)}) copy-start(bf16[2,96,128]{2,1,0:T(8,128)(2,1)} %constant.16.clone.basis_ref) | copy-start | bytes 147460
  34.4 2.4 %collective-permute-start.8 = (f32[12,128,128]{2,1,0:T(8,128)S(1)}, f32[12,128,128]{2,1,0:T(8,128)S(1)}, u32[]{:S(2)}, u32[]{:S(2)}) collective-permute-start(f32[12,128,128]{2,1,0:T(8,128)S(1)} %solve_window.9), channel_id=1, source_target_pairs={{0,4},{4,0},{8,12},{12,8},{16,20},{20,16},{24,28},{28,24},{1,5},{5... | collective-permute-start | bytes 2359304 | tf_op jit(solution)/shard_map/ppermute | solution.py:749
  36.3 19.2 %copy-start = (bf16[2,512,512]{2,1,0:T(8,128)(2,1)S(1)}, bf16[2,512,512]{2,1,0:T(8,128)(2,1)}, u32[]{:S(2)}) copy-start(bf16[2,512,512]{2,1,0:T(8,128)(2,1)} %constant.19.clone.wy_ref) | copy-start | bytes 3145732
  36.3 19.2 %copy-start.1 = (bf16[2,512,384]{2,1,0:T(8,128)(2,1)S(1)}, bf16[2,512,384]{2,1,0:T(8,128)(2,1)}, u32[]{:S(2)}) copy-start(bf16[2,512,384]{2,1,0:T(8,128)(2,1)} %constant.22.clone.wyb_ref) | copy-start | bytes 2359300
  36.3 19.1 %copy-start.2 = (bf16[2,288,288]{2,1,0:T(8,128)(2,1)S(1)}, bf16[2,288,288]{2,1,0:T(8,128)(2,1)}, u32[]{:S(2)}) copy-start(bf16[2,288,288]{2,1,0:T(8,128)(2,1)} %constant.20.clone.kz_ref) | copy-start | bytes 995332
  36.3 19.1 %copy-start.4 = (bf16[2,96,96]{2,1,0:T(8,128)(2,1)S(1)}, bf16[2,96,96]{2,1,0:T(8,128)(2,1)}, u32[]{:S(2)}) copy-start(bf16[2,96,96]{2,1,0:T(8,128)(2,1)} %constant.21.clone.kzb_ref) | copy-start | bytes 110596
  36.3 19.1 %copy-start.5 = (f32[96,128]{1,0:T(8,128)S(1)}, f32[96,128]{1,0:T(8,128)}, u32[]{:S(2)}) copy-start(f32[96,128]{1,0:T(8,128)} %constant.18.clone.muzy_ref) | copy-start | bytes 147460
  36.3 19.1 %copy-start.7 = (f32[96]{0:T(128)S(1)}, f32[96]{0:T(128)}, u32[]{:S(2)}) copy-start(f32[96]{0:T(128)} %constant.17.clone.mux_ref) | copy-start | bytes 1156
  55.5 19.8 %copy-start.3 = (bf16[2,96,128]{2,1,0:T(8,128)(2,1)S(1)}, bf16[2,96,128]{2,1,0:T(8,128)(2,1)}, u32[]{:S(2)}) copy-start(bf16[2,96,128]{2,1,0:T(8,128)(2,1)} %constant.23.clone.basis_ref) | copy-start | bytes 147460
  76.7 6.4 %collective-permute-start.9 = (f32[216,128]{1,0:T(8,128)S(1)}, f32[216,128]{1,0:T(8,128)S(1)}, u32[]{:S(2)}, u32[]{:S(2)}) collective-permute-start(f32[216,128]{1,0:T(8,128)S(1)} %get-tuple-element.34), channel_id=1, source_target_pairs={{0,1},{1,2},{2,3},{3,0},{4,5},{5,6},{6,7},{7,4},{8,9},{9,10},{10,1... | collective-permute-start | bytes 331784 | tf_op jit(solution)/shard_map/ppermute | solution.py:754
  76.8 7.0 %collective-permute-start.10 = (f32[216,128]{1,0:T(8,128)S(1)}, f32[216,128]{1,0:T(8,128)S(1)}, u32[]{:S(2)}, u32[]{:S(2)}) collective-permute-start(f32[216,128]{1,0:T(8,128)S(1)} %get-tuple-element.35), channel_id=1, source_target_pairs={{0,2},{1,3},{2,0},{3,1},{4,6},{5,7},{6,4},{7,5},{8,10},{9,11},{10,... | collective-permute-start | bytes 331784 | tf_op jit(solution)/shard_map/ppermute | solution.py:754
  78.3 5.9 %collective-permute-start.11 = (f32[216,128]{1,0:T(8,128)S(1)}, f32[216,128]{1,0:T(8,128)S(1)}, u32[]{:S(2)}, u32[]{:S(2)}) collective-permute-start(f32[216,128]{1,0:T(8,128)S(1)} %get-tuple-element.36), channel_id=1, source_target_pairs={{0,3},{1,0},{2,1},{3,2},{4,7},{5,4},{6,5},{7,6},{8,11},{9,8},{10,9... | collective-permute-start | bytes 331784 | tf_op jit(solution)/shard_map/ppermute | solution.py:754
